TPU v7x, 128 devices: a whole 4x4x4 slice. The times are simulated.
128 devices in a mesh: dp: 16 (over y, x_lo, core), tensor: 8 (over z, x_hi).
Axes of the slice: x: 4 (x_hi: 2, x_lo: 2; x = x_hi * 2 + x_lo), y: 4, z: 4, core: 2. Of those that a mesh axis runs over, the one named last changes fastest.
Arguments:
- gate_pre: bfloat16 [8192, 14336], P('dp', 'tensor'), may hold values from -6 to 6
- up_pre: bfloat16 [8192, 14336], P('dp', 'tensor'), may hold values from -6 to 6
- out_grad: bfloat16 [8192, 4096], P(('dp', 'tensor')), may hold values from -24 to 24
- down_weight: bfloat16 [4096, 14336], P(('dp', 'tensor')), may hold values from -0.046875 to 0.046875
Outputs:
- gate_grad: bfloat16 [8192, 14336], P('dp', 'tensor')
- up_grad: bfloat16 [8192, 14336], P('dp', 'tensor')
- down_grad: bfloat16 [4096, 14336], P('dp', 'tensor')
All inputs are finite; a program needn't handle non-finite values.
Results may differ from a plain program's by a relative error of at most 0.022.
Values may be sent and summed in bfloat16 or wider, within the bound.
No kernel may reach another device: no remote copies, remote signals or barrier semaphores. Data moves between devices by JAX's collectives and lax.ppermute only.
A program may use at most 128 MiB of HBM per device.

v0:
```python
import jax
import jax.numpy as jnp
from jax import lax
from jax.sharding import PartitionSpec as P


def on_device(gate_pre, up_pre, out_grad, down_weight):
    relaid = lax.all_to_all(down_weight, "tensor", split_axis=1, concat_axis=0, tiled=True)
    gate = gate_pre.astype(jnp.float32)
    up = up_pre.astype(jnp.float32)
    sig = jax.nn.sigmoid(gate)
    hidden = (gate * sig * up).astype(jnp.bfloat16)
    group_rows = gate_pre.shape[0]
    total_tokens = group_rows * lax.axis_size("dp")
    factor = 1.0 / jnp.sqrt(jnp.float32(total_tokens))
    full_grad = lax.all_gather(out_grad, "tensor", axis=0, tiled=True)
    columns = full_grad
    hidden_grad = jnp.dot(
        columns,
        lax.all_gather(relaid, "dp", axis=0, tiled=True),
        preferred_element_type=jnp.float32,
    )
    columns = full_grad
    product = lax.dot_general(
        columns, hidden, (((0,), (0,)), ((), ())), preferred_element_type=jnp.float32
    )
    down_grad = lax.psum_scatter(
        (product * factor).astype(jnp.bfloat16), "dp", scatter_dimension=0, tiled=True
    )
    gate_grad = (hidden_grad * up * sig * (1.0 + gate * (1.0 - sig))).astype(jnp.bfloat16)
    up_grad = (hidden_grad * gate * sig).astype(jnp.bfloat16)
    return (gate_grad, up_grad, down_grad)


def solution(mesh):
    return jax.shard_map(
        on_device,
        mesh=mesh,
        in_specs=(
            P("dp", "tensor"),
            P("dp", "tensor"),
            P(("dp", "tensor"), None),
            P(("dp", "tensor"), None),
        ),
        out_specs=(P("dp", "tensor"), P("dp", "tensor"), P("dp", "tensor")),
        check_vma=False,
    )
```

profile of v0, /device:TPU:0, one launch (start us, length us, event | category | flops | bytes accessed | tf_op | source)
XLA Modules:
  0.0 341.8 jit_solution(3324972827190699715)
XLA Ops:
  7.2 0.0 copy-start
  7.2 0.0 all-gather.3.cloned.1.call-start
  7.2 0.7 all-gather.3.cloned.1.call-update
  7.9 0.0 all-gather.5.cloned.1.call-start
  8.0 1.2 copy.15
  9.2 28.1 %all_to_all.19 = bf16[32,8,1792]{2,0,1:T(8,128)(2,1)} all-to-all(bf16[32,8,1792]{2,0,1:T(8,128)(2,1)S(1)} %bitcast.13), channel_id=1, replica_groups=mesh['dp'=16,'tensor'=8] {'tensor'}, dimensions={1} | all-to-all | bytes 1835008 | tf_op jit(solution)/shard_map/all_to_all | solution.py:8
  37.3 0.0 all-gather.5.cloned.1.call-update
  37.3 0.0 reduce-scatter.2.cloned.1.call-start
  37.4 49.9 %all-gather.3.cloned.1.call-done = bf16[512,4096]{1,0:T(8,128)(2,1)} async-done(((bf16[64,4096]{1,0:T(8,128)(2,1)}), bf16[512,4096]{1,0:T(8,128)(2,1)}) %all-gather.3.cloned.1.call-update) | async-done | bytes 4194320 | tf_op jit(solution)/shard_map/all_gather | solution.py:16
  87.2 0.0 copy-done
  87.2 13.8 %fusion = bf16[4096,1792]{0,1:T(8,128)(2,1)} fusion(bf16[512,4096]{1,0:T(8,128)(2,1)} %all-gather.3.cloned.1.call-done, bf16[512,1792]{1,0:T(8,128)(2,1)} %param.5, bf16[512,1792]{1,0:T(8,128)(2,1)S(1)} %copy-done), kind=kOutput, calls=%fused_computation.1 | convolution fusion | flops 7538212864 | bytes 22544384 | tf_op jit(solution)/shard_map/dot_general | solution.py:24
  101.0 0.0 reduce-scatter.2.cloned.1.call-update
  101.0 67.4 %all-gather.5.cloned.1.call-done = bf16[4096,1792]{1,0:T(8,128)(2,1)} async-done(((bf16[256,1792]{1,0:T(8,128)(2,1)}), bf16[4096,1792]{1,0:T(8,128)(2,1)}) %all-gather.5.cloned.1.call-update) | async-done | bytes 14680080 | tf_op jit(solution)/shard_map/all_gather | solution.py:20
  168.5 15.9 %fusion.10 = (bf16[512,1792]{1,0:T(8,128)(2,1)}, bf16[512,1792]{1,0:T(8,128)(2,1)}) fusion(bf16[512,1792]{1,0:T(8,128)(2,1)S(1)} %copy-done, bf16[512,1792]{1,0:T(8,128)(2,1)} %param.5, bf16[512,4096]{1,0:T(8,128)(2,1)} %all-gather.3.cloned.1.call-done, bf16[4096,1792]{1,0:T(8,128)(2,1)} %all-gather.5.cloned.1.call-done), kind=kOutput, calls=%fused_computation.17 | convolution fusion | flops 7529955328 | bytes 26214400 | tf_op jit(solution)/shard_map/dot_general | solution.py:18
  184.4 148.7 %reduce-scatter.2.cloned.1.call-done = bf16[256,1792]{0,1:T(8,128)(2,1)} async-done(((bf16[4096,1792]{0,1:T(8,128)(2,1)}), bf16[256,1792]{0,1:T(8,128)(2,1)}) %reduce-scatter.2.cloned.1.call-update) | async-done | bytes 917520 | tf_op jit(solution)/shard_map/reduce_scatter | solution.py:27
  333.1 2.2 copy.12
Async XLA Ops:
  7.2 80.1 %copy-start = (bf16[512,1792]{1,0:T(8,128)(2,1)S(1)}, bf16[512,1792]{1,0:T(8,128)(2,1)}, u32[]{:S(2)}) copy-start(bf16[512,1792]{1,0:T(8,128)(2,1)} %param.4) | copy-start | bytes 5505028
  7.2 80.1 %all-gather.3.cloned.1.call-start = ((), (), s32[]{:S(2)}) async-start(), calls=%async_computation.2 | async-start | bytes 4718592 | tf_op jit(solution)/shard_map/all_gather | solution.py:16
  7.9 160.5 %all-gather.5.cloned.1.call-start = ((), (), s32[]{:S(2)}) async-start(), calls=%async_computation.3 | async-start | bytes 15597568 | tf_op jit(solution)/shard_map/all_gather | solution.py:20
  37.3 295.7 %reduce-scatter.2.cloned.1.call-start = ((), (), s32[]{:S(2)}) async-start(), calls=%async_computation.4 | async-start | bytes 15597568 | tf_op jit(solution)/shard_map/reduce_scatter | solution.py:27
Sparse Core Ops, SparseCore 0:
  10.4 76.8 all-gather.2
  88.9 79.4 all-gather.4
  170.9 162.1 reduce-scatter.1
where the time goes:
time: 342 us
  waiting for transfers between devices  267 us (78%)
  matrix products  29.7 us (9%)
  blocking collectives  28.1 us (8%)
  between operations  13.8 us (4%)
  local copies, waits for them, and re-layouts  3.46 us (1%)
    reduce_scatter x1, waiting for transfers between devices, on_device(): lax.psum_scatter((product * factor).astype(jnp.bfloat16), 'dp', scatter_d...  149 us
    all_gather x1, waiting for transfers between devices, on_device(): lax.all_gather(relaid, 'dp', axis=0, tiled=True)  67.4 us
    all_gather x1, waiting for transfers between devices, on_device(): full_grad = lax.all_gather(out_grad, 'tensor', axis=0, tiled=True)  49.9 us
    all_to_all x1, blocking collectives, on_device(): lax.all_to_all(down_weight, 'tensor', split_axis=1, concat_axis=0, tiled=...  28.1 us
    dot_general x1, matrix products, on_device(): jnp.dot(columns, lax.all_gather(relaid, 'dp', axis=0, tiled=True), prefer...  15.9 us
    dot_general x1, matrix products, on_device(): lax.dot_general(columns, hidden, (((0,), (0,)), ((), ())), preferred_elem...  13.8 us
  transfers between devices with their start and end apart: 3, of which 3 were waited for; matrix products, arithmetic and copies ran while one was open for 9% of the time, Pallas kernels for 0%

commit v1 on v0

v1 whole, which is shorter than its diff:
```python
import jax
import jax.numpy as jnp
import numpy as np
from jax import lax
from jax.experimental import pallas as pl
from jax.experimental.pallas import tpu as pltpu
from jax.sharding import PartitionSpec as P

SIZES = (4, 2, 2, 4, 2)
BF16, F32 = jnp.bfloat16, jnp.float32
VMEM = pl.BlockSpec(memory_space=pltpu.VMEM)
SMEM = pl.BlockSpec(memory_space=pltpu.SMEM)
EIGHT = [(k, j) for k in range(4) for j in range(2)]


def send(x, y=0, l=0, c=0, z=0, h=0):
    pairs = []
    for source in range(int(np.prod(SIZES))):
        place = np.unravel_index(source, SIZES)
        target = [(int(p) + d) % n for p, d, n in zip(place, (y, l, c, z, h), SIZES)]
        pairs.append((source, int(np.ravel_multi_index(target, SIZES))))
    return lax.ppermute(x, ("dp", "tensor"), pairs)


def call(kernel, outs, place, *args, mib=40, flops=0):
    moved = sum(a.size * a.dtype.itemsize for a in args) + sum(o.size * o.dtype.itemsize for o in outs)
    return pl.pallas_call(
        kernel,
        out_shape=outs,
        in_specs=[SMEM] + [VMEM] * len(args),
        out_specs=[VMEM] * len(outs),
        compiler_params=pltpu.CompilerParams(vmem_limit_bytes=mib << 20),
        cost_estimate=pl.CostEstimate(flops=flops, bytes_accessed=moved, transcendentals=0),
    )(place, *args)


def shape(*dims, dtype=BF16):
    return jax.ShapeDtypeStruct(dims, dtype)


def at(start, size, step=128):
    return pl.ds(pl.multiple_of(start, step), size)


def slot(place, k, j):
    return (place[3] + k) % 4 * 2 + (place[4] + j) % 2


def pack_kernel(place, grad, weight, own, other, *parts):
    y, l = place[0], place[1]
    stripe = own.shape[1] // 4
    for k in range(4):
        start = (y + k) % 4 * 2 * stripe
        to = pl.ds(k * stripe, stripe)
        own[:, to] = grad[:, at(start + l * stripe, stripe)]
        other[:, to] = grad[:, at(start + (1 - l) * stripe, stripe)]
    columns = parts[0].shape[1]
    for part, (k, j) in zip(parts, EIGHT):
        part[...] = weight[:, at(slot(place, k, j) * columns, columns)]


def weight_kernel(place, *refs):
    parts, keep, give = refs[:8], refs[8], refs[9]
    c = place[2]
    rows, half = parts[0].shape[0], keep.shape[1]
    for part, (k, j) in zip(parts, EIGHT):
        to = at(slot(place, k, j) * rows, rows, 32)
        keep[to, :] = part[:, at(c * half, half)]
        give[to, :] = part[:, at((1 - c) * half, half)]


def hidden_kernel(place, gate_ref, up_ref, own, other):
    c = place[2]
    half = own.shape[1]
    rows = own.shape[0] // 8
    for n, (k, j) in enumerate(EIGHT):
        block = at(slot(place, k, j) * rows, rows, 64)
        for out, side in ((own, c), (other, 1 - c)):
            gate = gate_ref[block, at(side * half, half)].astype(F32)
            up = up_ref[block, at(side * half, half)].astype(F32)
            out[pl.ds(n * rows, rows), :] = (gate * jax.nn.sigmoid(gate) * up).astype(BF16)


def gather_kernel(place, *refs):
    chunks, weights = refs[:16], refs[16:24]
    o_all, w_all, first, second = refs[24:]
    c = place[2]
    rows = chunks[0].shape[0] // 2
    tokens = 16 * rows
    cut = weights[0].shape[0]
    for k in range(4):
        w_all[at(k * 2 * cut + c * cut, cut, 256), :] = weights[2 * k][...]
        w_all[at(k * 2 * cut + (1 - c) * cut, cut, 256), :] = weights[2 * k + 1][...]
    for n, chunk in enumerate(chunks):
        o_all[pl.ds(n * rows, rows), :] = chunk[:rows, :]
        o_all[pl.ds(tokens + n * rows, rows), :] = chunk[rows:, :]
    tile = 256
    for out, start in ((second, tokens + tokens // 2), (first, tokens)):

        @pl.loop(0, out.shape[0] // tile)
        def _(i):
            block = o_all[at(start + i * tile, tile, tile), :]
            out[at(i * tile, tile, tile), :] = jnp.dot(
                block, w_all[...], preferred_element_type=F32
            ).astype(BF16)


def gradient_kernel(place, gate_ref, up_ref, mine_ref, pair_ref, core_ref, gate_grad, up_grad):
    c = place[2]
    half = pair_ref.shape[1]
    rows = pair_ref.shape[0] // 8
    for n, (k, j) in enumerate(EIGHT):
        block = at(slot(place, k, j) * rows, rows, 64)
        here = pl.ds(n * rows, rows)
        for side in (c, 1 - c):
            if side is c:
                grad = mine_ref[here, :] + pair_ref[here, :].astype(F32)
            else:
                grad = core_ref[here, :].astype(F32)
            columns = at(side * half, half)
            gate = gate_ref[block, columns].astype(F32)
            up = up_ref[block, columns].astype(F32)
            sig = jax.nn.sigmoid(gate)
            gate_grad[block, columns] = (grad * up * sig * (1.0 + gate * (1.0 - sig))).astype(BF16)
            up_grad[block, columns] = (grad * gate * sig).astype(BF16)


def total_kernel(place, here, top, low, high, bottom, own, other):
    c = place[2]
    cut = own.shape[0]
    for out, side in ((own, c), (other, 1 - c)):
        for s, (one, two) in enumerate(((top, high), (low, bottom))):

            @pl.when(side == s)
            def _(s=s, one=one, two=two, out=out):
                total = here[pl.ds(s * cut, cut), :].astype(F32) + one[...].astype(F32) + two[...].astype(F32)
                out[...] = total.astype(BF16)


def join_kernel(place, own, core, out):
    c = place[2]
    half = own.shape[1]
    out[:, at(c * half, half)] = own[...]
    out[:, at((1 - c) * half, half)] = core[...]


def on_device(gate_pre, up_pre, out_grad, down_weight):
    dp, tensor = lax.axis_index("dp"), lax.axis_index("tensor")
    place = jnp.stack([dp // 4, dp // 2 % 2, dp % 2, tensor // 2, tensor % 2]).astype(jnp.int32)
    tokens, columns = gate_pre.shape
    half = columns // 2
    share, width = out_grad.shape
    stripe = width // 8
    shard = down_weight.shape[0]
    cut = stripe // 2

    packed = call(
        pack_kernel,
        [shape(share, width // 2)] * 2 + [shape(shard, columns)] * 8,
        place, out_grad, down_weight,
    )
    o_own, o_other, parts = packed[0], packed[1], dict(zip(EIGHT, packed[2:]))

    came = {}
    for k, j in [(2, 1), (2, 0), (1, 1), (3, 1), (1, 0), (3, 0), (0, 1), (0, 0)]:
        came[(-k) % 4, j] = parts[k, j] if k == j == 0 else send(parts[k, j], z=k, h=j)
    o_a = jnp.concatenate([o_own, send(o_other, l=1)])
    o_b = jnp.concatenate([send(o_own, h=1), send(o_other, l=1, h=1)])

    hid_own, hid_other = call(hidden_kernel, [shape(tokens, half)] * 2, place, gate_pre, up_pre)
    hid_core = send(hid_other, c=1)
    hid_pair_own = send(hid_own, l=1)
    hid_pair_core = send(hid_core, l=1)

    keep, give = call(weight_kernel, [shape(stripe // 2, half)] * 2, place, *[came[p] for p in EIGHT])
    got = send(give, c=1)
    keep_up, keep_down = send(keep, y=-1), send(keep, y=1)
    got_up, got_down = send(got, y=-1), send(got, y=1)
    keep_far, got_far = send(keep_up, y=-1), send(got_down, y=1)
    weights = [keep, got, keep_up, got_up, keep_far, got_far, keep_down, got_down]

    a_up, a_down = send(o_a, z=-1), send(o_a, z=1)
    b_up, b_down = send(o_b, z=-1), send(o_b, z=1)
    a_far, b_far = send(a_up, z=-1), send(b_down, z=1)
    chunks = [o_a, o_b, a_up, b_up, a_far, b_far, a_down, b_down]
    chunks = chunks + [send(x, c=1) for x in chunks]

    flops = 2 * 2 * tokens * 4 * stripe * half
    o_all, w_all, first, second = call(
        gather_kernel,
        [shape(4 * tokens, 4 * stripe), shape(4 * stripe, half), shape(tokens, half), shape(tokens, half)],
        place, *chunks, *weights,
        flops=flops, mib=48,
    )
    second_in = send(second, l=1)
    first_in = send(first, l=1)

    factor = 1.0 / jnp.sqrt(F32(tokens * 16))
    hid = jnp.concatenate([hid_own, hid_core, hid_pair_own, hid_pair_core])

    def term(k):
        lhs = lax.slice_in_dim(o_all, k * stripe, (k + 1) * stripe, axis=1)
        product = lax.dot_general(lhs, hid, (((0,), (0,)), ((), ())), preferred_element_type=F32)
        return (product * factor).astype(BF16)

    far, above, below, here = term(2), term(1), term(3), term(0)
    via_down, via_up = send(far[:cut], y=1), send(far[cut:], y=-1)
    low = send(above[cut:], y=1)
    high = send(below[:cut], y=-1)
    top = send((above[:cut].astype(F32) + via_down.astype(F32)).astype(BF16), y=1)
    bottom = send((below[cut:].astype(F32) + via_up.astype(F32)).astype(BF16), y=-1)
    d_own, d_other = call(total_kernel, [shape(cut, half)] * 2, place, here, top, low, high, bottom)
    (down_grad,) = call(join_kernel, [shape(cut, columns)], place, d_own, send(d_other, c=1))

    mine = jnp.dot(o_all[: 2 * tokens], w_all, preferred_element_type=F32)
    core_out = (mine[tokens:] + second_in.astype(F32)).astype(BF16)
    gate_grad, up_grad = call(
        gradient_kernel, [shape(tokens, columns)] * 2, place,
        gate_pre, up_pre, mine[:tokens], first_in, send(core_out, c=1),
    )
    return (gate_grad, up_grad, down_grad)


def solution(mesh):
    return jax.shard_map(
        on_device,
        mesh=mesh,
        in_specs=(
            P("dp", "tensor"),
            P("dp", "tensor"),
            P(("dp", "tensor"), None),
            P(("dp", "tensor"), None),
        ),
        out_specs=(P("dp", "tensor"), P("dp", "tensor"), P("dp", "tensor")),
        check_vma=False,
    )
```

time: 342 us -> 180 us (0.53)
  waiting for transfers between devices: 267 us -> 81.1 us
  starting transfers between devices: 0.12 us -> 53.9 us
  blocking collectives: 28.1 us -> 0 us
  Pallas kernels: 0 us -> 21.9 us
  matrix products: 29.7 us -> 15.6 us
  between operations: 13.8 us -> 1.13 us
    reduce_scatter x1 -> x0, waiting for transfers between devices: 149 us -> none  [on_device(): lax.psum_scatter((product * factor).astype(jnp.bfloat16), 'dp', scatter_d...]
    all_gather x2 -> x0, waiting for transfers between devices: 117 us -> none  [the longest x1 67.4 us: on_device(): lax.all_gather(relaid, 'dp', axis=0, tiled=True)]
    ppermute x0 -> x44, waiting for transfers between devices: none -> 81.1 us  [send(): return lax.ppermute(x, ('dp', 'tensor'), pairs)]
    ppermute x0 -> x44, starting transfers between devices: none -> 53.9 us  [send(): return lax.ppermute(x, ('dp', 'tensor'), pairs)]
    all_to_all x1 -> x0, blocking collectives: 28.1 us -> none  [on_device(): lax.all_to_all(down_weight, 'tensor', split_axis=1, concat_axis=0, tiled=...]
    pallas_call x0 -> x7, Pallas kernels: none -> 21.9 us  [call(): pl.pallas_call(kernel, out_shape=outs, in_specs=[SMEM] + [VMEM] * len(arg...]
    dot_general x2 -> x5, matrix products: 29.7 us -> 15.6 us  [the longest x4 11.1 us: term(): lax.dot_general(lhs, hid, (((0,), (0,)), ((), ())), preferred_element_typ...]
  transfers between devices with their start and end apart: 3 -> 44, of which waited for: 3 -> 19; matrix products, arithmetic and copies ran while one was open for 9% -> 3% of each run, Pallas kernels for 0% -> 2%
where the time goes in v1:
time: 180 us
  waiting for transfers between devices  81.1 us (45%)
  starting transfers between devices  53.9 us (30%)
  Pallas kernels  21.9 us (12%)
  matrix products  15.6 us (9%)
  local copies, waits for them, and re-layouts  5.46 us (3%)
    ppermute x44, waiting for transfers between devices, send(): return lax.ppermute(x, ('dp', 'tensor'), pairs)  81.1 us
    ppermute x44, starting transfers between devices, send(): return lax.ppermute(x, ('dp', 'tensor'), pairs)  53.9 us
    pallas_call x7, Pallas kernels, call(): pl.pallas_call(kernel, out_shape=outs, in_specs=[SMEM] + [VMEM] * len(arg...  21.9 us
    dot_general x4, matrix products, term(): lax.dot_general(lhs, hid, (((0,), (0,)), ((), ())), preferred_element_typ...  11.1 us
    unnamed x45, local copies, waits for them, and re-layouts  5.06 us
    dot_general x1, matrix products, on_device(): mine = jnp.dot(o_all[:2 * tokens], w_all, preferred_element_type=F32)  4.48 us
  transfers between devices with their start and end apart: 44, of which 19 were waited for; matrix products, arithmetic and copies ran while one was open for 3% of the time, Pallas kernels for 2%

profile of v1, /device:TPU:0, one launch (start us, length us, event | category | flops | bytes accessed | tf_op | source)
XLA Modules:
  0.0 179.6 jit_solution(11268372148512038244)
XLA Ops:
  3.8 3.2 %collective-permute-start.17 = (bf16[32,1792]{1,0:T(8,128)(2,1)S(1)}, bf16[32,1792]{1,0:T(8,128)(2,1)S(1)}, u32[]{:S(2)}, u32[]{:S(2)}) collective-permute-start(bf16[32,1792]{1,0:T(8,128)(2,1)S(1)} %get-tuple-element.28), channel_id=1, source_target_pairs={{0,1},{1,0},{2,3},{3,2},{4,5},{5,4},{6,7},{7,6},{8,9},{9,8},{10,11... | collective-permute-start | bytes 344072 | tf_op jit(solution)/shard_map/ppermute | solution.py:22
  6.9 4.0 %collective-permute-start.18 = (bf16[32,1792]{1,0:T(8,128)(2,1)S(1)}, bf16[32,1792]{1,0:T(8,128)(2,1)S(1)}, u32[]{:S(2)}, u32[]{:S(2)}) collective-permute-start(bf16[32,1792]{1,0:T(8,128)(2,1)S(1)} %get-tuple-element.29), channel_id=1, source_target_pairs={{0,6},{1,7},{2,0},{3,1},{4,2},{5,3},{6,4},{7,5},{8,14},{9,15},{10,... | collective-permute-start | bytes 344072 | tf_op jit(solution)/shard_map/ppermute | solution.py:22
  11.3 6.0 %collective-permute-start.21 = (bf16[32,1792]{1,0:T(8,128)(2,1)S(1)}, bf16[32,1792]{1,0:T(8,128)(2,1)S(1)}, u32[]{:S(2)}, u32[]{:S(2)}) collective-permute-start(bf16[32,1792]{1,0:T(8,128)(2,1)S(1)} %get-tuple-element.32), channel_id=1, source_target_pairs={{0,5},{1,4},{2,7},{3,6},{4,1},{5,0},{6,3},{7,2},{8,13},{9,12},{10,... | collective-permute-start | bytes 344072 | tf_op jit(solution)/shard_map/ppermute | solution.py:22
  20.5 3.1 %collective-permute-start.2 = (bf16[64,2048]{1,0:T(8,128)(2,1)S(1)}, bf16[64,2048]{1,0:T(8,128)(2,1)S(1)}, u32[]{:S(2)}, u32[]{:S(2)}) collective-permute-start(bf16[64,2048]{1,0:T(8,128)(2,1)S(1)} %get-tuple-element.26), channel_id=1, source_target_pairs={{0,17},{1,16},{2,19},{3,18},{4,21},{5,20},{6,23},{7,22},{8,25},{9,... | collective-permute-start | bytes 786440 | tf_op jit(solution)/shard_map/ppermute | solution.py:22
  25.6 3.5 %collective-permute-done.23.refs_7_ = bf16[32,1792]{1,0:T(8,128)(2,1)S(1)} collective-permute-done((bf16[32,1792]{1,0:T(8,128)(2,1)S(1)}, bf16[32,1792]{1,0:T(8,128)(2,1)S(1)}, u32[]{:S(2)}, u32[]{:S(2)}) %collective-permute-start.23) | collective-permute-done | bytes 114720 | tf_op jit(solution)/shard_map/ppermute | solution.py:22
  39.0 3.1 %collective-permute-start.25 = (bf16[256,896]{1,0:T(8,128)(2,1)S(1)}, bf16[256,896]{1,0:T(8,128)(2,1)S(1)}, u32[]{:S(2)}, u32[]{:S(2)}) collective-permute-start(bf16[256,896]{1,0:T(8,128)(2,1)S(1)} %get-tuple-element.35.refs_16_), channel_id=1, source_target_pairs={{0,96},{1,97},{2,98},{3,99},{4,100},{5,101},{6,102},{7,103},{8,104... | collective-permute-start | bytes 1376264 | tf_op jit(solution)/shard_map/ppermute | solution.py:22
  46.5 5.9 %collective-permute-done.25.refs_18_ = bf16[256,896]{1,0:T(8,128)(2,1)S(1)} collective-permute-done((bf16[256,896]{1,0:T(8,128)(2,1)S(1)}, bf16[256,896]{1,0:T(8,128)(2,1)S(1)}, u32[]{:S(2)}, u32[]{:S(2)}) %collective-permute-start.25) | collective-permute-done | bytes 458784 | tf_op jit(solution)/shard_map/ppermute | solution.py:22
  55.8 3.1 %collective-permute-done.3.refs_2_ = bf16[128,2048]{1,0:T(8,128)(2,1)S(1)} collective-permute-done((bf16[128,2048]{1,0:T(8,128)(2,1)S(1)}, bf16[128,2048]{1,0:T(8,128)(2,1)S(1)}, u32[]{:S(2)}, u32[]{:S(2)}) %collective-permute-start.3) | collective-permute-done | bytes 524320 | tf_op jit(solution)/shard_map/ppermute | solution.py:22
  59.6 8.4 %collective-permute-done.6.refs_7_ = bf16[128,2048]{1,0:T(8,128)(2,1)S(1)} collective-permute-done((bf16[128,2048]{1,0:T(8,128)(2,1)S(1)}, bf16[128,2048]{1,0:T(8,128)(2,1)S(1)}, u32[]{:S(2)}, u32[]{:S(2)}) %collective-permute-start.6) | collective-permute-done | bytes 524320 | tf_op jit(solution)/shard_map/ppermute | solution.py:22
  68.0 3.7 %collective-permute-start.26 = (bf16[256,896]{1,0:T(8,128)(2,1)S(1)}, bf16[256,896]{1,0:T(8,128)(2,1)S(1)}, u32[]{:S(2)}, u32[]{:S(2)}) collective-permute-start(bf16[256,896]{1,0:T(8,128)(2,1)S(1)} %collective-permute-done.24.refs_17_), channel_id=1, source_target_pairs={{0,96},{1,97},{2,98},{3,99},{4,100},{5,101},{6,102},{7,103},{8,104... | collective-permute-start | bytes 1376264 | tf_op jit(solution)/shard_map/ppermute | solution.py:22
  72.8 9.3 %collective-permute-done.35 = bf16[512,896]{1,0:T(8,128)(2,1)S(1)} collective-permute-done((bf16[512,896]{1,0:T(8,128)(2,1)S(1)}, bf16[512,896]{1,0:T(8,128)(2,1)S(1)}, u32[]{:S(2)}, u32[]{:S(2)}) %collective-permute-start.35) | collective-permute-done | bytes 917536 | tf_op jit(solution)/shard_map/ppermute | solution.py:22
  82.6 3.7 %collective-permute-start.5 = (bf16[128,2048]{1,0:T(8,128)(2,1)S(1)}, bf16[128,2048]{1,0:T(8,128)(2,1)S(1)}, u32[]{:S(2)}, u32[]{:S(2)}) collective-permute-start(bf16[128,2048]{1,0:T(8,128)(2,1)S(1)} %collective-permute-done.3.refs_2_), channel_id=1, source_target_pairs={{0,6},{1,7},{2,0},{3,1},{4,2},{5,3},{6,4},{7,5},{8,14},{9,15},{10,... | collective-permute-start | bytes 1572872 | tf_op jit(solution)/shard_map/ppermute | solution.py:22
  86.3 4.8 %collective-permute-done.27.refs_20_ = bf16[256,896]{1,0:T(8,128)(2,1)S(1)} collective-permute-done((bf16[256,896]{1,0:T(8,128)(2,1)S(1)}, bf16[256,896]{1,0:T(8,128)(2,1)S(1)}, u32[]{:S(2)}, u32[]{:S(2)}) %collective-permute-start.27) | collective-permute-done | bytes 458784 | tf_op jit(solution)/shard_map/ppermute | solution.py:22
  91.8 5.9 %collective-permute-done.5.refs_4_ = bf16[128,2048]{1,0:T(8,128)(2,1)S(1)} collective-permute-done((bf16[128,2048]{1,0:T(8,128)(2,1)S(1)}, bf16[128,2048]{1,0:T(8,128)(2,1)S(1)}, u32[]{:S(2)}, u32[]{:S(2)}) %collective-permute-start.5) | collective-permute-done | bytes 524320 | tf_op jit(solution)/shard_map/ppermute | solution.py:22
  97.8 7.1 %collective-permute-done.7.refs_5_ = bf16[128,2048]{1,0:T(8,128)(2,1)S(1)} collective-permute-done((bf16[128,2048]{1,0:T(8,128)(2,1)S(1)}, bf16[128,2048]{1,0:T(8,128)(2,1)S(1)}, u32[]{:S(2)}, u32[]{:S(2)}) %collective-permute-start.7) | collective-permute-done | bytes 524320 | tf_op jit(solution)/shard_map/ppermute | solution.py:22
  106.0 4.6 %collective-permute-done.29.refs_21_ = bf16[256,896]{1,0:T(8,128)(2,1)S(1)} collective-permute-done((bf16[256,896]{1,0:T(8,128)(2,1)S(1)}, bf16[256,896]{1,0:T(8,128)(2,1)S(1)}, u32[]{:S(2)}, u32[]{:S(2)}) %collective-permute-start.29) | collective-permute-done | bytes 458784 | tf_op jit(solution)/shard_map/ppermute | solution.py:22
  111.4 12.6 %shard_map.69 = (bf16[2048,2048]{1,0:T(8,128)(2,1)}, bf16[2048,896]{1,0:T(8,128)(2,1)}, bf16[512,896]{1,0:T(8,128)(2,1)}, bf16[512,896]{1,0:T(8,128)(2,1)}) custom-call(s32[5]{0:T(128)S(1)} %stack.23.place, bf16[128,2048]{1,0:T(8,128)(2,1)S(1)} %constant_dynamic-update-slice_fusion.refs_0_, ...), custom_call_target="tpu_custom_call" | custom-call | flops 3758096384 | bytes 25952256 | tf_op jit(solution)/shard_map/pallas_call | solution.py:27
  124.0 4.1 %multiply_convert_fusion = bf16[512,896]{1,0:T(8,128)(2,1)S(1)} fusion(bf16[2048,896]{1,0:T(8,128)(2,1)S(1)} %constant_dynamic-update-slice_fusion.4, bf16[2048,2048]{1,0:T(8,128)(2,1)} %get-tuple-element.37), kind=kOutput, calls=%fused_computation.12 | convolution fusion | flops 1879965696 | bytes 6684672 | tf_op jit(solution)/shard_map/dot_general | solution.py:203
  130.5 4.5 %fusion = f32[1024,896]{1,0:T(8,128)S(1)} fusion(bf16[2048,896]{1,0:T(8,128)(2,1)S(1)} %copy-done.19, bf16[2048,2048]{1,0:T(8,128)(2,1)S(1)} %copy-done.18), kind=kOutput, calls=%fused_computation | convolution fusion | flops 3758096384 | bytes 11534336 | tf_op jit(solution)/shard_map/dot_general | solution.py:215
  143.4 6.1 %collective-permute-done.41 = bf16[256,896]{1,0:T(8,128)(2,1)S(1)} collective-permute-done((bf16[256,896]{1,0:T(8,128)(2,1)S(1)}, bf16[256,896]{1,0:T(8,128)(2,1)S(1)}, u32[]{:S(2)}, u32[]{:S(2)}) %collective-permute-start.41) | collective-permute-done | bytes 458784 | tf_op jit(solution)/shard_map/ppermute | solution.py:22
  149.6 3.3 %collective-permute-start.42 = (bf16[256,896]{1,0:T(8,128)(2,1)S(1)}, bf16[256,896]{1,0:T(8,128)(2,1)S(1)}, u32[]{:S(2)}, u32[]{:S(2)}) collective-permute-start(bf16[256,896]{1,0:T(8,128)(2,1)S(1)} %add_convert_fusion), channel_id=1, source_target_pairs={{0,96},{1,97},{2,98},{3,99},{4,100},{5,101},{6,102},{7,103},{8,104... | collective-permute-start | bytes 1376264 | tf_op jit(solution)/shard_map/ppermute | solution.py:22
  153.0 5.4 %collective-permute-done.32 = bf16[512,896]{1,0:T(8,128)(2,1)S(1)} collective-permute-done((bf16[512,896]{1,0:T(8,128)(2,1)S(1)}, bf16[512,896]{1,0:T(8,128)(2,1)S(1)}, u32[]{:S(2)}, u32[]{:S(2)}) %collective-permute-start.32) | collective-permute-done | bytes 917536 | tf_op jit(solution)/shard_map/ppermute | solution.py:22
  161.7 4.4 %collective-permute-done.42.bottom = bf16[256,896]{1,0:T(8,128)(2,1)S(1)} collective-permute-done((bf16[256,896]{1,0:T(8,128)(2,1)S(1)}, bf16[256,896]{1,0:T(8,128)(2,1)S(1)}, u32[]{:S(2)}, u32[]{:S(2)}) %collective-permute-start.42) | collective-permute-done | bytes 458784 | tf_op jit(solution)/shard_map/ppermute | solution.py:22
  175.3 4.3 %shard_map.70 = (bf16[512,1792]{1,0:T(8,128)(2,1)}, bf16[512,1792]{1,0:T(8,128)(2,1)}) custom-call(s32[5]{0:T(128)S(1)} %stack.23.place, bf16[512,1792]{1,0:T(8,128)(2,1)S(1)} %copy-done, bf16[512,1792]{1,0:T(8,128)(2,1)S(1)} %copy-done.2, f32[512,896]{1,0:T(8,128)S(1)} %get-tuple-element.48.mine_ref, bf16[512,896]{1,0:T(8,128)(2,1)S(1)} %collective-permute-done.31.pair_ref, ...), custom_call_target="tpu_custom_call" | custom-call | bytes 11010048 | tf_op jit(solution)/shard_map/pallas_call | solution.py:27
  (131 shorter events, 54.4 us)
Async XLA Ops:
  3.8 13.6 %collective-permute-start.17 = (bf16[32,1792]{1,0:T(8,128)(2,1)S(1)}, bf16[32,1792]{1,0:T(8,128)(2,1)S(1)}, u32[]{:S(2)}, u32[]{:S(2)}) collective-permute-start(bf16[32,1792]{1,0:T(8,128)(2,1)S(1)} %get-tuple-element.28), channel_id=1, source_target_pairs={{0,1},{1,0},{2,3},{3,2},{4,5},{5,4},{6,7},{7,6},{8,9},{9,8},{10,11... | collective-permute-start | bytes 344072 | tf_op jit(solution)/shard_map/ppermute | solution.py:22
  20.5 18.4 %collective-permute-start.2 = (bf16[64,2048]{1,0:T(8,128)(2,1)S(1)}, bf16[64,2048]{1,0:T(8,128)(2,1)S(1)}, u32[]{:S(2)}, u32[]{:S(2)}) collective-permute-start(bf16[64,2048]{1,0:T(8,128)(2,1)S(1)} %get-tuple-element.26), channel_id=1, source_target_pairs={{0,17},{1,16},{2,19},{3,18},{4,21},{5,20},{6,23},{7,22},{8,25},{9,... | collective-permute-start | bytes 786440 | tf_op jit(solution)/shard_map/ppermute | solution.py:22
  29.8 14.2 %collective-permute-start.30 = (bf16[256,896]{1,0:T(8,128)(2,1)S(1)}, bf16[256,896]{1,0:T(8,128)(2,1)S(1)}, u32[]{:S(2)}, u32[]{:S(2)}) collective-permute-start(bf16[256,896]{1,0:T(8,128)(2,1)S(1)} %get-tuple-element.35.refs_16_), channel_id=1, source_target_pairs={{0,32},{1,33},{2,34},{3,35},{4,36},{5,37},{6,38},{7,39},{8,40},{9,... | collective-permute-start | bytes 1376264 | tf_op jit(solution)/shard_map/ppermute | solution.py:22
  31.5 20.9 %collective-permute-start.9 = (bf16[128,2048]{1,0:T(8,128)(2,1)S(1)}, bf16[128,2048]{1,0:T(8,128)(2,1)S(1)}, u32[]{:S(2)}, u32[]{:S(2)}) collective-permute-start(bf16[128,2048]{1,0:T(8,128)(2,1)S(1)} %constant_dynamic-update-slice_fusion.refs_0_), channel_id=1, source_target_pairs={{0,8},{1,9},{2,10},{3,11},{4,12},{5,13},{6,14},{7,15},{8,0},{9,1},... | collective-permute-start | bytes 1572872 | tf_op jit(solution)/shard_map/ppermute | solution.py:22
  34.7 19.2 %collective-permute-start.8 = (bf16[128,2048]{1,0:T(8,128)(2,1)S(1)}, bf16[128,2048]{1,0:T(8,128)(2,1)S(1)}, u32[]{:S(2)}, u32[]{:S(2)}) collective-permute-start(bf16[128,2048]{1,0:T(8,128)(2,1)S(1)} %constant_dynamic-update-slice_fusion.refs_0_), channel_id=1, source_target_pairs={{0,2},{1,3},{2,4},{3,5},{4,6},{5,7},{6,0},{7,1},{8,10},{9,11},{10,... | collective-permute-start | bytes 1572872 | tf_op jit(solution)/shard_map/ppermute | solution.py:22
  38.9 32.9 %collective-permute-start.34 = (bf16[512,896]{1,0:T(8,128)(2,1)S(1)}, bf16[512,896]{1,0:T(8,128)(2,1)S(1)}, u32[]{:S(2)}, u32[]{:S(2)}) collective-permute-start(bf16[512,896]{1,0:T(8,128)(2,1)S(1)} %get-tuple-element.44), channel_id=1, source_target_pairs={{0,8},{1,9},{2,10},{3,11},{4,12},{5,13},{6,14},{7,15},{8,0},{9,1},... | collective-permute-start | bytes 2752520 | tf_op jit(solution)/shard_map/ppermute | solution.py:22
  44.0 14.8 %collective-permute-start.3 = (bf16[128,2048]{1,0:T(8,128)(2,1)S(1)}, bf16[128,2048]{1,0:T(8,128)(2,1)S(1)}, u32[]{:S(2)}, u32[]{:S(2)}) collective-permute-start(bf16[128,2048]{1,0:T(8,128)(2,1)S(1)} %constant_dynamic-update-slice_fusion.refs_0_), channel_id=1, source_target_pairs={{0,6},{1,7},{2,0},{3,1},{4,2},{5,3},{6,4},{7,5},{8,14},{9,15},{10,... | collective-permute-start | bytes 1572872 | tf_op jit(solution)/shard_map/ppermute | solution.py:22
  52.5 15.5 %collective-permute-start.6 = (bf16[128,2048]{1,0:T(8,128)(2,1)S(1)}, bf16[128,2048]{1,0:T(8,128)(2,1)S(1)}, u32[]{:S(2)}, u32[]{:S(2)}) collective-permute-start(bf16[128,2048]{1,0:T(8,128)(2,1)S(1)} %constant_dynamic-update-slice_fusion.2.refs_1_), channel_id=1, source_target_pairs={{0,2},{1,3},{2,4},{3,5},{4,6},{5,7},{6,0},{7,1},{8,10},{9,11},{10,... | collective-permute-start | bytes 1572872 | tf_op jit(solution)/shard_map/ppermute | solution.py:22
  53.9 17.8 %collective-permute-start.4 = (bf16[128,2048]{1,0:T(8,128)(2,1)S(1)}, bf16[128,2048]{1,0:T(8,128)(2,1)S(1)}, u32[]{:S(2)}, u32[]{:S(2)}) collective-permute-start(bf16[128,2048]{1,0:T(8,128)(2,1)S(1)} %constant_dynamic-update-slice_fusion.2.refs_1_), channel_id=1, source_target_pairs={{0,6},{1,7},{2,0},{3,1},{4,2},{5,3},{6,4},{7,5},{8,14},{9,15},{10,... | collective-permute-start | bytes 1572872 | tf_op jit(solution)/shard_map/ppermute | solution.py:22
  58.8 23.3 %collective-permute-start.35 = (bf16[512,896]{1,0:T(8,128)(2,1)S(1)}, bf16[512,896]{1,0:T(8,128)(2,1)S(1)}, u32[]{:S(2)}, u32[]{:S(2)}) collective-permute-start(bf16[512,896]{1,0:T(8,128)(2,1)S(1)} %get-tuple-element.43), channel_id=1, source_target_pairs={{0,16},{1,17},{2,18},{3,19},{4,20},{5,21},{6,22},{7,23},{8,24},{9,... | collective-permute-start | bytes 2752520 | tf_op jit(solution)/shard_map/ppermute | solution.py:22
  59.6 22.5 %collective-permute-start.28 = (bf16[256,896]{1,0:T(8,128)(2,1)S(1)}, bf16[256,896]{1,0:T(8,128)(2,1)S(1)}, u32[]{:S(2)}, u32[]{:S(2)}) collective-permute-start(bf16[256,896]{1,0:T(8,128)(2,1)S(1)} %collective-permute-done.24.refs_17_), channel_id=1, source_target_pairs={{0,32},{1,33},{2,34},{3,35},{4,36},{5,37},{6,38},{7,39},{8,40},{9,... | collective-permute-start | bytes 1376264 | tf_op jit(solution)/shard_map/ppermute | solution.py:22
  68.0 14.6 %collective-permute-start.26 = (bf16[256,896]{1,0:T(8,128)(2,1)S(1)}, bf16[256,896]{1,0:T(8,128)(2,1)S(1)}, u32[]{:S(2)}, u32[]{:S(2)}) collective-permute-start(bf16[256,896]{1,0:T(8,128)(2,1)S(1)} %collective-permute-done.24.refs_17_), channel_id=1, source_target_pairs={{0,96},{1,97},{2,98},{3,99},{4,100},{5,101},{6,102},{7,103},{8,104... | collective-permute-start | bytes 1376264 | tf_op jit(solution)/shard_map/ppermute | solution.py:22
  71.7 19.4 %collective-permute-start.27 = (bf16[256,896]{1,0:T(8,128)(2,1)S(1)}, bf16[256,896]{1,0:T(8,128)(2,1)S(1)}, u32[]{:S(2)}, u32[]{:S(2)}) collective-permute-start(bf16[256,896]{1,0:T(8,128)(2,1)S(1)} %collective-permute-done.25.refs_18_), channel_id=1, source_target_pairs={{0,96},{1,97},{2,98},{3,99},{4,100},{5,101},{6,102},{7,103},{8,104... | collective-permute-start | bytes 1376264 | tf_op jit(solution)/shard_map/ppermute | solution.py:22
  71.8 33.1 %collective-permute-start.36 = (bf16[512,896]{1,0:T(8,128)(2,1)S(1)}, bf16[512,896]{1,0:T(8,128)(2,1)S(1)}, u32[]{:S(2)}, u32[]{:S(2)}) collective-permute-start(bf16[512,896]{1,0:T(8,128)(2,1)S(1)} %collective-permute-done.34), channel_id=1, source_target_pairs={{0,16},{1,17},{2,18},{3,19},{4,20},{5,21},{6,22},{7,23},{8,24},{9,... | collective-permute-start | bytes 2752520 | tf_op jit(solution)/shard_map/ppermute | solution.py:22
  82.6 15.1 %collective-permute-start.5 = (bf16[128,2048]{1,0:T(8,128)(2,1)S(1)}, bf16[128,2048]{1,0:T(8,128)(2,1)S(1)}, u32[]{:S(2)}, u32[]{:S(2)}) collective-permute-start(bf16[128,2048]{1,0:T(8,128)(2,1)S(1)} %collective-permute-done.3.refs_2_), channel_id=1, source_target_pairs={{0,6},{1,7},{2,0},{3,1},{4,2},{5,3},{6,4},{7,5},{8,14},{9,15},{10,... | collective-permute-start | bytes 1572872 | tf_op jit(solution)/shard_map/ppermute | solution.py:22
  91.1 13.8 %collective-permute-start.7 = (bf16[128,2048]{1,0:T(8,128)(2,1)S(1)}, bf16[128,2048]{1,0:T(8,128)(2,1)S(1)}, u32[]{:S(2)}, u32[]{:S(2)}) collective-permute-start(bf16[128,2048]{1,0:T(8,128)(2,1)S(1)} %collective-permute-done.6.refs_7_), channel_id=1, source_target_pairs={{0,2},{1,3},{2,4},{3,5},{4,6},{5,7},{6,0},{7,1},{8,10},{9,11},{10,... | collective-permute-start | bytes 1572872 | tf_op jit(solution)/shard_map/ppermute | solution.py:22
  91.3 14.7 %collective-permute-start.16 = (bf16[128,2048]{1,0:T(8,128)(2,1)S(1)}, bf16[128,2048]{1,0:T(8,128)(2,1)S(1)}, u32[]{:S(2)}, u32[]{:S(2)}) collective-permute-start(bf16[128,2048]{1,0:T(8,128)(2,1)S(1)} %collective-permute-done.6.refs_7_), channel_id=1, source_target_pairs={{0,8},{1,9},{2,10},{3,11},{4,12},{5,13},{6,14},{7,15},{8,0},{9,1},... | collective-permute-start | bytes 1572872 | tf_op jit(solution)/shard_map/ppermute | solution.py:22
  91.3 14.7 %collective-permute-start.12 = (bf16[128,2048]{1,0:T(8,128)(2,1)S(1)}, bf16[128,2048]{1,0:T(8,128)(2,1)S(1)}, u32[]{:S(2)}, u32[]{:S(2)}) collective-permute-start(bf16[128,2048]{1,0:T(8,128)(2,1)S(1)} %collective-permute-done.4.refs_3_), channel_id=1, source_target_pairs={{0,8},{1,9},{2,10},{3,11},{4,12},{5,13},{6,14},{7,15},{8,0},{9,1},... | collective-permute-start | bytes 1572872 | tf_op jit(solution)/shard_map/ppermute | solution.py:22
  135.0 23.4 %collective-permute-start.32 = (bf16[512,896]{1,0:T(8,128)(2,1)S(1)}, bf16[512,896]{1,0:T(8,128)(2,1)S(1)}, u32[]{:S(2)}, u32[]{:S(2)}) collective-permute-start(bf16[512,896]{1,0:T(8,128)(2,1)S(1)} %copy-done.6), channel_id=1, source_target_pairs={{0,16},{1,17},{2,18},{3,19},{4,20},{5,21},{6,22},{7,23},{8,24},{9,... | collective-permute-start | bytes 2752520 | tf_op jit(solution)/shard_map/ppermute | solution.py:22
  135.9 13.5 %collective-permute-start.41 = (bf16[256,896]{1,0:T(8,128)(2,1)S(1)}, bf16[256,896]{1,0:T(8,128)(2,1)S(1)}, u32[]{:S(2)}, u32[]{:S(2)}) collective-permute-start(bf16[256,896]{1,0:T(8,128)(2,1)S(1)} %get-tuple-element.49), channel_id=1, source_target_pairs={{0,96},{1,97},{2,98},{3,99},{4,100},{5,101},{6,102},{7,103},{8,104... | collective-permute-start | bytes 1376264 | tf_op jit(solution)/shard_map/ppermute | solution.py:22
  140.4 34.9 %collective-permute-start.31 = (bf16[512,896]{1,0:T(8,128)(2,1)S(1)}, bf16[512,896]{1,0:T(8,128)(2,1)S(1)}, u32[]{:S(2)}, u32[]{:S(2)}) collective-permute-start(bf16[512,896]{1,0:T(8,128)(2,1)S(1)} %copy-done.5), channel_id=1, source_target_pairs={{0,16},{1,17},{2,18},{3,19},{4,20},{5,21},{6,22},{7,23},{8,24},{9,... | collective-permute-start | bytes 2752520 | tf_op jit(solution)/shard_map/ppermute | solution.py:22
  141.7 17.5 %collective-permute-start.40 = (bf16[256,896]{1,0:T(8,128)(2,1)S(1)}, bf16[256,896]{1,0:T(8,128)(2,1)S(1)}, u32[]{:S(2)}, u32[]{:S(2)}) collective-permute-start(bf16[256,896]{1,0:T(8,128)(2,1)S(1)} %slice.57), channel_id=1, source_target_pairs={{0,96},{1,97},{2,98},{3,99},{4,100},{5,101},{6,102},{7,103},{8,104... | collective-permute-start | bytes 1376264 | tf_op jit(solution)/shard_map/ppermute | solution.py:22
  149.6 16.5 %collective-permute-start.42 = (bf16[256,896]{1,0:T(8,128)(2,1)S(1)}, bf16[256,896]{1,0:T(8,128)(2,1)S(1)}, u32[]{:S(2)}, u32[]{:S(2)}) collective-permute-start(bf16[256,896]{1,0:T(8,128)(2,1)S(1)} %add_convert_fusion), channel_id=1, source_target_pairs={{0,96},{1,97},{2,98},{3,99},{4,100},{5,101},{6,102},{7,103},{8,104... | collective-permute-start | bytes 1376264 | tf_op jit(solution)/shard_map/ppermute | solution.py:22
  159.3 16.0 %collective-permute-start.33 = (bf16[512,896]{1,0:T(8,128)(2,1)S(1)}, bf16[512,896]{1,0:T(8,128)(2,1)S(1)}, u32[]{:S(2)}, u32[]{:S(2)}) collective-permute-start(bf16[512,896]{1,0:T(8,128)(2,1)S(1)} %get-tuple-element.47), channel_id=1, source_target_pairs={{0,8},{1,9},{2,10},{3,11},{4,12},{5,13},{6,14},{7,15},{8,0},{9,1},... | collective-permute-start | bytes 2752520 | tf_op jit(solution)/shard_map/ppermute | solution.py:22
  (40 other events, 501.3 us)

commit v2 on v1

v2 whole, which is shorter than its diff:
```python
import jax
import jax.numpy as jnp
import numpy as np
from jax import lax
from jax.experimental import pallas as pl
from jax.experimental.pallas import tpu as pltpu
from jax.sharding import PartitionSpec as P

SIZES = (4, 2, 2, 4, 2)
BF16, F32 = jnp.bfloat16, jnp.float32
VMEM = pl.BlockSpec(memory_space=pltpu.VMEM)
SMEM = pl.BlockSpec(memory_space=pltpu.SMEM)
EIGHT = [(k, j) for k in range(4) for j in range(2)]


def permuted(x, step):
    pairs = []
    for source in range(int(np.prod(SIZES))):
        place = [int(p) for p in np.unravel_index(source, SIZES)]
        target = [(p + d) % n for p, d, n in zip(place, step(place[2]), SIZES)]
        pairs.append((source, int(np.ravel_multi_index(target, SIZES))))
    return lax.ppermute(x, ("dp", "tensor"), pairs)


def send(x, y=0, l=0, c=0, z=0, h=0):
    return permuted(x, lambda core: (y, l, c, z, h))


def ring_y(x):
    return permuted(x, lambda core: (1 - 2 * core, 0, 0, 0, 0))


def ring_z(x):
    return permuted(x, lambda core: (0, 0, 0, 1 - 2 * core, 0))


def call(kernel, outs, place, *args, mib=40, flops=0, specs=None, grid=None, scratch=()):
    moved = sum(a.size * a.dtype.itemsize for a in args) + sum(o.size * o.dtype.itemsize for o in outs)
    whole = VMEM
    if grid is not None:
        whole = None
    specs = specs or [whole] * len(args)
    specs = [pl.BlockSpec(a.shape, lambda *_, n=a.ndim: (0,) * n) if s is None else s for s, a in zip(specs, args)]
    if grid is None:
        placed = dict(in_specs=[SMEM] + specs, out_specs=[VMEM] * len(outs), scratch_shapes=scratch)
    else:
        out_specs = [pl.BlockSpec(o.shape, lambda *_, n=len(o.shape): (0,) * n) for o in outs]
        placed = dict(
            grid_spec=pltpu.PrefetchScalarGridSpec(
                num_scalar_prefetch=1, grid=grid, in_specs=specs, out_specs=out_specs, scratch_shapes=scratch
            )
        )
    return pl.pallas_call(
        kernel,
        out_shape=outs,
        compiler_params=pltpu.CompilerParams(vmem_limit_bytes=mib << 20),
        cost_estimate=pl.CostEstimate(flops=flops, bytes_accessed=moved, transcendentals=0),
        **placed,
    )(place, *args)


def shape(*dims, dtype=BF16):
    return jax.ShapeDtypeStruct(dims, dtype)


def at(start, size, step=128):
    return pl.ds(pl.multiple_of(start, step), size)


def slot(place, k, j):
    return (place[3] + k) % 4 * 2 + (place[4] + j) % 2


def behind(place, axis, s):
    return (place[axis] + 4 + (2 * place[2] - 1) * s) % 4


def token_rows(place, n, rows):
    return at((behind(place, 3, n // 2) * 2 + (place[4] + n) % 2) * rows, rows, 64)


def pack_kernel(place, grad, weight, own, other, *parts):
    l = place[1]
    stripe = own.shape[1] // 4
    for k in range(4):
        start = k * 2 * stripe
        to = pl.ds(k * stripe, stripe)
        own[:, to] = grad[:, at(start + l * stripe, stripe)]
        other[:, to] = grad[:, at(start + (1 - l) * stripe, stripe)]
    columns = parts[0].shape[1]
    for part, (k, j) in zip(parts, EIGHT):
        part[...] = weight[:, at(slot(place, k, j) * columns, columns)]


def weight_kernel(place, *refs):
    parts, keep, give = refs[:8], refs[8], refs[9]
    c = place[2]
    rows, half = parts[0].shape[0], keep.shape[1]
    for part, (k, j) in zip(parts, EIGHT):
        to = at(slot(place, k, j) * rows, rows, 32)
        keep[to, :] = part[:, at(c * half, half)]
        give[to, :] = part[:, at((1 - c) * half, half)]


def hidden_kernel(place, gate_ref, up_ref, own, other):
    c = place[2]
    half = own.shape[1]
    rows = own.shape[0] // 8
    for n in range(8):
        block = token_rows(place, n, rows)
        for out, side in ((own, c), (other, 1 - c)):
            gate = gate_ref[block, at(side * half, half)].astype(F32)
            up = up_ref[block, at(side * half, half)].astype(F32)
            out[pl.ds(n * rows, rows), :] = (gate * jax.nn.sigmoid(gate) * up).astype(BF16)


def product_kernel(place, *refs):
    chunks, weights, out, rows_of, all_of = refs[:4], refs[4:12], refs[12], refs[13], refs[14]
    c = place[2]
    cut = weights[0].shape[0]
    for s in range(4):
        start = behind(place, 0, s) * 2 * cut
        all_of[at(start + c * cut, cut, 256), :] = weights[2 * s][...]
        all_of[at(start + (1 - c) * cut, cut, 256), :] = weights[2 * s + 1][...]
    rows = chunks[0].shape[0]
    for n in range(0, 4, 2):
        rows_of[:rows, :] = chunks[n][...]
        rows_of[rows:, :] = chunks[n + 1][...]
        product = jnp.dot(rows_of[...], all_of[...], preferred_element_type=F32)
        out[n * rows : (n + 2) * rows, :] = product.astype(out.dtype)


def term_kernel(steps, factor, place, *refs):
    chunks, (own, core, pair), outs, lhs = refs[:8], refs[8:11], refs[11:-1], refs[-1]
    step = pl.program_id(0)
    rows = chunks[0].shape[0] // 2
    tokens = 4 * rows
    for n, chunk in enumerate(chunks):
        lhs[pl.ds(n * rows, rows), :] = chunk[:rows, :]
        lhs[pl.ds(2 * tokens + n * rows, rows), :] = chunk[rows:, :]

    def part(start, size, rhs):
        return lax.dot_general(
            lhs[start : start + size, :], rhs[...], (((0,), (0,)), ((), ())), preferred_element_type=F32
        )

    product = part(0, tokens, own) + part(tokens, tokens, core) + part(2 * tokens, 2 * tokens, pair)
    product = (product * factor).astype(BF16)
    for n, out in enumerate(outs):

        @pl.when(step == n)
        def _(out=out):
            out[...] = product


def gradient_kernel(place, gate_ref, up_ref, mine_a, mine_b, pair_a, pair_b, core_ref, gate_grad, up_grad):
    c = place[2]
    half = core_ref.shape[1]
    rows = core_ref.shape[0] // 8
    for n in range(8):
        block = token_rows(place, n, rows)
        here = pl.ds(n * rows, rows)
        part = pl.ds(n % 4 * rows, rows)
        mine, pair = (mine_a, pair_a) if n < 4 else (mine_b, pair_b)
        for side, grad in (
            (c, mine[part, :] + pair[part, :].astype(F32)),
            (1 - c, core_ref[here, :].astype(F32)),
        ):
            columns = at(side * half, half)
            gate = gate_ref[block, columns].astype(F32)
            up = up_ref[block, columns].astype(F32)
            sig = jax.nn.sigmoid(gate)
            gate_grad[block, columns] = (grad * up * sig * (1.0 + gate * (1.0 - sig))).astype(BF16)
            up_grad[block, columns] = (grad * gate * sig).astype(BF16)


def join_kernel(place, mine, came, core, out):
    c = place[2]
    half = core.shape[1]
    out[:, at(c * half, half)] = (mine[...].astype(F32) + came[...].astype(F32)).astype(BF16)
    out[:, at((1 - c) * half, half)] = core[...]


def added(a, b):
    return (a.astype(F32) + b.astype(F32)).astype(BF16)


def on_device(gate_pre, up_pre, out_grad, down_weight):
    dp, tensor = lax.axis_index("dp"), lax.axis_index("tensor")
    place = jnp.stack([dp // 4, dp // 2 % 2, dp % 2, tensor // 2, tensor % 2]).astype(jnp.int32)
    tokens, columns = gate_pre.shape
    half = columns // 2
    share, width = out_grad.shape
    stripe = width // 8
    shard = down_weight.shape[0]
    cut = stripe // 2

    packed = call(
        pack_kernel,
        [shape(share, width // 2)] * 2 + [shape(shard, columns)] * 8,
        place, out_grad, down_weight,
    )
    o_own, o_other, parts = packed[0], packed[1], dict(zip(EIGHT, packed[2:]))

    o_here = jnp.concatenate([o_own, send(o_own, h=1), send(o_other, l=1), send(o_other, l=1, h=1)])
    came = {}
    for k, j in [(2, 1), (1, 1), (3, 1), (0, 1), (2, 0), (1, 0), (3, 0), (0, 0)]:
        came[(-k) % 4, j] = parts[k, j] if k == j == 0 else send(parts[k, j], z=k, h=j)

    hid_own, hid_other = call(hidden_kernel, [shape(tokens, half)] * 2, place, gate_pre, up_pre)
    hid_core = send(hid_other, c=1)
    hid_pair = send(jnp.concatenate([hid_own, hid_core]), l=1)

    keep, give = call(weight_kernel, [shape(cut, half)] * 2, place, *[came[p] for p in EIGHT])
    got = send(give, c=1)
    weights = [keep, got]
    for _ in range(3):
        weights += [ring_y(weights[-2]), ring_y(weights[-1])]

    chunks = [o_here]
    for _ in range(3):
        chunks.append(ring_z(chunks[-1]))
    cores = [send(x, c=1) for x in chunks]

    def hidden_grad(first, side, dtype):
        picked = chunks[first : first + 2] + cores[first : first + 2]
        rows = 2 * share
        specs = [pl.BlockSpec((rows, width // 2), lambda *_: (side, 0))] * 4 + [None] * 8
        return call(
            product_kernel, [shape(4 * rows, half, dtype=dtype)], place, *picked, *weights,
            specs=specs, grid=(1,), flops=2 * 4 * rows * 4 * stripe * half,
            scratch=[pltpu.VMEM((2 * rows, width // 2), BF16), pltpu.VMEM((width // 2, half), BF16)],
        )[0]

    pair_a = send(hidden_grad(0, 1, BF16), l=1)
    pair_b = send(hidden_grad(2, 1, BF16), l=1)

    factor = 1.0 / float(np.sqrt(np.float32(tokens * 16)))

    def terms(steps):
        def block(i, place):
            s = steps[0]
            for n in range(1, len(steps)):
                s = jnp.where(i // 2 == n, steps[n], s)
            return 0, behind(place, 0, s) * 2 + (1 - place[2] + i) % 2

        specs = [pl.BlockSpec((4 * share, cut), block)] * 8 + [None] * 3

        def kernel(*refs):
            term_kernel(steps, factor, *refs)

        return call(
            kernel, [shape(cut, half)] * (2 * len(steps)), place, *chunks, *cores, hid_own, hid_core, hid_pair,
            specs=specs, grid=(2 * len(steps),), flops=4 * len(steps) * 4 * tokens * cut * half,
            scratch=[pltpu.VMEM((4 * tokens, cut), BF16)],
        )

    other_1, own_1 = terms([1])
    other_2, own_2, other_3, own_3, other_0, own_0 = terms([2, 3, 0])
    other = ring_y(added(other_3, ring_y(added(other_2, ring_y(other_1)))))
    own = ring_y(added(own_3, ring_y(added(own_2, ring_y(own_1)))))
    d_core = send(added(other_0, other), c=1)
    (down_grad,) = call(join_kernel, [shape(cut, columns)], place, own_0, own, d_core)

    mine_a, mine_b = hidden_grad(0, 0, F32), hidden_grad(2, 0, F32)
    core_out = jnp.concatenate(
        [(m[tokens // 2 :] + p[tokens // 2 :].astype(F32)).astype(BF16) for m, p in ((mine_a, pair_a), (mine_b, pair_b))]
    )
    gate_grad, up_grad = call(
        gradient_kernel, [shape(tokens, columns)] * 2, place,
        gate_pre, up_pre, mine_a, mine_b, pair_a, pair_b, send(core_out, c=1),
    )
    return (gate_grad, up_grad, down_grad)


def solution(mesh):
    return jax.shard_map(
        on_device,
        mesh=mesh,
        in_specs=(
            P("dp", "tensor"),
            P("dp", "tensor"),
            P(("dp", "tensor"), None),
            P(("dp", "tensor"), None),
        ),
        out_specs=(P("dp", "tensor"), P("dp", "tensor"), P("dp", "tensor")),
        check_vma=False,
    )
```

time: 180 us -> 176 us (0.978)
  Pallas kernels: 21.9 us -> 39.1 us
  matrix products: 15.6 us -> 0 us
  starting transfers between devices: 53.9 us -> 39.8 us
  waiting for transfers between devices: 81.1 us -> 90.3 us
  local copies, waits for them, and re-layouts: 5.46 us -> 2.5 us
    pallas_call x7 -> x11, Pallas kernels: 21.9 us -> 39.1 us  [call(): pl.pallas_call(kernel, out_shape=outs, compiler_params=pltpu.CompilerPara...]
    dot_general x5 -> x0, matrix products: 15.6 us -> none  [the longest x4 11.1 us: term(): lax.dot_general(lhs, hid, (((0,), (0,)), ((), ())), preferred_element_typ...]
    ppermute x44 -> x36, starting transfers between devices: 53.9 us -> 39.8 us  [permuted(): return lax.ppermute(x, ('dp', 'tensor'), pairs)]
    ppermute x44 -> x36, waiting for transfers between devices: 81.1 us -> 90.3 us  [permuted(): return lax.ppermute(x, ('dp', 'tensor'), pairs)]
    unnamed x45 -> x15, local copies, waits for them, and re-layouts: 5.06 us -> 2.4 us
  transfers between devices with their start and end apart: 44 -> 36, of which waited for: 19 -> 18; matrix products, arithmetic and copies ran while one was open for 3% -> 1% of each run, Pallas kernels for 2% -> 21%
where the time goes in v2:
time: 176 us; the launch traced here: 175 us
  waiting for transfers between devices  90.3 us (51%)
  starting transfers between devices  39.8 us (23%)
  Pallas kernels  39.1 us (22%)
  local copies, waits for them, and re-layouts  2.5 us (1%)
  other arithmetic  1.99 us (1%)
    ppermute x36, waiting for transfers between devices, permuted(): return lax.ppermute(x, ('dp', 'tensor'), pairs)  90.3 us
    ppermute x36, starting transfers between devices, permuted(): return lax.ppermute(x, ('dp', 'tensor'), pairs)  39.8 us
    pallas_call x11, Pallas kernels, call(): pl.pallas_call(kernel, out_shape=outs, compiler_params=pltpu.CompilerPara...  39.1 us
  transfers between devices with their start and end apart: 36, of which 18 were waited for; matrix products, arithmetic and copies ran while one was open for 1% of the time, Pallas kernels for 21%

profile of v2, /device:TPU:0, one launch (start us, length us, event | category | flops | bytes accessed | tf_op | source)
XLA Modules:
  0.0 174.6 jit_solution(1976168617567803252)
XLA Ops:
  3.8 3.2 %collective-permute-start = (bf16[64,2048]{1,0:T(8,128)(2,1)S(1)}, bf16[64,2048]{1,0:T(8,128)(2,1)S(1)}, u32[]{:S(2)}, u32[]{:S(2)}) collective-permute-start(bf16[64,2048]{1,0:T(8,128)(2,1)S(1)} %get-tuple-element.27), channel_id=1, source_target_pairs={{0,1},{1,0},{2,3},{3,2},{4,5},{5,4},{6,7},{7,6},{8,9},{9,8},{10,11... | collective-permute-start | bytes 786440 | tf_op jit(solution)/shard_map/ppermute | solution.py:22
  8.1 6.4 %collective-permute-done = bf16[64,2048]{1,0:T(8,128)(2,1)S(1)} collective-permute-done((bf16[64,2048]{1,0:T(8,128)(2,1)S(1)}, bf16[64,2048]{1,0:T(8,128)(2,1)S(1)}, u32[]{:S(2)}, u32[]{:S(2)}) %collective-permute-start) | collective-permute-done | bytes 262176 | tf_op jit(solution)/shard_map/ppermute | solution.py:22
  14.6 4.6 %collective-permute-done.1 = bf16[64,2048]{1,0:T(8,128)(2,1)S(1)} collective-permute-done((bf16[64,2048]{1,0:T(8,128)(2,1)S(1)}, bf16[64,2048]{1,0:T(8,128)(2,1)S(1)}, u32[]{:S(2)}, u32[]{:S(2)}) %collective-permute-start.1) | collective-permute-done | bytes 262176 | tf_op jit(solution)/shard_map/ppermute | solution.py:22
  21.3 14.9 %collective-permute-done.3.refs_1_.refs_2_ = bf16[256,2048]{1,0:T(8,128)(2,1)S(1)} collective-permute-done((bf16[256,2048]{1,0:T(8,128)(2,1)S(1)}, bf16[256,2048]{1,0:T(8,128)(2,1)S(1)}, u32[]{:S(2)}, u32[]{:S(2)}) %collective-permute-start.3) | collective-permute-done | bytes 1048608 | tf_op jit(solution)/shard_map/ppermute | solution.py:22
  39.2 4.2 %collective-permute-start.10 = (bf16[32,1792]{1,0:T(8,128)(2,1)S(1)}, bf16[32,1792]{1,0:T(8,128)(2,1)S(1)}, u32[]{:S(2)}, u32[]{:S(2)}) collective-permute-start(bf16[32,1792]{1,0:T(8,128)(2,1)S(1)} %get-tuple-element.34), channel_id=1, source_target_pairs={{0,5},{1,4},{2,7},{3,6},{4,1},{5,0},{6,3},{7,2},{8,13},{9,12},{10,... | collective-permute-start | bytes 344072 | tf_op jit(solution)/shard_map/ppermute | solution.py:22
  45.1 3.3 %collective-permute-done.10.refs_5_ = bf16[32,1792]{1,0:T(8,128)(2,1)S(1)} collective-permute-done((bf16[32,1792]{1,0:T(8,128)(2,1)S(1)}, bf16[32,1792]{1,0:T(8,128)(2,1)S(1)}, u32[]{:S(2)}, u32[]{:S(2)}) %collective-permute-start.10) | collective-permute-done | bytes 114720 | tf_op jit(solution)/shard_map/ppermute | solution.py:22
  48.5 3.5 %collective-permute-start.6 = (bf16[32,1792]{1,0:T(8,128)(2,1)S(1)}, bf16[32,1792]{1,0:T(8,128)(2,1)S(1)}, u32[]{:S(2)}, u32[]{:S(2)}) collective-permute-start(bf16[32,1792]{1,0:T(8,128)(2,1)S(1)} %get-tuple-element.30), channel_id=1, source_target_pairs={{0,1},{1,0},{2,3},{3,2},{4,5},{5,4},{6,7},{7,6},{8,9},{9,8},{10,11... | collective-permute-start | bytes 344072 | tf_op jit(solution)/shard_map/ppermute | solution.py:22
  51.9 7.6 %collective-permute-done.11.refs_6_ = bf16[32,1792]{1,0:T(8,128)(2,1)S(1)} collective-permute-done((bf16[32,1792]{1,0:T(8,128)(2,1)S(1)}, bf16[32,1792]{1,0:T(8,128)(2,1)S(1)}, u32[]{:S(2)}, u32[]{:S(2)}) %collective-permute-start.11) | collective-permute-done | bytes 114720 | tf_op jit(solution)/shard_map/ppermute | solution.py:22
  75.3 4.6 %collective-permute-done.14.refs_6_ = bf16[256,896]{1,0:T(8,128)(2,1)S(1)} collective-permute-done((bf16[256,896]{1,0:T(8,128)(2,1)S(1)}, bf16[256,896]{1,0:T(8,128)(2,1)S(1)}, u32[]{:S(2)}, u32[]{:S(2)}) %collective-permute-start.14) | collective-permute-done | bytes 458784 | tf_op jit(solution)/shard_map/ppermute | solution.py:22
  81.1 3.9 %collective-permute-done.15.refs_7_ = bf16[256,896]{1,0:T(8,128)(2,1)S(1)} collective-permute-done((bf16[256,896]{1,0:T(8,128)(2,1)S(1)}, bf16[256,896]{1,0:T(8,128)(2,1)S(1)}, u32[]{:S(2)}, u32[]{:S(2)}) %collective-permute-start.15) | collective-permute-done | bytes 458784 | tf_op jit(solution)/shard_map/ppermute | solution.py:22
  85.2 4.7 %collective-permute-done.16.refs_8_ = bf16[256,896]{1,0:T(8,128)(2,1)S(1)} collective-permute-done((bf16[256,896]{1,0:T(8,128)(2,1)S(1)}, bf16[256,896]{1,0:T(8,128)(2,1)S(1)}, u32[]{:S(2)}, u32[]{:S(2)}) %collective-permute-start.16) | collective-permute-done | bytes 458784 | tf_op jit(solution)/shard_map/ppermute | solution.py:22
  90.1 4.7 %collective-permute-done.17.refs_9_ = bf16[256,896]{1,0:T(8,128)(2,1)S(1)} collective-permute-done((bf16[256,896]{1,0:T(8,128)(2,1)S(1)}, bf16[256,896]{1,0:T(8,128)(2,1)S(1)}, u32[]{:S(2)}, u32[]{:S(2)}) %collective-permute-start.17) | collective-permute-done | bytes 458784 | tf_op jit(solution)/shard_map/ppermute | solution.py:22
  95.3 4.4 %collective-permute-done.18.refs_10_ = bf16[256,896]{1,0:T(8,128)(2,1)S(1)} collective-permute-done((bf16[256,896]{1,0:T(8,128)(2,1)S(1)}, bf16[256,896]{1,0:T(8,128)(2,1)S(1)}, u32[]{:S(2)}, u32[]{:S(2)}) %collective-permute-start.18) | collective-permute-done | bytes 458784 | tf_op jit(solution)/shard_map/ppermute | solution.py:22
  99.9 9.5 %collective-permute-done.19.refs_11_ = bf16[256,896]{1,0:T(8,128)(2,1)S(1)} collective-permute-done((bf16[256,896]{1,0:T(8,128)(2,1)S(1)}, bf16[256,896]{1,0:T(8,128)(2,1)S(1)}, u32[]{:S(2)}, u32[]{:S(2)}) %collective-permute-start.19) | collective-permute-done | bytes 458784 | tf_op jit(solution)/shard_map/ppermute | solution.py:22
  109.4 4.1 %shard_map.71 = bf16[512,896]{1,0:T(8,128)(2,1)} custom-call(s32[5]{0:T(128)S(1)} %stack.23.place.refs_0_, bf16[256,2048]{1,0:T(8,128)(2,1)S(1)} %constant_dynamic-update-slice_fusion.refs_0_.refs_1_, bf16[256,2048]{1,0:T(8,128)(2,1)S(1)} %collective-permute-done.3.refs_1_.refs_2_, bf16[256,2048]{1,0:T(8,128)(2,1)S(1)} %collective-permute-done.4.refs_2_.refs_5_, ...), custom_call_target="tpu_custom_call" | custom-call | flops 1879048192 | bytes 8781824 | tf_op jit(solution)/shard_map/pallas_call | solution.py:53
  117.3 5.1 %collective-permute-done.28.refs_11_ = bf16[1024,896]{1,0:T(8,128)(2,1)S(1)} collective-permute-done((bf16[1024,896]{1,0:T(8,128)(2,1)S(1)}, bf16[1024,896]{1,0:T(8,128)(2,1)S(1)}, u32[]{:S(2)}, u32[]{:S(2)}) %collective-permute-start.28) | collective-permute-done | bytes 1835040 | tf_op jit(solution)/shard_map/ppermute | solution.py:22
  122.4 4.7 %shard_map.76 = (bf16[256,896]{1,0:T(8,128)(2,1)S(1)}, bf16[256,896]{1,0:T(8,128)(2,1)}) custom-call(s32[5]{0:T(128)S(1)} %stack.23.place.refs_0_, bf16[256,2048]{1,0:T(8,128)(2,1)S(1)} %constant_dynamic-update-slice_fusion.refs_0_.refs_1_, bf16[256,2048]{1,0:T(8,128)(2,1)S(1)} %collective-permute-done.3.refs_1_.refs_2_, ...), custom_call_target="tpu_custom_call" | custom-call | flops 1879048192 | bytes 12976128 | tf_op jit(solution)/shard_map/pallas_call | solution.py:53
  131.0 3.2 %shard_map.72 = bf16[512,896]{1,0:T(8,128)(2,1)S(1)} custom-call(s32[5]{0:T(128)S(1)} %stack.23.place.refs_0_, bf16[256,2048]{1,0:T(8,128)(2,1)S(1)} %collective-permute-done.20.refs_0_.refs_3_, bf16[256,2048]{1,0:T(8,128)(2,1)S(1)} %collective-permute-done.21.refs_1_.refs_4_, bf16[256,2048]{1,0:T(8,128)(2,1)S(1)} %collective-permute-done.22.refs_2_.refs_7_, ...), custom_call_target="tpu_custom_call" | custom-call | flops 1879048192 | bytes 8781824 | tf_op jit(solution)/shard_map/pallas_call | solution.py:53
  134.8 12.2 %shard_map.75 = (bf16[256,896]{1,0:T(8,128)(2,1)S(1)}, bf16[256,896]{1,0:T(8,128)(2,1)S(1)}, bf16[256,896]{1,0:T(8,128)(2,1)S(1)}, bf16[256,896]{1,0:T(8,128)(2,...) custom-call(s32[5]{0:T(128)S(1)} %stack.23.place.refs_0_, ...), custom_call_target="tpu_custom_call" | custom-call | flops 5637144576 | bytes 14811136 | tf_op jit(solution)/shard_map/pallas_call | solution.py:53
  149.0 3.2 %shard_map.70.mine_b = f32[512,896]{1,0:T(8,128)S(1)} custom-call(s32[5]{0:T(128)S(1)} %stack.23.place.refs_0_, bf16[256,2048]{1,0:T(8,128)(2,1)S(1)} %collective-permute-done.20.refs_0_.refs_3_, bf16[256,2048]{1,0:T(8,128)(2,1)S(1)} %collective-permute-done.21.refs_1_.refs_4_, bf16[256,2048]{1,0:T(8,128)(2,1)S(1)} %collective-permute-done.22.refs_2_.refs_7_, ...), custom_call_target="tpu_custom_call" | custom-call | flops 1879048192 | bytes 9699328 | tf_op jit(solution)/shard_map/pallas_call | solution.py:53
  153.4 3.7 %collective-permute-done.33 = bf16[256,896]{1,0:T(8,128)(2,1)S(1)} collective-permute-done((bf16[256,896]{1,0:T(8,128)(2,1)S(1)}, bf16[256,896]{1,0:T(8,128)(2,1)S(1)}, u32[]{:S(2)}, u32[]{:S(2)}) %collective-permute-start.33) | collective-permute-done | bytes 458784 | tf_op jit(solution)/shard_map/ppermute | solution.py:22
  157.6 4.2 %collective-permute-done.25.pair_b = bf16[512,896]{1,0:T(8,128)(2,1)S(1)} collective-permute-done((bf16[512,896]{1,0:T(8,128)(2,1)S(1)}, bf16[512,896]{1,0:T(8,128)(2,1)S(1)}, u32[]{:S(2)}, u32[]{:S(2)}) %collective-permute-start.25) | collective-permute-done | bytes 917536 | tf_op jit(solution)/shard_map/ppermute | solution.py:22
  163.3 4.7 %collective-permute-done.34 = bf16[256,896]{1,0:T(8,128)(2,1)S(1)} collective-permute-done((bf16[256,896]{1,0:T(8,128)(2,1)S(1)}, bf16[256,896]{1,0:T(8,128)(2,1)S(1)}, u32[]{:S(2)}, u32[]{:S(2)}) %collective-permute-start.34) | collective-permute-done | bytes 458784 | tf_op jit(solution)/shard_map/ppermute | solution.py:22
  168.2 4.3 %shard_map.73 = (bf16[512,1792]{1,0:T(8,128)(2,1)}, bf16[512,1792]{1,0:T(8,128)(2,1)}) custom-call(s32[5]{0:T(128)S(1)} %stack.23.place.refs_0_, bf16[512,1792]{1,0:T(8,128)(2,1)S(1)} %copy-done, bf16[512,1792]{1,0:T(8,128)(2,1)S(1)} %copy-done.2, f32[512,896]{1,0:T(8,128)S(1)} %shard_map.69.mine_a, f32[512,896]{1,0:T(8,128)S(1)} %shard_map.70.mine_b, ...), custom_call_target="tpu_custom_call" | custom-call | bytes 13762560 | tf_op jit(solution)/shard_map/pallas_call | solution.py:53
  (85 shorter events, 44.7 us)
Async XLA Ops:
  3.8 10.8 %collective-permute-start = (bf16[64,2048]{1,0:T(8,128)(2,1)S(1)}, bf16[64,2048]{1,0:T(8,128)(2,1)S(1)}, u32[]{:S(2)}, u32[]{:S(2)}) collective-permute-start(bf16[64,2048]{1,0:T(8,128)(2,1)S(1)} %get-tuple-element.27), channel_id=1, source_target_pairs={{0,1},{1,0},{2,3},{3,2},{4,5},{5,4},{6,7},{7,6},{8,9},{9,8},{10,11... | collective-permute-start | bytes 786440 | tf_op jit(solution)/shard_map/ppermute | solution.py:22
  6.9 12.3 %collective-permute-start.1 = (bf16[64,2048]{1,0:T(8,128)(2,1)S(1)}, bf16[64,2048]{1,0:T(8,128)(2,1)S(1)}, u32[]{:S(2)}, u32[]{:S(2)}) collective-permute-start(bf16[64,2048]{1,0:T(8,128)(2,1)S(1)} %get-tuple-element.28), channel_id=1, source_target_pairs={{0,16},{1,17},{2,18},{3,19},{4,20},{5,21},{6,22},{7,23},{8,24},{9,... | collective-permute-start | bytes 786440 | tf_op jit(solution)/shard_map/ppermute | solution.py:22
  7.5 11.7 %collective-permute-start.2 = (bf16[64,2048]{1,0:T(8,128)(2,1)S(1)}, bf16[64,2048]{1,0:T(8,128)(2,1)S(1)}, u32[]{:S(2)}, u32[]{:S(2)}) collective-permute-start(bf16[64,2048]{1,0:T(8,128)(2,1)S(1)} %get-tuple-element.28), channel_id=1, source_target_pairs={{0,17},{1,16},{2,19},{3,18},{4,21},{5,20},{6,23},{7,22},{8,25},{9,... | collective-permute-start | bytes 786440 | tf_op jit(solution)/shard_map/ppermute | solution.py:22
  19.3 16.9 %collective-permute-start.3 = (bf16[256,2048]{1,0:T(8,128)(2,1)S(1)}, bf16[256,2048]{1,0:T(8,128)(2,1)S(1)}, u32[]{:S(2)}, u32[]{:S(2)}) collective-permute-start(bf16[256,2048]{1,0:T(8,128)(2,1)S(1)} %constant_dynamic-update-slice_fusion.refs_0_.refs_1_), channel_id=1, source_target_pairs={{0,2},{1,3},{2,4},{3,5},{4,6},{5,7},{6,0},{7,1},{8,14},{9,15},{10,... | collective-permute-start | bytes 3145736 | tf_op jit(solution)/shard_map/ppermute | solution.py:22
  36.2 37.2 %collective-permute-start.20 = (bf16[256,2048]{1,0:T(8,128)(2,1)S(1)}, bf16[256,2048]{1,0:T(8,128)(2,1)S(1)}, u32[]{:S(2)}, u32[]{:S(2)}) collective-permute-start(bf16[256,2048]{1,0:T(8,128)(2,1)S(1)} %collective-permute-done.3.refs_1_.refs_2_), channel_id=1, source_target_pairs={{0,2},{1,3},{2,4},{3,5},{4,6},{5,7},{6,0},{7,1},{8,14},{9,15},{10,... | collective-permute-start | bytes 3145736 | tf_op jit(solution)/shard_map/ppermute | solution.py:22
  37.5 42.7 %collective-permute-start.27 = (bf16[512,896]{1,0:T(8,128)(2,1)S(1)}, bf16[512,896]{1,0:T(8,128)(2,1)S(1)}, u32[]{:S(2)}, u32[]{:S(2)}) collective-permute-start(bf16[512,896]{1,0:T(8,128)(2,1)S(1)} %get-tuple-element.42), channel_id=1, source_target_pairs={{0,8},{1,9},{2,10},{3,11},{4,12},{5,13},{6,14},{7,15},{8,0},{9,1},... | collective-permute-start | bytes 2752520 | tf_op jit(solution)/shard_map/ppermute | solution.py:22
  43.5 16.1 %collective-permute-start.11 = (bf16[32,1792]{1,0:T(8,128)(2,1)S(1)}, bf16[32,1792]{1,0:T(8,128)(2,1)S(1)}, u32[]{:S(2)}, u32[]{:S(2)}) collective-permute-start(bf16[32,1792]{1,0:T(8,128)(2,1)S(1)} %get-tuple-element.35), channel_id=1, source_target_pairs={{0,2},{1,3},{2,4},{3,5},{4,6},{5,7},{6,0},{7,1},{8,10},{9,11},{10,... | collective-permute-start | bytes 344072 | tf_op jit(solution)/shard_map/ppermute | solution.py:22
  44.1 16.5 %collective-permute-start.12 = (bf16[32,1792]{1,0:T(8,128)(2,1)S(1)}, bf16[32,1792]{1,0:T(8,128)(2,1)S(1)}, u32[]{:S(2)}, u32[]{:S(2)}) collective-permute-start(bf16[32,1792]{1,0:T(8,128)(2,1)S(1)} %get-tuple-element.36), channel_id=1, source_target_pairs={{0,3},{1,2},{2,5},{3,4},{4,7},{5,6},{6,1},{7,0},{8,11},{9,10},{10,... | collective-permute-start | bytes 344072 | tf_op jit(solution)/shard_map/ppermute | solution.py:22
  48.5 14.6 %collective-permute-start.6 = (bf16[32,1792]{1,0:T(8,128)(2,1)S(1)}, bf16[32,1792]{1,0:T(8,128)(2,1)S(1)}, u32[]{:S(2)}, u32[]{:S(2)}) collective-permute-start(bf16[32,1792]{1,0:T(8,128)(2,1)S(1)} %get-tuple-element.30), channel_id=1, source_target_pairs={{0,1},{1,0},{2,3},{3,2},{4,5},{5,4},{6,7},{7,6},{8,9},{9,8},{10,11... | collective-permute-start | bytes 344072 | tf_op jit(solution)/shard_map/ppermute | solution.py:22
  71.8 18.1 %collective-permute-start.4 = (bf16[256,2048]{1,0:T(8,128)(2,1)S(1)}, bf16[256,2048]{1,0:T(8,128)(2,1)S(1)}, u32[]{:S(2)}, u32[]{:S(2)}) collective-permute-start(bf16[256,2048]{1,0:T(8,128)(2,1)S(1)} %constant_dynamic-update-slice_fusion.refs_0_.refs_1_), channel_id=1, source_target_pairs={{0,8},{1,9},{2,10},{3,11},{4,12},{5,13},{6,14},{7,15},{8,0},{9,1},... | collective-permute-start | bytes 3145736 | tf_op jit(solution)/shard_map/ppermute | solution.py:22
  73.4 21.5 %collective-permute-start.21 = (bf16[256,2048]{1,0:T(8,128)(2,1)S(1)}, bf16[256,2048]{1,0:T(8,128)(2,1)S(1)}, u32[]{:S(2)}, u32[]{:S(2)}) collective-permute-start(bf16[256,2048]{1,0:T(8,128)(2,1)S(1)} %collective-permute-done.20.refs_0_.refs_3_), channel_id=1, source_target_pairs={{0,2},{1,3},{2,4},{3,5},{4,6},{5,7},{6,0},{7,1},{8,14},{9,15},{10,... | collective-permute-start | bytes 3145736 | tf_op jit(solution)/shard_map/ppermute | solution.py:22
  79.9 10.0 %collective-permute-start.16 = (bf16[256,896]{1,0:T(8,128)(2,1)S(1)}, bf16[256,896]{1,0:T(8,128)(2,1)S(1)}, u32[]{:S(2)}, u32[]{:S(2)}) collective-permute-start(bf16[256,896]{1,0:T(8,128)(2,1)S(1)} %collective-permute-done.14.refs_6_), channel_id=1, source_target_pairs={{0,32},{1,33},{2,34},{3,35},{4,36},{5,37},{6,38},{7,39},{8,104},{9... | collective-permute-start | bytes 1376264 | tf_op jit(solution)/shard_map/ppermute | solution.py:22
  80.4 42.0 %collective-permute-start.28 = (bf16[1024,896]{1,0:T(8,128)(2,1)S(1)}, bf16[1024,896]{1,0:T(8,128)(2,1)S(1)}, u32[]{:S(2)}, u32[]{:S(2)}) collective-permute-start(bf16[1024,896]{1,0:T(8,128)(2,1)S(1)} %pad_maximum_fusion), channel_id=1, source_target_pairs={{0,16},{1,17},{2,18},{3,19},{4,20},{5,21},{6,22},{7,23},{8,24},{9,... | collective-permute-start | bytes 5505032 | tf_op jit(solution)/shard_map/ppermute | solution.py:22
  85.0 9.8 %collective-permute-start.17 = (bf16[256,896]{1,0:T(8,128)(2,1)S(1)}, bf16[256,896]{1,0:T(8,128)(2,1)S(1)}, u32[]{:S(2)}, u32[]{:S(2)}) collective-permute-start(bf16[256,896]{1,0:T(8,128)(2,1)S(1)} %collective-permute-done.15.refs_7_), channel_id=1, source_target_pairs={{0,32},{1,33},{2,34},{3,35},{4,36},{5,37},{6,38},{7,39},{8,104},{9... | collective-permute-start | bytes 1376264 | tf_op jit(solution)/shard_map/ppermute | solution.py:22
  89.9 19.5 %collective-permute-start.5 = (bf16[256,2048]{1,0:T(8,128)(2,1)S(1)}, bf16[256,2048]{1,0:T(8,128)(2,1)S(1)}, u32[]{:S(2)}, u32[]{:S(2)}) collective-permute-start(bf16[256,2048]{1,0:T(8,128)(2,1)S(1)} %collective-permute-done.3.refs_1_.refs_2_), channel_id=1, source_target_pairs={{0,8},{1,9},{2,10},{3,11},{4,12},{5,13},{6,14},{7,15},{8,0},{9,1},... | collective-permute-start | bytes 3145736 | tf_op jit(solution)/shard_map/ppermute | solution.py:22
  89.9 9.8 %collective-permute-start.18 = (bf16[256,896]{1,0:T(8,128)(2,1)S(1)}, bf16[256,896]{1,0:T(8,128)(2,1)S(1)}, u32[]{:S(2)}, u32[]{:S(2)}) collective-permute-start(bf16[256,896]{1,0:T(8,128)(2,1)S(1)} %collective-permute-done.16.refs_8_), channel_id=1, source_target_pairs={{0,32},{1,33},{2,34},{3,35},{4,36},{5,37},{6,38},{7,39},{8,104},{9... | collective-permute-start | bytes 1376264 | tf_op jit(solution)/shard_map/ppermute | solution.py:22
  94.8 27.6 %collective-permute-start.22 = (bf16[256,2048]{1,0:T(8,128)(2,1)S(1)}, bf16[256,2048]{1,0:T(8,128)(2,1)S(1)}, u32[]{:S(2)}, u32[]{:S(2)}) collective-permute-start(bf16[256,2048]{1,0:T(8,128)(2,1)S(1)} %collective-permute-done.20.refs_0_.refs_3_), channel_id=1, source_target_pairs={{0,8},{1,9},{2,10},{3,11},{4,12},{5,13},{6,14},{7,15},{8,0},{9,1},... | collective-permute-start | bytes 3145736 | tf_op jit(solution)/shard_map/ppermute | solution.py:22
  94.8 27.6 %collective-permute-start.23 = (bf16[256,2048]{1,0:T(8,128)(2,1)S(1)}, bf16[256,2048]{1,0:T(8,128)(2,1)S(1)}, u32[]{:S(2)}, u32[]{:S(2)}) collective-permute-start(bf16[256,2048]{1,0:T(8,128)(2,1)S(1)} %collective-permute-done.21.refs_1_.refs_4_), channel_id=1, source_target_pairs={{0,8},{1,9},{2,10},{3,11},{4,12},{5,13},{6,14},{7,15},{8,0},{9,1},... | collective-permute-start | bytes 3145736 | tf_op jit(solution)/shard_map/ppermute | solution.py:22
  113.5 35.4 %collective-permute-start.24 = (bf16[512,896]{1,0:T(8,128)(2,1)}, bf16[512,896]{1,0:T(8,128)(2,1)S(1)}, u32[]{:S(2)}, u32[]{:S(2)}) collective-permute-start(bf16[512,896]{1,0:T(8,128)(2,1)} %shard_map.71), channel_id=1, source_target_pairs={{0,16},{1,17},{2,18},{3,19},{4,20},{5,21},{6,22},{7,23},{8,24},{9,... | collective-permute-start | bytes 2752520 | tf_op jit(solution)/shard_map/ppermute | solution.py:22
  127.1 19.9 %collective-permute-start.32 = (bf16[256,896]{1,0:T(8,128)(2,1)S(1)}, bf16[256,896]{1,0:T(8,128)(2,1)S(1)}, u32[]{:S(2)}, u32[]{:S(2)}) collective-permute-start(bf16[256,896]{1,0:T(8,128)(2,1)S(1)} %get-tuple-element.50), channel_id=1, source_target_pairs={{0,32},{1,33},{2,34},{3,35},{4,36},{5,37},{6,38},{7,39},{8,104},{9... | collective-permute-start | bytes 1376264 | tf_op jit(solution)/shard_map/ppermute | solution.py:22
  129.7 22.5 %collective-permute-start.29 = (bf16[256,896]{1,0:T(8,128)(2,1)}, bf16[256,896]{1,0:T(8,128)(2,1)}, u32[]{:S(2)}, u32[]{:S(2)}) collective-permute-start(bf16[256,896]{1,0:T(8,128)(2,1)} %get-tuple-element.46), channel_id=1, source_target_pairs={{0,32},{1,33},{2,34},{3,35},{4,36},{5,37},{6,38},{7,39},{8,104},{9... | collective-permute-start | bytes 1376264 | tf_op jit(solution)/shard_map/ppermute | solution.py:22
  134.2 27.5 %collective-permute-start.25 = (bf16[512,896]{1,0:T(8,128)(2,1)S(1)}, bf16[512,896]{1,0:T(8,128)(2,1)S(1)}, u32[]{:S(2)}, u32[]{:S(2)}) collective-permute-start(bf16[512,896]{1,0:T(8,128)(2,1)S(1)} %shard_map.72), channel_id=1, source_target_pairs={{0,16},{1,17},{2,18},{3,19},{4,20},{5,21},{6,22},{7,23},{8,24},{9,... | collective-permute-start | bytes 2752520 | tf_op jit(solution)/shard_map/ppermute | solution.py:22
  147.2 10.0 %collective-permute-start.33 = (bf16[256,896]{1,0:T(8,128)(2,1)S(1)}, bf16[256,896]{1,0:T(8,128)(2,1)S(1)}, u32[]{:S(2)}, u32[]{:S(2)}) collective-permute-start(bf16[256,896]{1,0:T(8,128)(2,1)S(1)} %add_convert_fusion.2), channel_id=1, source_target_pairs={{0,32},{1,33},{2,34},{3,35},{4,36},{5,37},{6,38},{7,39},{8,104},{9... | collective-permute-start | bytes 1376264 | tf_op jit(solution)/shard_map/ppermute | solution.py:22
  157.3 10.8 %collective-permute-start.34 = (bf16[256,896]{1,0:T(8,128)(2,1)S(1)}, bf16[256,896]{1,0:T(8,128)(2,1)S(1)}, u32[]{:S(2)}, u32[]{:S(2)}) collective-permute-start(bf16[256,896]{1,0:T(8,128)(2,1)S(1)} %add_convert_fusion.1), channel_id=1, source_target_pairs={{0,32},{1,33},{2,34},{3,35},{4,36},{5,37},{6,38},{7,39},{8,104},{9... | collective-permute-start | bytes 1376264 | tf_op jit(solution)/shard_map/ppermute | solution.py:22
  (18 other events, 176.3 us)

commit v3 on v2

--- a/solution.py
+++ b/solution.py
@@ -115,7 +115,7 @@
 
 
 def product_kernel(place, *refs):
-    chunks, weights, out, rows_of, all_of = refs[:4], refs[4:12], refs[12], refs[13], refs[14]
+    chunks, weights, out, rows_of, all_of = refs[:8], refs[8:16], refs[16], refs[17], refs[18]
     c = place[2]
     cut = weights[0].shape[0]
     for s in range(4):
@@ -123,28 +123,30 @@
         all_of[at(start + c * cut, cut, 256), :] = weights[2 * s][...]
         all_of[at(start + (1 - c) * cut, cut, 256), :] = weights[2 * s + 1][...]
     rows = chunks[0].shape[0]
-    for n in range(0, 4, 2):
-        rows_of[:rows, :] = chunks[n][...]
-        rows_of[rows:, :] = chunks[n + 1][...]
+    for n in range(0, 8, 4):
+        for m in range(4):
+            rows_of[m * rows : (m + 1) * rows, :] = chunks[n + m][...]
         product = jnp.dot(rows_of[...], all_of[...], preferred_element_type=F32)
-        out[n * rows : (n + 2) * rows, :] = product.astype(out.dtype)
+        out[n * rows : (n + 4) * rows, :] = product.astype(out.dtype)
 
 
 def term_kernel(steps, factor, place, *refs):
-    chunks, (own, core, pair), outs, lhs = refs[:8], refs[8:11], refs[11:-1], refs[-1]
+    chunks, rights, outs, lhs = refs[:16], refs[16:21], refs[21:-1], refs[-1]
     step = pl.program_id(0)
     rows = chunks[0].shape[0] // 2
-    tokens = 4 * rows
+    tokens = 8 * rows
     for n, chunk in enumerate(chunks):
-        lhs[pl.ds(n * rows, rows), :] = chunk[:rows, :]
-        lhs[pl.ds(2 * tokens + n * rows, rows), :] = chunk[rows:, :]
-
-    def part(start, size, rhs):
-        return lax.dot_general(
-            lhs[start : start + size, :], rhs[...], (((0,), (0,)), ((), ())), preferred_element_type=F32
+        to = n // 8 * tokens + (n % 4 * 2 + n // 4 % 2) * rows
+        lhs[pl.ds(to, rows), :] = chunk[:rows, :]
+        lhs[pl.ds(2 * tokens + to, rows), :] = chunk[rows:, :]
+
+    product, start = None, 0
+    for right in rights:
+        stop = start + right.shape[0]
+        part = lax.dot_general(
+            lhs[start:stop, :], right[...], (((0,), (0,)), ((), ())), preferred_element_type=F32
         )
-
-    product = part(0, tokens, own) + part(tokens, tokens, core) + part(2 * tokens, 2 * tokens, pair)
+        product, start = part if product is None else product + part, stop
     product = (product * factor).astype(BF16)
     for n, out in enumerate(outs):
 
@@ -181,6 +183,10 @@
     out[:, at((1 - c) * half, half)] = core[...]
 
 
+def tied(x, *first):
+    return lax.optimization_barrier((x, first))[0]
+
+
 def added(a, b):
     return (a.astype(F32) + b.astype(F32)).astype(BF16)
 
@@ -202,67 +208,79 @@
     )
     o_own, o_other, parts = packed[0], packed[1], dict(zip(EIGHT, packed[2:]))
 
-    o_here = jnp.concatenate([o_own, send(o_own, h=1), send(o_other, l=1), send(o_other, l=1, h=1)])
-    came = {}
-    for k, j in [(2, 1), (1, 1), (3, 1), (0, 1), (2, 0), (1, 0), (3, 0), (0, 0)]:
-        came[(-k) % 4, j] = parts[k, j] if k == j == 0 else send(parts[k, j], z=k, h=j)
+    o_pair = send(o_other, l=1)
+    came = {(0, 0): parts[0, 0]}
+    for k, j in [(2, 0), (2, 1), (1, 0), (3, 0), (1, 1), (3, 1), (0, 1)]:
+        came[(-k) % 4, j] = send(parts[k, j], z=k, h=j)
+    o_near = tied(jnp.concatenate([o_own, o_pair]), came[2, 0], came[2, 1])
+    o_far = jnp.concatenate([send(o_own, h=1), send(o_other, l=1, h=1)])
 
     hid_own, hid_other = call(hidden_kernel, [shape(tokens, half)] * 2, place, gate_pre, up_pre)
     hid_core = send(hid_other, c=1)
-    hid_pair = send(jnp.concatenate([hid_own, hid_core]), l=1)
-
-    keep, give = call(weight_kernel, [shape(cut, half)] * 2, place, *[came[p] for p in EIGHT])
-    got = send(give, c=1)
-    weights = [keep, got]
-    for _ in range(3):
-        weights += [ring_y(weights[-2]), ring_y(weights[-1])]
-
-    chunks = [o_here]
-    for _ in range(3):
-        chunks.append(ring_z(chunks[-1]))
-    cores = [send(x, c=1) for x in chunks]
-
-    def hidden_grad(first, side, dtype):
-        picked = chunks[first : first + 2] + cores[first : first + 2]
+    hid_pair_own = send(hid_own, l=1)
+    hid_pair_core = [send(hid_core[:cut], l=1), send(hid_core[cut:], l=1)]
+
+    arrived = tied([came[p] for p in EIGHT], hid_core)
+    keep, give = call(weight_kernel, [shape(cut, half)] * 2, place, *arrived)
+    keep, got, near, far = [keep], [send(give, c=1)], [o_near], [o_far]
+    near.append(ring_z(near[0]))
+    far.append(ring_z(far[0]))
+    for s in range(3):
+        keep.append(ring_y(keep[s]))
+        got.append(ring_y(got[s]))
+    near.append(ring_z(tied(near[1], keep[0])))
+    far.append(ring_z(tied(far[1], got[0])))
+    near.append(ring_z(tied(near[2], keep[1], hid_pair_own)))
+    far.append(ring_z(tied(far[2], got[1])))
+    weights = [w for pair in zip(keep, got) for w in pair]
+    chunks = near + far
+    last = tied(near[3], keep[2], hid_pair_core[0]), tied(far[3], got[2], hid_pair_core[1])
+    cores = [send(x, c=1) for x in near[:3] + [last[0]] + far[:3] + [last[1]]]
+
+    def hidden_grad(first, side, dtype, *after):
+        picked = [x[n + f] for x in (chunks, cores) for n in (first, first + 1) for f in (0, 4)]
         rows = 2 * share
-        specs = [pl.BlockSpec((rows, width // 2), lambda *_: (side, 0))] * 4 + [None] * 8
+        specs = [pl.BlockSpec((share, width // 2), lambda *_: (side, 0))] * 8 + [None] * 8
         return call(
-            product_kernel, [shape(4 * rows, half, dtype=dtype)], place, *picked, *weights,
+            product_kernel, [shape(4 * rows, half, dtype=dtype)], place, *tied(picked, *after), *weights,
             specs=specs, grid=(1,), flops=2 * 4 * rows * 4 * stripe * half,
-            scratch=[pltpu.VMEM((2 * rows, width // 2), BF16), pltpu.VMEM((width // 2, half), BF16)],
+            scratch=[pltpu.VMEM((4 * share, width // 2), BF16), pltpu.VMEM((width // 2, half), BF16)],
         )[0]
 
-    pair_a = send(hidden_grad(0, 1, BF16), l=1)
-    pair_b = send(hidden_grad(2, 1, BF16), l=1)
-
     factor = 1.0 / float(np.sqrt(np.float32(tokens * 16)))
 
-    def terms(steps):
+    def terms(steps, *after):
         def block(i, place):
             s = steps[0]
             for n in range(1, len(steps)):
                 s = jnp.where(i // 2 == n, steps[n], s)
             return 0, behind(place, 0, s) * 2 + (1 - place[2] + i) % 2
 
-        specs = [pl.BlockSpec((4 * share, cut), block)] * 8 + [None] * 3
+        specs = [pl.BlockSpec((2 * share, cut), block)] * 16 + [None] * 5
 
         def kernel(*refs):
             term_kernel(steps, factor, *refs)
 
         return call(
-            kernel, [shape(cut, half)] * (2 * len(steps)), place, *chunks, *cores, hid_own, hid_core, hid_pair,
+            kernel, [shape(cut, half)] * (2 * len(steps)), place, *tied(chunks + cores, *after),
+            hid_own, hid_core, hid_pair_own, *hid_pair_core,
             specs=specs, grid=(2 * len(steps),), flops=4 * len(steps) * 4 * tokens * cut * half,
             scratch=[pltpu.VMEM((4 * tokens, cut), BF16)],
         )
 
-    other_1, own_1 = terms([1])
-    other_2, own_2, other_3, own_3, other_0, own_0 = terms([2, 3, 0])
+    pair_a = hidden_grad(0, 1, BF16)
+    other_1, own_1 = terms([1], pair_a)
+    pair_b = hidden_grad(2, 1, BF16, other_1)
+    other_2, own_2 = terms([2], pair_b)
+    mine_a = hidden_grad(0, 0, F32, other_2)
+    other_3, own_3 = terms([3], mine_a)
+    mine_b = hidden_grad(2, 0, F32, other_3)
+    other_0, own_0 = terms([0], mine_b)
+    pair_a, pair_b = send(pair_a, l=1), send(pair_b, l=1)
     other = ring_y(added(other_3, ring_y(added(other_2, ring_y(other_1)))))
     own = ring_y(added(own_3, ring_y(added(own_2, ring_y(own_1)))))
     d_core = send(added(other_0, other), c=1)
     (down_grad,) = call(join_kernel, [shape(cut, columns)], place, own_0, own, d_core)
-
-    mine_a, mine_b = hidden_grad(0, 0, F32), hidden_grad(2, 0, F32)
     core_out = jnp.concatenate(
         [(m[tokens // 2 :] + p[tokens // 2 :].astype(F32)).astype(BF16) for m, p in ((mine_a, pair_a), (mine_b, pair_b))]
     )

time: 176 us -> 174 us (0.989)
  waiting for transfers between devices: 90.3 us -> 78.1 us
  starting transfers between devices: 39.8 us -> 45 us
  local copies, waits for them, and re-layouts: 2.5 us -> 6.22 us
    ppermute x36 -> x45, waiting for transfers between devices: 90.3 us -> 78.1 us  [permuted(): return lax.ppermute(x, ('dp', 'tensor'), pairs)]
    ppermute x36 -> x45, starting transfers between devices: 39.8 us -> 45 us  [permuted(): return lax.ppermute(x, ('dp', 'tensor'), pairs)]
    unnamed x15 -> x25, local copies, waits for them, and re-layouts: 2.4 us -> 6.05 us
    pallas_call x11 -> x13, Pallas kernels: 39.1 us -> 39.8 us  [call(): pl.pallas_call(kernel, out_shape=outs, compiler_params=pltpu.CompilerPara...]
  transfers between devices with their start and end apart: 36 -> 45, of which waited for: 18 -> 17; matrix products, arithmetic and copies ran while one was open for 1% -> 2% of each run, Pallas kernels for 21% -> 22%
where the time goes in v3:
time: 174 us; the launch traced here: 173 us
  waiting for transfers between devices  78.1 us (45%)
  starting transfers between devices  45 us (26%)
  Pallas kernels  39.8 us (23%)
  local copies, waits for them, and re-layouts  6.22 us (4%)
  other arithmetic  2.91 us (2%)
    ppermute x45, waiting for transfers between devices, permuted(): return lax.ppermute(x, ('dp', 'tensor'), pairs)  78.1 us
    ppermute x45, starting transfers between devices, permuted(): return lax.ppermute(x, ('dp', 'tensor'), pairs)  45 us
    pallas_call x13, Pallas kernels, call(): pl.pallas_call(kernel, out_shape=outs, compiler_params=pltpu.CompilerPara...  39.8 us
    unnamed x25, local copies, waits for them, and re-layouts  6.05 us
  transfers between devices with their start and end apart: 45, of which 17 were waited for; matrix products, arithmetic and copies ran while one was open for 2% of the time, Pallas kernels for 22%

profile of v3, /device:TPU:0, one launch (start us, length us, event | category | flops | bytes accessed | tf_op | source)
XLA Modules:
  0.0 173.0 jit_solution(13364905897701182047)
XLA Ops:
  9.7 2.8 %collective-permute-start.3 = (bf16[64,2048]{1,0:T(8,128)(2,1)S(1)}, bf16[64,2048]{1,0:T(8,128)(2,1)S(1)}, u32[]{:S(2)}, u32[]{:S(2)}) collective-permute-start(bf16[64,2048]{1,0:T(8,128)(2,1)S(1)} %get-tuple-element.138), channel_id=1, source_target_pairs={{0,1},{1,0},{2,3},{3,2},{4,5},{5,4},{6,7},{7,6},{8,9},{9,8},{10,11... | collective-permute-start | bytes 786440 | tf_op jit(solution)/shard_map/ppermute | solution.py:22
  12.9 4.0 %collective-permute-start.1 = (bf16[32,1792]{1,0:T(8,128)(2,1)S(1)}, bf16[32,1792]{1,0:T(8,128)(2,1)S(1)}, u32[]{:S(2)}, u32[]{:S(2)}) collective-permute-start(bf16[32,1792]{1,0:T(8,128)(2,1)S(1)} %get-tuple-element.140), channel_id=1, source_target_pairs={{0,4},{1,5},{2,6},{3,7},{4,0},{5,1},{6,2},{7,3},{8,12},{9,13},{10,... | collective-permute-start | bytes 344072 | tf_op jit(solution)/shard_map/ppermute | solution.py:22
  21.9 3.9 %collective-permute-done.2.refs_5_ = bf16[32,1792]{1,0:T(8,128)(2,1)S(1)} collective-permute-done((bf16[32,1792]{1,0:T(8,128)(2,1)S(1)}, bf16[32,1792]{1,0:T(8,128)(2,1)S(1)}, u32[]{:S(2)}, u32[]{:S(2)}) %collective-permute-start.2) | collective-permute-done | bytes 114720 | tf_op jit(solution)/shard_map/ppermute | solution.py:22
  27.1 5.2 %collective-permute-start.13 = (bf16[32,1792]{1,0:T(8,128)(2,1)S(1)}, bf16[32,1792]{1,0:T(8,128)(2,1)S(1)}, u32[]{:S(2)}, u32[]{:S(2)}) collective-permute-start(bf16[32,1792]{1,0:T(8,128)(2,1)S(1)} %get-tuple-element.146), channel_id=1, source_target_pairs={{0,7},{1,6},{2,1},{3,0},{4,3},{5,2},{6,5},{7,4},{8,15},{9,14},{10,... | collective-permute-start | bytes 344072 | tf_op jit(solution)/shard_map/ppermute | solution.py:22
  33.5 18.8 %collective-permute-done.13.refs_3_ = bf16[32,1792]{1,0:T(8,128)(2,1)S(1)} collective-permute-done((bf16[32,1792]{1,0:T(8,128)(2,1)S(1)}, bf16[32,1792]{1,0:T(8,128)(2,1)S(1)}, u32[]{:S(2)}, u32[]{:S(2)}) %collective-permute-start.13) | collective-permute-done | bytes 114720 | tf_op jit(solution)/shard_map/ppermute | solution.py:22
  54.1 7.8 %collective-permute-done.15.refs_7_ = bf16[32,1792]{1,0:T(8,128)(2,1)S(1)} collective-permute-done((bf16[32,1792]{1,0:T(8,128)(2,1)S(1)}, bf16[32,1792]{1,0:T(8,128)(2,1)S(1)}, u32[]{:S(2)}, u32[]{:S(2)}) %collective-permute-start.15) | collective-permute-done | bytes 114720 | tf_op jit(solution)/shard_map/ppermute | solution.py:22
  67.8 4.7 %collective-permute-done.18.refs_10_ = bf16[256,896]{1,0:T(8,128)(2,1)S(1)} collective-permute-done((bf16[256,896]{1,0:T(8,128)(2,1)S(1)}, bf16[256,896]{1,0:T(8,128)(2,1)S(1)}, u32[]{:S(2)}, u32[]{:S(2)}) %collective-permute-start.18) | collective-permute-done | bytes 458784 | tf_op jit(solution)/shard_map/ppermute | solution.py:22
  80.3 5.6 %collective-permute-done.31.refs_21_ = bf16[256,896]{1,0:T(8,128)(2,1)S(1)} collective-permute-done((bf16[256,896]{1,0:T(8,128)(2,1)S(1)}, bf16[256,896]{1,0:T(8,128)(2,1)S(1)}, u32[]{:S(2)}, u32[]{:S(2)}) %collective-permute-start.31) | collective-permute-done | bytes 458784 | tf_op jit(solution)/shard_map/ppermute | solution.py:22
  86.9 7.3 %collective-permute-done.27.refs_20_ = bf16[256,896]{1,0:T(8,128)(2,1)S(1)} collective-permute-done((bf16[256,896]{1,0:T(8,128)(2,1)S(1)}, bf16[256,896]{1,0:T(8,128)(2,1)S(1)}, u32[]{:S(2)}, u32[]{:S(2)}) %collective-permute-start.27) | collective-permute-done | bytes 458784 | tf_op jit(solution)/shard_map/ppermute | solution.py:22
  98.6 6.0 %collective-permute-done.33.refs_14_ = bf16[256,896]{1,0:T(8,128)(2,1)S(1)} collective-permute-done((bf16[256,896]{1,0:T(8,128)(2,1)S(1)}, bf16[256,896]{1,0:T(8,128)(2,1)S(1)}, u32[]{:S(2)}, u32[]{:S(2)}) %collective-permute-start.33) | collective-permute-done | bytes 458784 | tf_op jit(solution)/shard_map/ppermute | solution.py:22
  104.6 4.9 %collective-permute-done.34.refs_15_ = bf16[256,896]{1,0:T(8,128)(2,1)S(1)} collective-permute-done((bf16[256,896]{1,0:T(8,128)(2,1)S(1)}, bf16[256,896]{1,0:T(8,128)(2,1)S(1)}, u32[]{:S(2)}, u32[]{:S(2)}) %collective-permute-start.34) | collective-permute-done | bytes 458784 | tf_op jit(solution)/shard_map/ppermute | solution.py:22
  109.5 3.2 %shard_map.70 = bf16[512,896]{1,0:T(8,128)(2,1)S(1)} custom-call(s32[5]{0:T(128)S(1)} %stack.23.place.refs_0_, bf16[128,2048]{1,0:T(8,128)(2,1)S(1)} %pad_maximum_fusion.1.refs_0_.refs_1_, bf16[128,2048]{1,0:T(8,128)(2,1)S(1)} %constant_dynamic-update-slice_fusion.refs_1_.refs_5_, bf16[128,2048]{1,0:T(8,128)(2,1)S(1)} %collective-permute-done.5.refs_2_, ...), custom_call_target="tpu_custom_call" | custom-call | flops 1879048192 | bytes 8781824 | tf_op jit(solution)/shard_map/pallas_call | solution.py:53
  113.9 5.2 %shard_map.71 = (bf16[256,896]{1,0:T(8,128)(2,1)}, bf16[256,896]{1,0:T(8,128)(2,1)}) custom-call(s32[5]{0:T(128)S(1)} %stack.23.place.refs_0_, bf16[128,2048]{1,0:T(8,128)(2,1)S(1)} %pad_maximum_fusion.1.refs_0_.refs_1_, bf16[128,2048]{1,0:T(8,128)(2,1)S(1)} %collective-permute-done.5.refs_2_, bf16[128,2048]{1,0:T(8,128)(2,1)S(1)} %collective-permute-done.17.refs_3_.refs_0_, ...), custom_call_target="tpu_custom_call" | custom-call | flops 1879048192 | bytes 12976128 | tf_op jit(solution)/shard_map/pallas_call | solution.py:53
  120.6 3.2 %shard_map.72 = bf16[512,896]{1,0:T(8,128)(2,1)S(1)} custom-call(s32[5]{0:T(128)S(1)} %stack.23.place.refs_0_, bf16[128,2048]{1,0:T(8,128)(2,1)S(1)} %collective-permute-done.17.refs_3_.refs_0_, bf16[128,2048]{1,0:T(8,128)(2,1)S(1)} %collective-permute-done.22.refs_7_.refs_1_, bf16[128,2048]{1,0:T(8,128)(2,1)S(1)} %collective-permute-done.20.refs_4_.refs_2_, ...), custom_call_target="tpu_custom_call" | custom-call | flops 1879048192 | bytes 8781824 | tf_op jit(solution)/shard_map/pallas_call | solution.py:53
  125.0 4.4 %shard_map.73 = (bf16[256,896]{1,0:T(8,128)(2,1)S(1)}, bf16[256,896]{1,0:T(8,128)(2,1)S(1)}) custom-call(s32[5]{0:T(128)S(1)} %stack.23.place.refs_0_, bf16[128,2048]{1,0:T(8,128)(2,1)S(1)} %pad_maximum_fusion.1.refs_0_.refs_1_, bf16[128,2048]{1,0:T(8,128)(2,1)S(1)} %collective-permute-done.5.refs_2_, ...), custom_call_target="tpu_custom_call" | custom-call | flops 1879048192 | bytes 12976128 | tf_op jit(solution)/shard_map/pallas_call | solution.py:53
  130.2 3.2 %shard_map.74.mine_a = f32[512,896]{1,0:T(8,128)S(1)} custom-call(s32[5]{0:T(128)S(1)} %stack.23.place.refs_0_, bf16[128,2048]{1,0:T(8,128)(2,1)S(1)} %pad_maximum_fusion.1.refs_0_.refs_1_, bf16[128,2048]{1,0:T(8,128)(2,1)S(1)} %constant_dynamic-update-slice_fusion.refs_1_.refs_5_, bf16[128,2048]{1,0:T(8,128)(2,1)S(1)} %collective-permute-done.5.refs_2_, ...), custom_call_target="tpu_custom_call" | custom-call | flops 1879048192 | bytes 9699328 | tf_op jit(solution)/shard_map/pallas_call | solution.py:53
  133.3 4.4 %shard_map.75 = (bf16[256,896]{1,0:T(8,128)(2,1)S(1)}, bf16[256,896]{1,0:T(8,128)(2,1)S(1)}) custom-call(s32[5]{0:T(128)S(1)} %stack.23.place.refs_0_, bf16[128,2048]{1,0:T(8,128)(2,1)S(1)} %pad_maximum_fusion.1.refs_0_.refs_1_, bf16[128,2048]{1,0:T(8,128)(2,1)S(1)} %collective-permute-done.5.refs_2_, ...), custom_call_target="tpu_custom_call" | custom-call | flops 1879048192 | bytes 12976128 | tf_op jit(solution)/shard_map/pallas_call | solution.py:53
  137.8 3.2 %shard_map.76.mine_b = f32[512,896]{1,0:T(8,128)S(1)} custom-call(s32[5]{0:T(128)S(1)} %stack.23.place.refs_0_, bf16[128,2048]{1,0:T(8,128)(2,1)S(1)} %collective-permute-done.17.refs_3_.refs_0_, bf16[128,2048]{1,0:T(8,128)(2,1)S(1)} %collective-permute-done.22.refs_7_.refs_1_, bf16[128,2048]{1,0:T(8,128)(2,1)S(1)} %collective-permute-done.20.refs_4_.refs_2_, ...), custom_call_target="tpu_custom_call" | custom-call | flops 1879048192 | bytes 9699328 | tf_op jit(solution)/shard_map/pallas_call | solution.py:53
  141.0 4.4 %shard_map.78 = (bf16[256,896]{1,0:T(8,128)(2,1)S(1)}, bf16[256,896]{1,0:T(8,128)(2,1)S(1)}) custom-call(s32[5]{0:T(128)S(1)} %stack.23.place.refs_0_, bf16[128,2048]{1,0:T(8,128)(2,1)S(1)} %pad_maximum_fusion.1.refs_0_.refs_1_, bf16[128,2048]{1,0:T(8,128)(2,1)S(1)} %collective-permute-done.5.refs_2_, ...), custom_call_target="tpu_custom_call" | custom-call | flops 1879048192 | bytes 12976128 | tf_op jit(solution)/shard_map/pallas_call | solution.py:53
  146.6 2.1 %collective-permute-start.42 = (bf16[256,896]{1,0:T(8,128)(2,1)S(1)}, bf16[256,896]{1,0:T(8,128)(2,1)S(1)}, u32[]{:S(2)}, u32[]{:S(2)}) collective-permute-start(bf16[256,896]{1,0:T(8,128)(2,1)S(1)} %add_convert_fusion.2), channel_id=1, source_target_pairs={{0,32},{1,33},{2,34},{3,35},{4,36},{5,37},{6,38},{7,39},{8,104},{9... | collective-permute-start | bytes 1376264 | tf_op jit(solution)/shard_map/ppermute | solution.py:22
  151.2 5.1 %collective-permute-done.42 = bf16[256,896]{1,0:T(8,128)(2,1)S(1)} collective-permute-done((bf16[256,896]{1,0:T(8,128)(2,1)S(1)}, bf16[256,896]{1,0:T(8,128)(2,1)S(1)}, u32[]{:S(2)}, u32[]{:S(2)}) %collective-permute-start.42) | collective-permute-done | bytes 458784 | tf_op jit(solution)/shard_map/ppermute | solution.py:22
  157.7 3.6 %collective-permute-done.39 = bf16[256,896]{1,0:T(8,128)(2,1)S(1)} collective-permute-done((bf16[256,896]{1,0:T(8,128)(2,1)S(1)}, bf16[256,896]{1,0:T(8,128)(2,1)S(1)}, u32[]{:S(2)}, u32[]{:S(2)}) %collective-permute-start.39) | collective-permute-done | bytes 458784 | tf_op jit(solution)/shard_map/ppermute | solution.py:22
  162.5 3.7 %collective-permute-done.43 = bf16[256,896]{1,0:T(8,128)(2,1)S(1)} collective-permute-done((bf16[256,896]{1,0:T(8,128)(2,1)S(1)}, bf16[256,896]{1,0:T(8,128)(2,1)S(1)}, u32[]{:S(2)}, u32[]{:S(2)}) %collective-permute-start.43) | collective-permute-done | bytes 458784 | tf_op jit(solution)/shard_map/ppermute | solution.py:22
  166.4 4.3 %shard_map.77 = (bf16[512,1792]{1,0:T(8,128)(2,1)}, bf16[512,1792]{1,0:T(8,128)(2,1)}) custom-call(s32[5]{0:T(128)S(1)} %stack.23.place.refs_0_, bf16[512,1792]{1,0:T(8,128)(2,1)S(1)} %copy-done.3, bf16[512,1792]{1,0:T(8,128)(2,1)S(1)} %copy-done.5, f32[512,896]{1,0:T(8,128)S(1)} %shard_map.74.mine_a, f32[512,896]{1,0:T(8,128)S(1)} %copy-done.1, ...), custom_call_target="tpu_custom_call" | custom-call | bytes 13762560 | tf_op jit(solution)/shard_map/pallas_call | solution.py:53
  (116 shorter events, 50.9 us)
Async XLA Ops:
  3.6 13.3 %collective-permute-start = (bf16[64,2048]{1,0:T(8,128)(2,1)S(1)}, bf16[64,2048]{1,0:T(8,128)(2,1)S(1)}, u32[]{:S(2)}, u32[]{:S(2)}) collective-permute-start(bf16[64,2048]{1,0:T(8,128)(2,1)S(1)} %get-tuple-element.139), channel_id=1, source_target_pairs={{0,16},{1,17},{2,18},{3,19},{4,20},{5,21},{6,22},{7,23},{8,24},{9,... | collective-permute-start | bytes 786440 | tf_op jit(solution)/shard_map/ppermute | solution.py:22
  9.6 52.2 %collective-permute-start.16 = (bf16[512,896]{1,0:T(8,128)(2,1)S(1)}, bf16[512,896]{1,0:T(8,128)(2,1)S(1)}, u32[]{:S(2)}, u32[]{:S(2)}) collective-permute-start(bf16[512,896]{1,0:T(8,128)(2,1)S(1)} %get-tuple-element.149), channel_id=1, source_target_pairs={{0,8},{1,9},{2,10},{3,11},{4,12},{5,13},{6,14},{7,15},{8,0},{9,1},... | collective-permute-start | bytes 2752520 | tf_op jit(solution)/shard_map/ppermute | solution.py:22
  9.7 16.8 %collective-permute-start.3 = (bf16[64,2048]{1,0:T(8,128)(2,1)S(1)}, bf16[64,2048]{1,0:T(8,128)(2,1)S(1)}, u32[]{:S(2)}, u32[]{:S(2)}) collective-permute-start(bf16[64,2048]{1,0:T(8,128)(2,1)S(1)} %get-tuple-element.138), channel_id=1, source_target_pairs={{0,1},{1,0},{2,3},{3,2},{4,5},{5,4},{6,7},{7,6},{8,9},{9,8},{10,11... | collective-permute-start | bytes 786440 | tf_op jit(solution)/shard_map/ppermute | solution.py:22
  12.5 19.8 %collective-permute-start.4 = (bf16[64,2048]{1,0:T(8,128)(2,1)S(1)}, bf16[64,2048]{1,0:T(8,128)(2,1)S(1)}, u32[]{:S(2)}, u32[]{:S(2)}) collective-permute-start(bf16[64,2048]{1,0:T(8,128)(2,1)S(1)} %get-tuple-element.139), channel_id=1, source_target_pairs={{0,17},{1,16},{2,19},{3,18},{4,21},{5,20},{6,23},{7,22},{8,25},{9,... | collective-permute-start | bytes 786440 | tf_op jit(solution)/shard_map/ppermute | solution.py:22
  26.5 40.2 %collective-permute-start.19 = (bf16[512,896]{1,0:T(8,128)(2,1)S(1)}, bf16[512,896]{1,0:T(8,128)(2,1)S(1)}, u32[]{:S(2)}, u32[]{:S(2)}) collective-permute-start(bf16[512,896]{1,0:T(8,128)(2,1)S(1)} %get-tuple-element.160.refs_17_), channel_id=1, source_target_pairs={{0,16},{1,17},{2,18},{3,19},{4,20},{5,21},{6,22},{7,23},{8,24},{9,... | collective-permute-start | bytes 2752520 | tf_op jit(solution)/shard_map/ppermute | solution.py:22
  27.1 25.2 %collective-permute-start.13 = (bf16[32,1792]{1,0:T(8,128)(2,1)S(1)}, bf16[32,1792]{1,0:T(8,128)(2,1)S(1)}, u32[]{:S(2)}, u32[]{:S(2)}) collective-permute-start(bf16[32,1792]{1,0:T(8,128)(2,1)S(1)} %get-tuple-element.146), channel_id=1, source_target_pairs={{0,7},{1,6},{2,1},{3,0},{4,3},{5,2},{6,5},{7,4},{8,15},{9,14},{10,... | collective-permute-start | bytes 344072 | tf_op jit(solution)/shard_map/ppermute | solution.py:22
  32.3 21.0 %collective-permute-start.14 = (bf16[32,1792]{1,0:T(8,128)(2,1)S(1)}, bf16[32,1792]{1,0:T(8,128)(2,1)S(1)}, u32[]{:S(2)}, u32[]{:S(2)}) collective-permute-start(bf16[32,1792]{1,0:T(8,128)(2,1)S(1)} %get-tuple-element.147), channel_id=1, source_target_pairs={{0,2},{1,3},{2,4},{3,5},{4,6},{5,7},{6,0},{7,1},{8,10},{9,11},{10,... | collective-permute-start | bytes 344072 | tf_op jit(solution)/shard_map/ppermute | solution.py:22
  32.3 30.3 %collective-permute-start.5 = (bf16[128,2048]{1,0:T(8,128)(2,1)S(1)}, bf16[128,2048]{1,0:T(8,128)(2,1)S(1)}, u32[]{:S(2)}, u32[]{:S(2)}) collective-permute-start(bf16[128,2048]{1,0:T(8,128)(2,1)S(1)} %pad_maximum_fusion.1.refs_0_.refs_1_), channel_id=1, source_target_pairs={{0,2},{1,3},{2,4},{3,5},{4,6},{5,7},{6,0},{7,1},{8,14},{9,15},{10,... | collective-permute-start | bytes 1572872 | tf_op jit(solution)/shard_map/ppermute | solution.py:22
  52.3 12.8 %collective-permute-start.6 = (bf16[128,2048]{1,0:T(8,128)(2,1)S(1)}, bf16[128,2048]{1,0:T(8,128)(2,1)S(1)}, u32[]{:S(2)}, u32[]{:S(2)}) collective-permute-start(bf16[128,2048]{1,0:T(8,128)(2,1)S(1)} %constant_dynamic-update-slice_fusion.refs_1_.refs_5_), channel_id=1, source_target_pairs={{0,2},{1,3},{2,4},{3,5},{4,6},{5,7},{6,0},{7,1},{8,14},{9,15},{10,... | collective-permute-start | bytes 1572872 | tf_op jit(solution)/shard_map/ppermute | solution.py:22
  66.8 12.0 %collective-permute-start.22 = (bf16[128,2048]{1,0:T(8,128)(2,1)S(1)}, bf16[128,2048]{1,0:T(8,128)(2,1)S(1)}, u32[]{:S(2)}, u32[]{:S(2)}) collective-permute-start(bf16[128,2048]{1,0:T(8,128)(2,1)S(1)} %collective-permute-done.6.refs_3_.refs_6_), channel_id=1, source_target_pairs={{0,2},{1,3},{2,4},{3,5},{4,6},{5,7},{6,0},{7,1},{8,14},{9,15},{10,... | collective-permute-start | bytes 1572872 | tf_op jit(solution)/shard_map/ppermute | solution.py:22
  72.5 13.5 %collective-permute-start.31 = (bf16[256,896]{1,0:T(8,128)(2,1)S(1)}, bf16[256,896]{1,0:T(8,128)(2,1)S(1)}, u32[]{:S(2)}, u32[]{:S(2)}) collective-permute-start(bf16[256,896]{1,0:T(8,128)(2,1)S(1)} %get-tuple-element.273), channel_id=1, source_target_pairs={{0,16},{1,17},{2,18},{3,19},{4,20},{5,21},{6,22},{7,23},{8,24},{9,... | collective-permute-start | bytes 1376264 | tf_op jit(solution)/shard_map/ppermute | solution.py:22
  73.6 21.2 %collective-permute-start.20 = (bf16[128,2048]{1,0:T(8,128)(2,1)S(1)}, bf16[128,2048]{1,0:T(8,128)(2,1)S(1)}, u32[]{:S(2)}, u32[]{:S(2)}) collective-permute-start(bf16[128,2048]{1,0:T(8,128)(2,1)S(1)} %collective-permute-done.17.refs_3_.refs_0_), channel_id=1, source_target_pairs={{0,2},{1,3},{2,4},{3,5},{4,6},{5,7},{6,0},{7,1},{8,14},{9,15},{10,... | collective-permute-start | bytes 1572872 | tf_op jit(solution)/shard_map/ppermute | solution.py:22
  74.6 19.6 %collective-permute-start.27 = (bf16[256,896]{1,0:T(8,128)(2,1)S(1)}, bf16[256,896]{1,0:T(8,128)(2,1)S(1)}, u32[]{:S(2)}, u32[]{:S(2)}) collective-permute-start(bf16[256,896]{1,0:T(8,128)(2,1)S(1)} %get-tuple-element.274), channel_id=1, source_target_pairs={{0,16},{1,17},{2,18},{3,19},{4,20},{5,21},{6,22},{7,23},{8,24},{9,... | collective-permute-start | bytes 1376264 | tf_op jit(solution)/shard_map/ppermute | solution.py:22
  77.4 16.9 %collective-permute-start.26 = (bf16[256,896]{1,0:T(8,128)(2,1)S(1)}, bf16[256,896]{1,0:T(8,128)(2,1)S(1)}, u32[]{:S(2)}, u32[]{:S(2)}) collective-permute-start(bf16[256,896]{1,0:T(8,128)(2,1)S(1)} %collective-permute-done.18.refs_10_), channel_id=1, source_target_pairs={{0,32},{1,33},{2,34},{3,35},{4,36},{5,37},{6,38},{7,39},{8,104},{9... | collective-permute-start | bytes 1376264 | tf_op jit(solution)/shard_map/ppermute | solution.py:22
  78.7 16.2 %collective-permute-start.30 = (bf16[256,896]{1,0:T(8,128)(2,1)S(1)}, bf16[256,896]{1,0:T(8,128)(2,1)S(1)}, u32[]{:S(2)}, u32[]{:S(2)}) collective-permute-start(bf16[256,896]{1,0:T(8,128)(2,1)S(1)} %collective-permute-done.23.refs_11_), channel_id=1, source_target_pairs={{0,32},{1,33},{2,34},{3,35},{4,36},{5,37},{6,38},{7,39},{8,104},{9... | collective-permute-start | bytes 1376264 | tf_op jit(solution)/shard_map/ppermute | solution.py:22
  96.3 13.2 %collective-permute-start.34 = (bf16[256,896]{1,0:T(8,128)(2,1)S(1)}, bf16[256,896]{1,0:T(8,128)(2,1)S(1)}, u32[]{:S(2)}, u32[]{:S(2)}) collective-permute-start(bf16[256,896]{1,0:T(8,128)(2,1)S(1)} %collective-permute-done.30.refs_13_), channel_id=1, source_target_pairs={{0,32},{1,33},{2,34},{3,35},{4,36},{5,37},{6,38},{7,39},{8,104},{9... | collective-permute-start | bytes 1376264 | tf_op jit(solution)/shard_map/ppermute | solution.py:22
  97.5 16.4 %collective-permute-start.25 = (bf16[128,2048]{1,0:T(8,128)(2,1)S(1)}, bf16[128,2048]{1,0:T(8,128)(2,1)S(1)}, u32[]{:S(2)}, u32[]{:S(2)}) collective-permute-start(bf16[128,2048]{1,0:T(8,128)(2,1)S(1)} %collective-permute-done.17.refs_3_.refs_0_), channel_id=1, source_target_pairs={{0,8},{1,9},{2,10},{3,11},{4,12},{5,13},{6,14},{7,15},{8,0},{9,1},... | collective-permute-start | bytes 1572872 | tf_op jit(solution)/shard_map/ppermute | solution.py:22
  98.1 15.9 %collective-permute-start.29 = (bf16[128,2048]{1,0:T(8,128)(2,1)S(1)}, bf16[128,2048]{1,0:T(8,128)(2,1)S(1)}, u32[]{:S(2)}, u32[]{:S(2)}) collective-permute-start(bf16[128,2048]{1,0:T(8,128)(2,1)S(1)} %collective-permute-done.22.refs_7_.refs_1_), channel_id=1, source_target_pairs={{0,8},{1,9},{2,10},{3,11},{4,12},{5,13},{6,14},{7,15},{8,0},{9,1},... | collective-permute-start | bytes 1572872 | tf_op jit(solution)/shard_map/ppermute | solution.py:22
  98.3 15.6 %collective-permute-start.28 = (bf16[128,2048]{1,0:T(8,128)(2,1)S(1)}, bf16[128,2048]{1,0:T(8,128)(2,1)S(1)}, u32[]{:S(2)}, u32[]{:S(2)}) collective-permute-start(bf16[128,2048]{1,0:T(8,128)(2,1)S(1)} %collective-permute-done.20.refs_4_.refs_2_), channel_id=1, source_target_pairs={{0,8},{1,9},{2,10},{3,11},{4,12},{5,13},{6,14},{7,15},{8,0},{9,1},... | collective-permute-start | bytes 1572872 | tf_op jit(solution)/shard_map/ppermute | solution.py:22
  112.7 38.4 %collective-permute-start.35 = (bf16[512,896]{1,0:T(8,128)(2,1)S(1)}, bf16[512,896]{1,0:T(8,128)(2,1)S(1)}, u32[]{:S(2)}, u32[]{:S(2)}) collective-permute-start(bf16[512,896]{1,0:T(8,128)(2,1)S(1)} %shard_map.70), channel_id=1, source_target_pairs={{0,16},{1,17},{2,18},{3,19},{4,20},{5,21},{6,22},{7,23},{8,24},{9,... | collective-permute-start | bytes 2752520 | tf_op jit(solution)/shard_map/ppermute | solution.py:22
  119.2 26.2 %collective-permute-start.41 = (bf16[256,896]{1,0:T(8,128)(2,1)}, bf16[256,896]{1,0:T(8,128)(2,1)}, u32[]{:S(2)}, u32[]{:S(2)}) collective-permute-start(bf16[256,896]{1,0:T(8,128)(2,1)} %get-tuple-element.191), channel_id=1, source_target_pairs={{0,32},{1,33},{2,34},{3,35},{4,36},{5,37},{6,38},{7,39},{8,104},{9... | collective-permute-start | bytes 1376264 | tf_op jit(solution)/shard_map/ppermute | solution.py:22
  119.2 29.5 %collective-permute-start.38 = (bf16[256,896]{1,0:T(8,128)(2,1)}, bf16[256,896]{1,0:T(8,128)(2,1)}, u32[]{:S(2)}, u32[]{:S(2)}) collective-permute-start(bf16[256,896]{1,0:T(8,128)(2,1)} %get-tuple-element.271), channel_id=1, source_target_pairs={{0,32},{1,33},{2,34},{3,35},{4,36},{5,37},{6,38},{7,39},{8,104},{9... | collective-permute-start | bytes 1376264 | tf_op jit(solution)/shard_map/ppermute | solution.py:22
  123.7 33.6 %collective-permute-start.36 = (bf16[512,896]{1,0:T(8,128)(2,1)S(1)}, bf16[512,896]{1,0:T(8,128)(2,1)S(1)}, u32[]{:S(2)}, u32[]{:S(2)}) collective-permute-start(bf16[512,896]{1,0:T(8,128)(2,1)S(1)} %shard_map.72), channel_id=1, source_target_pairs={{0,16},{1,17},{2,18},{3,19},{4,20},{5,21},{6,22},{7,23},{8,24},{9,... | collective-permute-start | bytes 2752520 | tf_op jit(solution)/shard_map/ppermute | solution.py:22
  149.9 11.4 %collective-permute-start.39 = (bf16[256,896]{1,0:T(8,128)(2,1)S(1)}, bf16[256,896]{1,0:T(8,128)(2,1)S(1)}, u32[]{:S(2)}, u32[]{:S(2)}) collective-permute-start(bf16[256,896]{1,0:T(8,128)(2,1)S(1)} %add_convert_fusion.4), channel_id=1, source_target_pairs={{0,32},{1,33},{2,34},{3,35},{4,36},{5,37},{6,38},{7,39},{8,104},{9... | collective-permute-start | bytes 1376264 | tf_op jit(solution)/shard_map/ppermute | solution.py:22
  (33 other events, 231.6 us)

commit v4 on v0

v4 whole, which is shorter than its diff:
```python
import jax
import jax.numpy as jnp
import numpy as np
from jax import lax
from jax.experimental import pallas as pl
from jax.experimental.pallas import tpu as pltpu
from jax.sharding import PartitionSpec as P

SIZES = (4, 2, 2, 4, 2)
BF16, F32 = jnp.bfloat16, jnp.float32
VMEM = pl.BlockSpec(memory_space=pltpu.VMEM)
SMEM = pl.BlockSpec(memory_space=pltpu.SMEM)
EIGHT = [(k, j) for k in range(4) for j in range(2)]


def permuted(x, step):
    pairs = []
    for source in range(int(np.prod(SIZES))):
        place = [int(p) for p in np.unravel_index(source, SIZES)]
        target = [(p + d) % n for p, d, n in zip(place, step(place[2]), SIZES)]
        pairs.append((source, int(np.ravel_multi_index(target, SIZES))))
    return lax.ppermute(x, ("dp", "tensor"), pairs)


def send(x, y=0, l=0, c=0, z=0, h=0):
    return permuted(x, lambda core: (y, l, c, z, h))


def ring_y(x):
    return permuted(x, lambda core: (1 - 2 * core, 0, 0, 0, 0))


def ring_z(x):
    return permuted(x, lambda core: (0, 0, 0, 1 - 2 * core, 0))


def call(kernel, outs, place, *args, mib=24, specs=None, grid=None, to=None, scratch=(), us=0.0, alias=None):
    specs, to = specs or [VMEM] * len(args), to or [VMEM] * len(outs)
    if grid is None:
        placed = dict(in_specs=[SMEM] + specs, out_specs=to, scratch_shapes=scratch)
    else:
        placed = dict(
            grid_spec=pltpu.PrefetchScalarGridSpec(
                num_scalar_prefetch=1, grid=grid, in_specs=specs, out_specs=to, scratch_shapes=scratch
            )
        )
    return pl.pallas_call(
        kernel,
        out_shape=outs,
        input_output_aliases=alias or {},
        compiler_params=pltpu.CompilerParams(vmem_limit_bytes=mib << 20),
        cost_estimate=pl.CostEstimate(flops=int(us * 1.1e9), bytes_accessed=0, transcendentals=0),
        **placed,
    )(place, *args)


def shape(*dims, dtype=BF16):
    return jax.ShapeDtypeStruct(dims, dtype)


def at(start, size, step=128):
    return pl.ds(pl.multiple_of(start, step), size)


def slot(place, k, j):
    return (place[3] + k) % 4 * 2 + (place[4] + j) % 2


def behind(place, axis, s):
    return (place[axis] + 4 + (2 * place[2] - 1) * s) % 4


def chunk_rows(place, s, rows):
    return at((4 + (2 * place[2] - 1) * s) % 4 * rows, rows, 128)


def pack_kernel(place, grad, weight, own, other, *parts):
    l, c = place[1], place[2]
    stripe = own.shape[1] // 8
    for out, side in ((own, l), (other, 1 - l)):
        for i, core in enumerate((c, 1 - c)):
            for k in range(4):
                to = pl.ds((i * 4 + k) * stripe, stripe)
                out[:, to] = grad[:, at((k * 4 + side * 2 + core) * stripe, stripe)]
    rows, columns = weight.shape[0], parts[0].shape[1]
    for n, (k, j) in enumerate(EIGHT):
        parts[k][j * rows : (j + 1) * rows, :] = weight[:, at(slot(place, k, j) * columns, columns)]


def split_kernel(place, *refs):
    parts, (keep, give) = refs[:4], refs[4:]
    rows, quarter = parts[0].shape[0], keep.shape[1]
    for n, part in enumerate(parts):
        keep[n * rows : (n + 1) * rows, :] = part[:, :quarter]
        give[n * rows : (n + 1) * rows, :] = part[:, quarter:]


def weight_kernel(place, *refs):
    parts, outs = refs[:4], refs[4:]
    rows = parts[0].shape[0] // 2
    for k, part in enumerate(parts):
        to = at((place[3] + k) % 4 * rows, rows, 32)
        for j, out in enumerate(outs):
            out[to, :] = part[j * rows : (j + 1) * rows, :]


def hidden_kernel(place, gate_ref, up_ref, out):
    gate, up = gate_ref[...].astype(F32), up_ref[...].astype(F32)
    out[...] = (gate * jax.nn.sigmoid(gate) * up).astype(BF16)


def product_kernel(l, columns, count, place, *refs):
    chunks, weights, more, outs, (rows_of, all_of) = refs[:4], refs[4:12], refs[12 : -2 - count], refs[-2 - count : -2], refs[-2:]
    rows, cut = chunks[0].shape[0] // 2, weights[0].shape[0] // 4
    for s in range(4):
        rows_of[chunk_rows(place, s, rows), :] = chunks[s][l * rows : (l + 1) * rows, :]
        for j in range(2):
            for z in range(4):
                to = ((behind(place, 0, s) * 4 + z) * 2 + (place[4] + j) % 2) * cut
                all_of[at(to, cut, 32), :] = weights[4 * j + s][z * cut : (z + 1) * cut, columns]
    half = weights[0].shape[1] // 2
    for i in range(all_of.shape[1] // half):
        part = slice(i * half, (i + 1) * half)
        product = jnp.dot(rows_of[...], all_of[:, part], preferred_element_type=F32)
        if more:
            product = product + more[i][...].astype(F32)
        if count == 1:
            outs[0][:, part] = product.astype(outs[0].dtype)
        else:
            outs[i][...] = product.astype(outs[i].dtype)


def term_kernel(s, factor, place, *refs):
    chunks, rights, outs, lhs = refs[:8], refs[8:12], refs[12:14], refs[14]
    rows = chunks[0].shape[0] // 2
    cut, half = outs[0].shape
    block = at(behind(place, 0, s) * cut, cut, 256)
    for n, chunk in enumerate(chunks):
        to = chunk_rows(place, n % 4, rows)
        for l in range(2):
            lhs[2 * l + n // 4, to, :] = chunk[l * rows : (l + 1) * rows, block]
    for i, out in enumerate(outs):
        product = None
        for n, right in enumerate(rights):
            right = right[:, i * half : (i + 1) * half]
            part = lax.dot_general(lhs[n], right, (((0,), (0,)), ((), ())), preferred_element_type=F32)
            product = part if product is None else product + part
        out[...] = (product * factor).astype(BF16)


def chip_kernel(place, *refs):
    half, start = refs[0].shape[1], 0
    for out in refs[4:]:
        rows = slice(start, start + out.shape[0])
        for i in range(2):
            total = refs[i][rows, :] + refs[2 + i][rows, :].astype(F32)
            out[:, i * half : (i + 1) * half] = total.astype(BF16)
        start = rows.stop


def gradient_kernel(first, sizes, place, *refs):
    pieces = len(sizes)
    gate_hbm, up_hbm, mine = refs[:3]
    sums = refs[3 : 3 + pieces]
    outs_hbm, (loaded, stored, load_sem, store_sem) = refs[-6:-4], refs[-4:]
    rows = mine.shape[0] // 8
    at_block = []
    for piece, size in zip(sums, sizes):
        at_block += [(piece, n) for n in range(size)]
    blocks = [at(slot(place, *EIGHT[first + n]) * rows, rows, 64) for n in range(len(at_block))]
    loads, stores = [], []
    for n, block in enumerate(blocks):
        for i, ref in enumerate((gate_hbm, up_hbm)):
            loads.append(pltpu.make_async_copy(ref.at[block, :], loaded.at[n, i], load_sem.at[n, i]))
            loads[-1].start()
    for n, block in enumerate(blocks):
        piece, m = at_block[n]
        grad = mine[(first + n) * rows : (first + n + 1) * rows, :] + piece[m * rows : (m + 1) * rows, :].astype(F32)
        for load in loads[2 * n : 2 * n + 2]:
            load.wait()
        gate, up = loaded[n, 0].astype(F32), loaded[n, 1].astype(F32)
        sig = jax.nn.sigmoid(gate)
        stored[n, 0] = (grad * up * sig * (1.0 + gate * (1.0 - sig))).astype(BF16)
        stored[n, 1] = (grad * gate * sig).astype(BF16)
        for i, ref in enumerate(outs_hbm):
            stores.append(pltpu.make_async_copy(stored.at[n, i], ref.at[block, :], store_sem.at[n, i]))
            stores[-1].start()
    for store in stores:
        store.wait()


def join_kernel(place, *refs):
    half = refs[0].shape[1]
    for i in range(2):
        total = refs[i][...].astype(F32) + refs[2 + i][...].astype(F32)
        refs[4][:, i * half : (i + 1) * half] = total.astype(BF16)


def tied(x, *first):
    return lax.optimization_barrier((x, first))[0]


def added(a, b):
    return (a.astype(F32) + b.astype(F32)).astype(BF16)


def on_device(gate_pre, up_pre, out_grad, down_weight):
    dp, tensor = lax.axis_index("dp"), lax.axis_index("tensor")
    place = jnp.stack([dp // 4, dp // 2 % 2, dp % 2, tensor // 2, tensor % 2]).astype(jnp.int32)
    tokens, columns = gate_pre.shape
    half = columns // 2
    share, width = out_grad.shape
    quarter = width // 4
    cut = quarter // 4
    shard = down_weight.shape[0]

    packed = call(
        pack_kernel, [shape(share, 2 * quarter)] * 2 + [shape(2 * shard, columns)] * 4, place, out_grad, down_weight
    )
    o_own, o_other, parts = packed[0], packed[1], packed[2:]

    parts = [parts[0]] + [send(parts[4 - k], z=4 - k) for k in (1, 2, 3)]
    near, give = call(weight_kernel, [shape(4 * shard, columns)] * 2, place, *parts)
    near, far = [near], [send(give, h=1)]
    o_l, o_h, o_lh = send(o_other, l=1), send(o_own, h=1), send(o_other, l=1, h=1)
    own, give = call(split_kernel, [shape(4 * share, quarter)] * 2, place, o_own, o_h, o_l, o_lh)

    block = pl.BlockSpec((share, columns), lambda n, place: (slot(place, n // 2, n % 2), 0))
    there = pl.BlockSpec((share, columns), lambda n, place: (n, 0))
    (hid_own,) = call(
        hidden_kernel, [shape(tokens, columns)], place, *tied((gate_pre, up_pre), o_own),
        specs=[block] * 2, grid=(8,), to=[there],
    )
    hid_core = send(hid_own, c=1)
    hid_pair = send(tied(hid_own, far[0], o_h, o_l, o_lh), l=1)

    near.append(ring_y(near[0]))
    own, core = [own], [send(give, c=1)]
    own.append(ring_z(own[0]))
    core.append(ring_z(core[0]))
    far.append(ring_y(far[0]))
    near.append(ring_y(near[1]))
    own.append(ring_z(tied(own[1], near[2])))
    core.append(ring_z(tied(core[1], far[1])))
    far.append(ring_y(far[1]))
    near.append(ring_y(near[2]))
    own.append(ring_z(tied(own[2], near[3])))
    core.append(ring_z(tied(core[2], far[2])))
    far.append(ring_y(far[2]))
    weights = near + far
    hid_last = send(tied(hid_pair, hid_core, own[3], core[3], far[3]), c=1)

    def hidden_grad(l, c, side, outs, *after, more=()):
        wide = slice(0, columns) if side is None else slice(side * half, (side + 1) * half)
        size = wide.stop - wide.start

        def kernel(*refs):
            product_kernel(l, wide, len(outs), *refs)

        return call(
            kernel, outs, place, *tied((own, core)[c], *after), *weights, *more,
            us=size / half * 1.6, scratch=[pltpu.VMEM((tokens, quarter), BF16), pltpu.VMEM((quarter, size), BF16)],
        )

    factor = 1.0 / float(np.sqrt(np.float32(tokens * 16)))

    def term(s, *after):
        def kernel(*refs):
            term_kernel(s, factor, *refs)

        return call(
            kernel, [shape(cut, half)] * 2, place, *tied(own + core, *after), hid_own, hid_core, hid_pair, hid_last,
            us=3.1, scratch=[pltpu.VMEM((4, tokens, cut), BF16)],
        )

    out, wide = [shape(tokens, half)], [shape(tokens, half, dtype=F32)]
    out_0 = hidden_grad(1, 1, 0, out)[0]
    pair_0 = hidden_grad(1, 0, 0, wide, out_0)[0]
    out_1 = hidden_grad(1, 1, 1, out, pair_0)[0]
    pair_1 = hidden_grad(1, 0, 1, wide, out_1)[0]
    out_0, out_1 = send(out_0, c=1), send(out_1, c=1)
    sizes = [6, 2]
    pairs = call(chip_kernel, [shape(n * share, columns) for n in sizes], place, pair_0, pair_1, out_0, out_1)
    first = term(1, pairs[0])
    second = term(2, first[0])
    core_out = [send(x, c=1) for x in hidden_grad(0, 1, None, out * 2, second[0])]
    first = [ring_y(x) for x in first]
    second = [ring_y(added(a, b)) for a, b in zip(second, first)]
    third = term(3, first[0])
    (mine,) = hidden_grad(0, 0, None, [shape(tokens, columns, dtype=F32)], third[0], second[0], more=core_out)
    third = [ring_y(added(a, b)) for a, b in zip(third, second)]
    pairs = [send(x, l=1) for x in pairs]
    def gradients(first, pieces, mine, before=()):
        def kernel(*refs):
            gradient_kernel(first, [p.shape[0] // share for p in pieces], *refs)

        count = sum(p.shape[0] for p in pieces) // share
        hbm = pl.BlockSpec(memory_space=pltpu.HBM)
        return call(
            kernel, [shape(tokens, columns)] * 2, place, gate_pre, up_pre, mine, *pieces, *before,
            specs=[hbm] * 2 + [VMEM] * (1 + len(pieces)) + [hbm] * len(before), to=[hbm] * 2,
            alias={4 + len(pieces) + i: i for i in range(len(before))},
            scratch=[pltpu.VMEM((count, 2, share, columns), BF16)] * 2 + [pltpu.SemaphoreType.DMA((count, 2))] * 2,
        )

    gradient = gradients(0, pairs[:1], mine)
    last = term(0, gradient[0])
    (down_grad,) = call(join_kernel, [shape(cut, columns)], place, *last, *third)
    gate_grad, up_grad = gradients(sizes[0], pairs[1:], mine, gradient)
    return (gate_grad, up_grad, down_grad)


def solution(mesh):
    return jax.shard_map(
        on_device,
        mesh=mesh,
        in_specs=(
            P("dp", "tensor"),
            P("dp", "tensor"),
            P(("dp", "tensor"), None),
            P(("dp", "tensor"), None),
        ),
        out_specs=(P("dp", "tensor"), P("dp", "tensor"), P("dp", "tensor")),
        check_vma=False,
    )
```

time: 342 us -> 148 us (0.43)
  waiting for transfers between devices: 267 us -> 54.9 us
  starting transfers between devices: 0.12 us -> 44.1 us
  Pallas kernels: 0 us -> 42.5 us
  matrix products: 29.7 us -> 0 us
  blocking collectives: 28.1 us -> 0 us
  between operations: 13.8 us -> 0.96 us
    reduce_scatter x1 -> x0, waiting for transfers between devices: 149 us -> none  [on_device(): lax.psum_scatter((product * factor).astype(jnp.bfloat16), 'dp', scatter_d...]
    all_gather x2 -> x0, waiting for transfers between devices: 117 us -> none  [the longest x1 67.4 us: on_device(): lax.all_gather(relaid, 'dp', axis=0, tiled=True)]
    ppermute x0 -> x35, waiting for transfers between devices: none -> 54.9 us  [permuted(): return lax.ppermute(x, ('dp', 'tensor'), pairs)]
    ppermute x0 -> x35, starting transfers between devices: none -> 44.1 us  [permuted(): return lax.ppermute(x, ('dp', 'tensor'), pairs)]
    pallas_call x0 -> x18, Pallas kernels: none -> 42.5 us  [call(): pl.pallas_call(kernel, out_shape=outs, input_output_aliases=alias or {},...]
    dot_general x2 -> x0, matrix products: 29.7 us -> none  [the longest x1 15.9 us: on_device(): jnp.dot(columns, lax.all_gather(relaid, 'dp', axis=0, tiled=True), prefer...]
    all_to_all x1 -> x0, blocking collectives: 28.1 us -> none  [on_device(): lax.all_to_all(down_weight, 'tensor', split_axis=1, concat_axis=0, tiled=...]
  transfers between devices with their start and end apart: 3 -> 35, of which waited for: 3 -> 16; matrix products, arithmetic and copies ran while one was open for 9% -> 0% of each run, Pallas kernels for 0% -> 27%
where the time goes in v4:
time: 148 us; the launch traced here: 147 us
  waiting for transfers between devices  54.9 us (37%)
  starting transfers between devices  44.1 us (30%)
  Pallas kernels  42.5 us (29%)
  local copies, waits for them, and re-layouts  3.92 us (3%)
    ppermute x35, waiting for transfers between devices, permuted(): return lax.ppermute(x, ('dp', 'tensor'), pairs)  54.9 us
    ppermute x35, starting transfers between devices, permuted(): return lax.ppermute(x, ('dp', 'tensor'), pairs)  44.1 us
    pallas_call x18, Pallas kernels, call(): pl.pallas_call(kernel, out_shape=outs, input_output_aliases=alias or {},...  42.5 us
    unnamed x10, local copies, waits for them, and re-layouts  3.84 us
  transfers between devices with their start and end apart: 35, of which 16 were waited for; matrix products, arithmetic and copies ran while one was open for 0% of the time, Pallas kernels for 27%

profile of v4, /device:TPU:0, one launch (start us, length us, event | category | flops | bytes accessed | tf_op | source)
XLA Modules:
  0.0 146.8 jit_solution(3400811782089033841)
XLA Ops:
  3.8 4.2 %collective-permute-start.4 = (bf16[64,1792]{1,0:T(8,128)(2,1)S(1)}, bf16[64,1792]{1,0:T(8,128)(2,1)S(1)}, u32[]{:S(2)}, u32[]{:S(2)}) collective-permute-start(bf16[64,1792]{1,0:T(8,128)(2,1)S(1)} %get-tuple-element.97), channel_id=1, source_target_pairs={{0,6},{1,7},{2,0},{3,1},{4,2},{5,3},{6,4},{7,5},{8,14},{9,15},{10,... | collective-permute-start | bytes 688136 | tf_op jit(solution)/shard_map/ppermute | solution.py:22
  12.8 4.9 %collective-permute-done.4.refs_1_ = bf16[64,1792]{1,0:T(8,128)(2,1)S(1)} collective-permute-done((bf16[64,1792]{1,0:T(8,128)(2,1)S(1)}, bf16[64,1792]{1,0:T(8,128)(2,1)S(1)}, u32[]{:S(2)}, u32[]{:S(2)}) %collective-permute-start.4) | collective-permute-done | bytes 229408 | tf_op jit(solution)/shard_map/ppermute | solution.py:22
  17.8 3.0 %collective-permute-start = (bf16[64,2048]{1,0:T(8,128)(2,1)S(1)}, bf16[64,2048]{1,0:T(8,128)(2,1)S(1)}, u32[]{:S(2)}, u32[]{:S(2)}) collective-permute-start(bf16[64,2048]{1,0:T(8,128)(2,1)S(1)} %get-tuple-element.93.refs_0_), channel_id=1, source_target_pairs={{0,1},{1,0},{2,3},{3,2},{4,5},{5,4},{6,7},{7,6},{8,9},{9,8},{10,11... | collective-permute-start | bytes 786440 | tf_op jit(solution)/shard_map/ppermute | solution.py:22
  23.4 3.0 %collective-permute-start.14 = (bf16[128,1792]{1,0:T(8,128)(2,1)S(1)}, bf16[128,1792]{1,0:T(8,128)(2,1)S(1)}, u32[]{:S(2)}, u32[]{:S(2)}) collective-permute-start(bf16[128,1792]{1,0:T(8,128)(2,1)S(1)} %get-tuple-element.104), channel_id=1, source_target_pairs={{0,1},{1,0},{2,3},{3,2},{4,5},{5,4},{6,7},{7,6},{8,9},{9,8},{10,11... | collective-permute-start | bytes 1376264 | tf_op jit(solution)/shard_map/ppermute | solution.py:22
  27.7 3.8 %collective-permute-done.7.refs_6_ = bf16[128,1792]{1,0:T(8,128)(2,1)S(1)} collective-permute-done((bf16[128,1792]{1,0:T(8,128)(2,1)S(1)}, bf16[128,1792]{1,0:T(8,128)(2,1)S(1)}, u32[]{:S(2)}, u32[]{:S(2)}) %collective-permute-start.7) | collective-permute-done | bytes 458784 | tf_op jit(solution)/shard_map/ppermute | solution.py:22
  31.6 7.4 %collective-permute-start.8 = (bf16[128,1792]{1,0:T(8,128)(2,1)S(1)}, bf16[128,1792]{1,0:T(8,128)(2,1)S(1)}, u32[]{:S(2)}, u32[]{:S(2)}) collective-permute-start(bf16[128,1792]{1,0:T(8,128)(2,1)S(1)} %collective-permute-done.7.refs_6_), channel_id=1, source_target_pairs={{0,32},{1,33},{2,34},{3,35},{4,36},{5,37},{6,38},{7,39},{8,104},{9... | collective-permute-start | bytes 1376264 | tf_op jit(solution)/shard_map/ppermute | solution.py:22
  47.4 6.1 %collective-permute-done.15.refs_10_ = bf16[128,1792]{1,0:T(8,128)(2,1)S(1)} collective-permute-done((bf16[128,1792]{1,0:T(8,128)(2,1)S(1)}, bf16[128,1792]{1,0:T(8,128)(2,1)S(1)}, u32[]{:S(2)}, u32[]{:S(2)}) %collective-permute-start.15) | collective-permute-done | bytes 458784 | tf_op jit(solution)/shard_map/ppermute | solution.py:22
  53.5 2.5 %collective-permute-start.9 = (bf16[256,1024]{1,0:T(8,128)(2,1)S(1)}, bf16[256,1024]{1,0:T(8,128)(2,1)S(1)}, u32[]{:S(2)}, u32[]{:S(2)}) collective-permute-start(bf16[256,1024]{1,0:T(8,128)(2,1)S(1)} %collective-permute-done.3.refs_2_), channel_id=1, source_target_pairs={{0,2},{1,3},{2,4},{3,5},{4,6},{5,7},{6,0},{7,1},{8,14},{9,15},{10,... | collective-permute-start | bytes 1572872 | tf_op jit(solution)/shard_map/ppermute | solution.py:22
  56.0 2.4 %collective-permute-done.10.refs_8_ = bf16[128,1792]{1,0:T(8,128)(2,1)S(1)} collective-permute-done((bf16[128,1792]{1,0:T(8,128)(2,1)S(1)}, bf16[128,1792]{1,0:T(8,128)(2,1)S(1)}, u32[]{:S(2)}, u32[]{:S(2)}) %collective-permute-start.10) | collective-permute-done | bytes 458784 | tf_op jit(solution)/shard_map/ppermute | solution.py:22
  59.0 4.9 %collective-permute-done.9.refs_3_ = bf16[256,1024]{1,0:T(8,128)(2,1)S(1)} collective-permute-done((bf16[256,1024]{1,0:T(8,128)(2,1)S(1)}, bf16[256,1024]{1,0:T(8,128)(2,1)S(1)}, u32[]{:S(2)}, u32[]{:S(2)}) %collective-permute-start.9) | collective-permute-done | bytes 524320 | tf_op jit(solution)/shard_map/ppermute | solution.py:22
  65.2 2.9 %collective-permute-done.17.refs_11_ = bf16[128,1792]{1,0:T(8,128)(2,1)S(1)} collective-permute-done((bf16[128,1792]{1,0:T(8,128)(2,1)S(1)}, bf16[128,1792]{1,0:T(8,128)(2,1)S(1)}, u32[]{:S(2)}, u32[]{:S(2)}) %collective-permute-start.17) | collective-permute-done | bytes 458784 | tf_op jit(solution)/shard_map/ppermute | solution.py:22
  71.4 9.1 %collective-permute-done.19.refs_12_ = bf16[128,1792]{1,0:T(8,128)(2,1)S(1)} collective-permute-done((bf16[128,1792]{1,0:T(8,128)(2,1)S(1)}, bf16[128,1792]{1,0:T(8,128)(2,1)S(1)}, u32[]{:S(2)}, u32[]{:S(2)}) %collective-permute-start.19) | collective-permute-done | bytes 458784 | tf_op jit(solution)/shard_map/ppermute | solution.py:22
  80.7 3.8 %collective-permute-done.23.refs_11_ = bf16[512,1792]{1,0:T(8,128)(2,1)S(1)} collective-permute-done((bf16[512,1792]{1,0:T(8,128)(2,1)S(1)}, bf16[512,1792]{1,0:T(8,128)(2,1)S(1)}, u32[]{:S(2)}, u32[]{:S(2)}) %collective-permute-start.23) | collective-permute-done | bytes 1835040 | tf_op jit(solution)/shard_map/ppermute | solution.py:22
  95.7 3.1 %shard_map.76 = (bf16[256,896]{1,0:T(8,128)(2,1)S(1)}, bf16[256,896]{1,0:T(8,128)(2,1)S(1)}) custom-call(s32[5]{0:T(128)S(1)} %stack.23.place.refs_0_, bf16[256,1024]{1,0:T(8,128)(2,1)S(1)} %get-tuple-element.170.refs_1_, bf16[256,1024]{1,0:T(8,128)(2,1)S(1)} %collective-permute-done.3.refs_2_, bf16[256,1024]{1,0:T(8,128)(2,1)S(1)} %collective-permute-done.9.refs_3_, ...), custom_call_target="tpu_custom_call" | custom-call | flops 3409999872 | tf_op jit(solution)/shard_map/pallas_call | solution.py:47
  101.7 3.1 %shard_map.78 = (bf16[256,896]{1,0:T(8,128)(2,1)S(1)}, bf16[256,896]{1,0:T(8,128)(2,1)S(1)}) custom-call(s32[5]{0:T(128)S(1)} %stack.23.place.refs_0_, bf16[256,1024]{1,0:T(8,128)(2,1)S(1)} %get-tuple-element.170.refs_1_, bf16[256,1024]{1,0:T(8,128)(2,1)S(1)} %collective-permute-done.3.refs_2_, bf16[256,1024]{1,0:T(8,128)(2,1)S(1)} %collective-permute-done.9.refs_3_, ...), custom_call_target="tpu_custom_call" | custom-call | flops 3409999872 | tf_op jit(solution)/shard_map/pallas_call | solution.py:47
  104.8 3.2 %shard_map.79 = (bf16[512,896]{1,0:T(8,128)(2,1)S(1)}, bf16[512,896]{1,0:T(8,128)(2,1)S(1)}) custom-call(s32[5]{0:T(128)S(1)} %stack.23.place.refs_0_, bf16[256,1024]{1,0:T(8,128)(2,1)S(1)} %collective-permute-done.12.refs_1_.refs_5_, bf16[256,1024]{1,0:T(8,128)(2,1)S(1)} %collective-permute-done.13.refs_2_.refs_6_, ...), custom_call_target="tpu_custom_call" | custom-call | flops 3520000000 | tf_op jit(solution)/shard_map/pallas_call | solution.py:47
  108.6 4.9 %collective-permute-done.32 = bf16[256,896]{1,0:T(8,128)(2,1)S(1)} collective-permute-done((bf16[256,896]{1,0:T(8,128)(2,1)S(1)}, bf16[256,896]{1,0:T(8,128)(2,1)S(1)}, u32[]{:S(2)}, u32[]{:S(2)}) %collective-permute-start.32) | collective-permute-done | bytes 458784 | tf_op jit(solution)/shard_map/ppermute | solution.py:22
  115.7 3.1 %shard_map.77 = (bf16[256,896]{1,0:T(8,128)(2,1)S(1)}, bf16[256,896]{1,0:T(8,128)(2,1)S(1)}) custom-call(s32[5]{0:T(128)S(1)} %stack.23.place.refs_0_, bf16[256,1024]{1,0:T(8,128)(2,1)S(1)} %get-tuple-element.170.refs_1_, bf16[256,1024]{1,0:T(8,128)(2,1)S(1)} %collective-permute-done.3.refs_2_, bf16[256,1024]{1,0:T(8,128)(2,1)S(1)} %collective-permute-done.9.refs_3_, ...), custom_call_target="tpu_custom_call" | custom-call | flops 3409999872 | tf_op jit(solution)/shard_map/pallas_call | solution.py:47
  118.8 4.5 %collective-permute-done.33 = bf16[256,896]{1,0:T(8,128)(2,1)S(1)} collective-permute-done((bf16[256,896]{1,0:T(8,128)(2,1)S(1)}, bf16[256,896]{1,0:T(8,128)(2,1)S(1)}, u32[]{:S(2)}, u32[]{:S(2)}) %collective-permute-start.33) | collective-permute-done | bytes 458784 | tf_op jit(solution)/shard_map/ppermute | solution.py:22
  125.2 3.0 %collective-permute-done.26 = bf16[256,896]{1,0:T(8,128)(2,1)S(1)} collective-permute-done((bf16[256,896]{1,0:T(8,128)(2,1)S(1)}, bf16[256,896]{1,0:T(8,128)(2,1)S(1)}, u32[]{:S(2)}, u32[]{:S(2)}) %collective-permute-start.26) | collective-permute-done | bytes 458784 | tf_op jit(solution)/shard_map/ppermute | solution.py:22
  128.9 3.2 %shard_map.80.refs_3_ = f32[512,1792]{1,0:T(8,128)S(1)} custom-call(s32[5]{0:T(128)S(1)} %stack.23.place.refs_0_, bf16[256,1024]{1,0:T(8,128)(2,1)S(1)} %get-tuple-element.170.refs_1_, bf16[256,1024]{1,0:T(8,128)(2,1)S(1)} %collective-permute-done.3.refs_2_, bf16[256,1024]{1,0:T(8,128)(2,1)S(1)} %collective-permute-done.9.refs_3_, ...), custom_call_target="tpu_custom_call" | custom-call | flops 3520000000 | tf_op jit(solution)/shard_map/pallas_call | solution.py:47
  132.1 6.7 %shard_map.81 = (bf16[512,1792]{1,0:T(8,128)(2,1)}, bf16[512,1792]{1,0:T(8,128)(2,1)}) custom-call(s32[5]{0:T(128)S(1)} %stack.23.place.refs_0_, bf16[512,1792]{1,0:T(8,128)(2,1)S(1)} %copy-done, bf16[512,1792]{1,0:T(8,128)(2,1)S(1)} %copy-done.2, f32[512,1792]{1,0:T(8,128)S(1)} %shard_map.80.refs_3_, bf16[384,1792]{1,0:T(8,128)(2,1)S(1)} %collective-permute-done.30.refs_4_), custom_call_target="tpu_custom_call" | custom-call | tf_op jit(solution)/shard_map/pallas_call | solution.py:47
  138.9 3.1 %shard_map.82 = (bf16[512,1792]{1,0:T(8,128)(2,1)}, bf16[512,1792]{1,0:T(8,128)(2,1)}) custom-call(s32[5]{0:T(128)S(1)} %stack.23.place.refs_0_, bf16[512,1792]{1,0:T(8,128)(2,1)S(1)} %copy-done, bf16[512,1792]{1,0:T(8,128)(2,1)S(1)} %copy-done.2, f32[512,1792]{1,0:T(8,128)S(1)} %shard_map.80.refs_3_, ...), custom_call_target="tpu_custom_call", output_to_operand_aliasing={{0}: (5, {}), {1}: (6, {})} | custom-call | tf_op jit(solution)/shard_map/pallas_call | solution.py:47
  142.0 3.1 %shard_map.83 = (bf16[256,896]{1,0:T(8,128)(2,1)S(1)}, bf16[256,896]{1,0:T(8,128)(2,1)S(1)}) custom-call(s32[5]{0:T(128)S(1)} %stack.23.place.refs_0_, bf16[256,1024]{1,0:T(8,128)(2,1)S(1)} %get-tuple-element.170.refs_1_, bf16[256,1024]{1,0:T(8,128)(2,1)S(1)} %collective-permute-done.3.refs_2_, bf16[256,1024]{1,0:T(8,128)(2,1)S(1)} %collective-permute-done.9.refs_3_, ...), custom_call_target="tpu_custom_call" | custom-call | flops 3409999872 | tf_op jit(solution)/shard_map/pallas_call | solution.py:47
  (79 shorter events, 46.8 us)
Async XLA Ops:
  3.8 14.0 %collective-permute-start.4 = (bf16[64,1792]{1,0:T(8,128)(2,1)S(1)}, bf16[64,1792]{1,0:T(8,128)(2,1)S(1)}, u32[]{:S(2)}, u32[]{:S(2)}) collective-permute-start(bf16[64,1792]{1,0:T(8,128)(2,1)S(1)} %get-tuple-element.97), channel_id=1, source_target_pairs={{0,6},{1,7},{2,0},{3,1},{4,2},{5,3},{6,4},{7,5},{8,14},{9,15},{10,... | collective-permute-start | bytes 688136 | tf_op jit(solution)/shard_map/ppermute | solution.py:22
  8.0 12.8 %collective-permute-start.5 = (bf16[64,1792]{1,0:T(8,128)(2,1)S(1)}, bf16[64,1792]{1,0:T(8,128)(2,1)S(1)}, u32[]{:S(2)}, u32[]{:S(2)}) collective-permute-start(bf16[64,1792]{1,0:T(8,128)(2,1)S(1)} %get-tuple-element.98), channel_id=1, source_target_pairs={{0,4},{1,5},{2,6},{3,7},{4,0},{5,1},{6,2},{7,3},{8,12},{9,13},{10,... | collective-permute-start | bytes 688136 | tf_op jit(solution)/shard_map/ppermute | solution.py:22
  8.0 13.2 %collective-permute-start.6 = (bf16[64,1792]{1,0:T(8,128)(2,1)S(1)}, bf16[64,1792]{1,0:T(8,128)(2,1)S(1)}, u32[]{:S(2)}, u32[]{:S(2)}) collective-permute-start(bf16[64,1792]{1,0:T(8,128)(2,1)S(1)} %get-tuple-element.99), channel_id=1, source_target_pairs={{0,2},{1,3},{2,4},{3,5},{4,6},{5,7},{6,0},{7,1},{8,10},{9,11},{10,... | collective-permute-start | bytes 688136 | tf_op jit(solution)/shard_map/ppermute | solution.py:22
  9.2 17.2 %collective-permute-start.1 = (bf16[64,2048]{1,0:T(8,128)(2,1)S(1)}, bf16[64,2048]{1,0:T(8,128)(2,1)S(1)}, u32[]{:S(2)}, u32[]{:S(2)}) collective-permute-start(bf16[64,2048]{1,0:T(8,128)(2,1)S(1)} %get-tuple-element.94), channel_id=1, source_target_pairs={{0,16},{1,17},{2,18},{3,19},{4,20},{5,21},{6,22},{7,23},{8,24},{9,... | collective-permute-start | bytes 786440 | tf_op jit(solution)/shard_map/ppermute | solution.py:22
  10.7 15.7 %collective-permute-start.2 = (bf16[64,2048]{1,0:T(8,128)(2,1)S(1)}, bf16[64,2048]{1,0:T(8,128)(2,1)S(1)}, u32[]{:S(2)}, u32[]{:S(2)}) collective-permute-start(bf16[64,2048]{1,0:T(8,128)(2,1)S(1)} %get-tuple-element.94), channel_id=1, source_target_pairs={{0,17},{1,16},{2,19},{3,18},{4,21},{5,20},{6,23},{7,22},{8,25},{9,... | collective-permute-start | bytes 786440 | tf_op jit(solution)/shard_map/ppermute | solution.py:22
  23.4 18.7 %collective-permute-start.14 = (bf16[128,1792]{1,0:T(8,128)(2,1)S(1)}, bf16[128,1792]{1,0:T(8,128)(2,1)S(1)}, u32[]{:S(2)}, u32[]{:S(2)}) collective-permute-start(bf16[128,1792]{1,0:T(8,128)(2,1)S(1)} %get-tuple-element.104), channel_id=1, source_target_pairs={{0,1},{1,0},{2,3},{3,2},{4,5},{5,4},{6,7},{7,6},{8,9},{9,8},{10,11... | collective-permute-start | bytes 1376264 | tf_op jit(solution)/shard_map/ppermute | solution.py:22
  27.1 15.1 %collective-permute-start.12 = (bf16[256,1024]{1,0:T(8,128)(2,1)S(1)}, bf16[256,1024]{1,0:T(8,128)(2,1)S(1)}, u32[]{:S(2)}, u32[]{:S(2)}) collective-permute-start(bf16[256,1024]{1,0:T(8,128)(2,1)S(1)} %get-tuple-element.103), channel_id=1, source_target_pairs={{0,8},{1,9},{2,10},{3,11},{4,12},{5,13},{6,14},{7,15},{8,0},{9,1},... | collective-permute-start | bytes 1572872 | tf_op jit(solution)/shard_map/ppermute | solution.py:22
  27.7 16.0 %collective-permute-start.3 = (bf16[256,1024]{1,0:T(8,128)(2,1)S(1)}, bf16[256,1024]{1,0:T(8,128)(2,1)S(1)}, u32[]{:S(2)}, u32[]{:S(2)}) collective-permute-start(bf16[256,1024]{1,0:T(8,128)(2,1)S(1)} %get-tuple-element.170.refs_1_), channel_id=1, source_target_pairs={{0,2},{1,3},{2,4},{3,5},{4,6},{5,7},{6,0},{7,1},{8,14},{9,15},{10,... | collective-permute-start | bytes 1572872 | tf_op jit(solution)/shard_map/ppermute | solution.py:22
  31.6 15.2 %collective-permute-start.8 = (bf16[128,1792]{1,0:T(8,128)(2,1)S(1)}, bf16[128,1792]{1,0:T(8,128)(2,1)S(1)}, u32[]{:S(2)}, u32[]{:S(2)}) collective-permute-start(bf16[128,1792]{1,0:T(8,128)(2,1)S(1)} %collective-permute-done.7.refs_6_), channel_id=1, source_target_pairs={{0,32},{1,33},{2,34},{3,35},{4,36},{5,37},{6,38},{7,39},{8,104},{9... | collective-permute-start | bytes 1376264 | tf_op jit(solution)/shard_map/ppermute | solution.py:22
  42.0 29.4 %collective-permute-start.22 = (bf16[512,1792]{1,0:T(8,128)(2,1)S(1)}, bf16[512,1792]{1,0:T(8,128)(2,1)S(1)}, u32[]{:S(2)}, u32[]{:S(2)}) collective-permute-start(bf16[512,1792]{1,0:T(8,128)(2,1)S(1)} %shard_map.75.refs_9_), channel_id=1, source_target_pairs={{0,8},{1,9},{2,10},{3,11},{4,12},{5,13},{6,14},{7,15},{8,0},{9,1},... | collective-permute-start | bytes 5505032 | tf_op jit(solution)/shard_map/ppermute | solution.py:22
  42.1 42.4 %collective-permute-start.23 = (bf16[512,1792]{1,0:T(8,128)(2,1)S(1)}, bf16[512,1792]{1,0:T(8,128)(2,1)S(1)}, u32[]{:S(2)}, u32[]{:S(2)}) collective-permute-start(bf16[512,1792]{1,0:T(8,128)(2,1)S(1)} %shard_map.75.refs_9_), channel_id=1, source_target_pairs={{0,16},{1,17},{2,18},{3,19},{4,20},{5,21},{6,22},{7,23},{8,24},{9,... | collective-permute-start | bytes 5505032 | tf_op jit(solution)/shard_map/ppermute | solution.py:22
  42.2 13.8 %collective-permute-start.13 = (bf16[256,1024]{1,0:T(8,128)(2,1)S(1)}, bf16[256,1024]{1,0:T(8,128)(2,1)S(1)}, u32[]{:S(2)}, u32[]{:S(2)}) collective-permute-start(bf16[256,1024]{1,0:T(8,128)(2,1)S(1)} %collective-permute-done.12.refs_1_.refs_5_), channel_id=1, source_target_pairs={{0,2},{1,3},{2,4},{3,5},{4,6},{5,7},{6,0},{7,1},{8,14},{9,15},{10,... | collective-permute-start | bytes 1572872 | tf_op jit(solution)/shard_map/ppermute | solution.py:22
  46.8 11.6 %collective-permute-start.10 = (bf16[128,1792]{1,0:T(8,128)(2,1)S(1)}, bf16[128,1792]{1,0:T(8,128)(2,1)S(1)}, u32[]{:S(2)}, u32[]{:S(2)}) collective-permute-start(bf16[128,1792]{1,0:T(8,128)(2,1)S(1)} %collective-permute-done.8.refs_7_), channel_id=1, source_target_pairs={{0,32},{1,33},{2,34},{3,35},{4,36},{5,37},{6,38},{7,39},{8,104},{9... | collective-permute-start | bytes 1376264 | tf_op jit(solution)/shard_map/ppermute | solution.py:22
  56.0 13.5 %collective-permute-start.16 = (bf16[256,1024]{1,0:T(8,128)(2,1)S(1)}, bf16[256,1024]{1,0:T(8,128)(2,1)S(1)}, u32[]{:S(2)}, u32[]{:S(2)}) collective-permute-start(bf16[256,1024]{1,0:T(8,128)(2,1)S(1)} %collective-permute-done.13.refs_2_.refs_6_), channel_id=1, source_target_pairs={{0,2},{1,3},{2,4},{3,5},{4,6},{5,7},{6,0},{7,1},{8,14},{9,15},{10,... | collective-permute-start | bytes 1572872 | tf_op jit(solution)/shard_map/ppermute | solution.py:22
  63.9 16.6 %collective-permute-start.11 = (bf16[256,1024]{1,0:T(8,128)(2,1)S(1)}, bf16[256,1024]{1,0:T(8,128)(2,1)S(1)}, u32[]{:S(2)}, u32[]{:S(2)}) collective-permute-start(bf16[256,1024]{1,0:T(8,128)(2,1)S(1)} %collective-permute-done.9.refs_3_), channel_id=1, source_target_pairs={{0,2},{1,3},{2,4},{3,5},{4,6},{5,7},{6,0},{7,1},{8,14},{9,15},{10,... | collective-permute-start | bytes 1572872 | tf_op jit(solution)/shard_map/ppermute | solution.py:22
  95.4 36.8 %collective-permute-start.30 = (bf16[384,1792]{1,0:T(8,128)(2,1)S(1)}, bf16[384,1792]{1,0:T(8,128)(2,1)S(1)}, u32[]{:S(2)}, u32[]{:S(2)}) collective-permute-start(bf16[384,1792]{1,0:T(8,128)(2,1)S(1)} %get-tuple-element.123), channel_id=1, source_target_pairs={{0,16},{1,17},{2,18},{3,19},{4,20},{5,21},{6,22},{7,23},{8,24},{9,... | collective-permute-start | bytes 4128776 | tf_op jit(solution)/shard_map/ppermute | solution.py:22
  98.8 15.2 %collective-permute-start.25 = (bf16[256,896]{1,0:T(8,128)(2,1)S(1)}, bf16[256,896]{1,0:T(8,128)(2,1)S(1)}, u32[]{:S(2)}, u32[]{:S(2)}) collective-permute-start(bf16[256,896]{1,0:T(8,128)(2,1)S(1)} %get-tuple-element.136), channel_id=1, source_target_pairs={{0,32},{1,33},{2,34},{3,35},{4,36},{5,37},{6,38},{7,39},{8,104},{9... | collective-permute-start | bytes 1376264 | tf_op jit(solution)/shard_map/ppermute | solution.py:22
  100.5 13.0 %collective-permute-start.32 = (bf16[256,896]{1,0:T(8,128)(2,1)S(1)}, bf16[256,896]{1,0:T(8,128)(2,1)S(1)}, u32[]{:S(2)}, u32[]{:S(2)}) collective-permute-start(bf16[256,896]{1,0:T(8,128)(2,1)S(1)} %get-tuple-element.182), channel_id=1, source_target_pairs={{0,32},{1,33},{2,34},{3,35},{4,36},{5,37},{6,38},{7,39},{8,104},{9... | collective-permute-start | bytes 1376264 | tf_op jit(solution)/shard_map/ppermute | solution.py:22
  108.0 20.4 %collective-permute-start.27 = (bf16[512,896]{1,0:T(8,128)(2,1)S(1)}, bf16[512,896]{1,0:T(8,128)(2,1)S(1)}, u32[]{:S(2)}, u32[]{:S(2)}) collective-permute-start(bf16[512,896]{1,0:T(8,128)(2,1)S(1)} %get-tuple-element.163), channel_id=1, source_target_pairs={{0,8},{1,9},{2,10},{3,11},{4,12},{5,13},{6,14},{7,15},{8,0},{9,1},... | collective-permute-start | bytes 2752520 | tf_op jit(solution)/shard_map/ppermute | solution.py:22
  108.3 20.7 %collective-permute-start.28 = (bf16[512,896]{1,0:T(8,128)(2,1)S(1)}, bf16[512,896]{1,0:T(8,128)(2,1)S(1)}, u32[]{:S(2)}, u32[]{:S(2)}) collective-permute-start(bf16[512,896]{1,0:T(8,128)(2,1)S(1)} %get-tuple-element.164), channel_id=1, source_target_pairs={{0,8},{1,9},{2,10},{3,11},{4,12},{5,13},{6,14},{7,15},{8,0},{9,1},... | collective-permute-start | bytes 2752520 | tf_op jit(solution)/shard_map/ppermute | solution.py:22
  114.2 14.1 %collective-permute-start.26 = (bf16[256,896]{1,0:T(8,128)(2,1)S(1)}, bf16[256,896]{1,0:T(8,128)(2,1)S(1)}, u32[]{:S(2)}, u32[]{:S(2)}) collective-permute-start(bf16[256,896]{1,0:T(8,128)(2,1)S(1)} %add_convert_fusion.3), channel_id=1, source_target_pairs={{0,32},{1,33},{2,34},{3,35},{4,36},{5,37},{6,38},{7,39},{8,104},{9... | collective-permute-start | bytes 1376264 | tf_op jit(solution)/shard_map/ppermute | solution.py:22
  123.4 15.5 %collective-permute-start.29 = (bf16[128,1792]{1,0:T(8,128)(2,1)S(1)}, bf16[128,1792]{1,0:T(8,128)(2,1)S(1)}, u32[]{:S(2)}, u32[]{:S(2)}) collective-permute-start(bf16[128,1792]{1,0:T(8,128)(2,1)S(1)} %get-tuple-element.165), channel_id=1, source_target_pairs={{0,16},{1,17},{2,18},{3,19},{4,20},{5,21},{6,22},{7,23},{8,24},{9,... | collective-permute-start | bytes 1376264 | tf_op jit(solution)/shard_map/ppermute | solution.py:22
  128.3 16.8 %collective-permute-start.34 = (bf16[256,896]{1,0:T(8,128)(2,1)S(1)}, bf16[256,896]{1,0:T(8,128)(2,1)S(1)}, u32[]{:S(2)}, u32[]{:S(2)}) collective-permute-start(bf16[256,896]{1,0:T(8,128)(2,1)S(1)} %add_convert_fusion), channel_id=1, source_target_pairs={{0,32},{1,33},{2,34},{3,35},{4,36},{5,37},{6,38},{7,39},{8,104},{9... | collective-permute-start | bytes 1376264 | tf_op jit(solution)/shard_map/ppermute | solution.py:22
  128.4 16.7 %collective-permute-start.31 = (bf16[256,896]{1,0:T(8,128)(2,1)S(1)}, bf16[256,896]{1,0:T(8,128)(2,1)S(1)}, u32[]{:S(2)}, u32[]{:S(2)}) collective-permute-start(bf16[256,896]{1,0:T(8,128)(2,1)S(1)} %add_convert_fusion.2), channel_id=1, source_target_pairs={{0,32},{1,33},{2,34},{3,35},{4,36},{5,37},{6,38},{7,39},{8,104},{9... | collective-permute-start | bytes 1376264 | tf_op jit(solution)/shard_map/ppermute | solution.py:22
  (16 other events, 142.3 us)

commit v5 on v4

--- a/solution.py
+++ b/solution.py
@@ -83,6 +83,8 @@
                 to = pl.ds((i * 4 + k) * stripe, stripe)
                 out[:, to] = grad[:, at((k * 4 + side * 2 + core) * stripe, stripe)]
     rows, columns = weight.shape[0], parts[0].shape[1]
+    for k in range(4):
+        parts[k][2 * rows :, :] = jnp.zeros_like(parts[k][2 * rows :, :])
     for n, (k, j) in enumerate(EIGHT):
         parts[k][j * rows : (j + 1) * rows, :] = weight[:, at(slot(place, k, j) * columns, columns)]
 
@@ -97,16 +99,19 @@
 
 def weight_kernel(place, *refs):
     parts, outs = refs[:4], refs[4:]
-    rows = parts[0].shape[0] // 2
+    rows = outs[0].shape[0] // 4
     for k, part in enumerate(parts):
         to = at((place[3] + k) % 4 * rows, rows, 32)
         for j, out in enumerate(outs):
             out[to, :] = part[j * rows : (j + 1) * rows, :]
 
 
-def hidden_kernel(place, gate_ref, up_ref, out):
+def hidden_kernel(place, gate_ref, up_ref, out, gate_factor, up_factor):
     gate, up = gate_ref[...].astype(F32), up_ref[...].astype(F32)
-    out[...] = (gate * jax.nn.sigmoid(gate) * up).astype(BF16)
+    sig = jax.nn.sigmoid(gate)
+    out[...] = (gate * sig * up).astype(BF16)
+    gate_factor[...] = (up * sig * (1.0 + gate * (1.0 - sig))).astype(BF16)
+    up_factor[...] = (gate * sig).astype(BF16)
 
 
 def product_kernel(l, columns, count, place, *refs):
@@ -131,20 +136,22 @@
 
 
 def term_kernel(s, factor, place, *refs):
-    chunks, rights, outs, lhs = refs[:8], refs[8:12], refs[12:14], refs[14]
+    chunks, rights, outs, lhs = refs[:8], refs[8:13], refs[13:15], refs[15]
     rows = chunks[0].shape[0] // 2
     cut, half = outs[0].shape
     block = at(behind(place, 0, s) * cut, cut, 256)
     for n, chunk in enumerate(chunks):
         to = chunk_rows(place, n % 4, rows)
         for l in range(2):
-            lhs[2 * l + n // 4, to, :] = chunk[l * rows : (l + 1) * rows, block]
+            lhs.at[pl.ds((2 * l + n // 4) * 4 * rows, 4 * rows), :][to, :] = chunk[l * rows : (l + 1) * rows, block]
     for i, out in enumerate(outs):
-        product = None
-        for n, right in enumerate(rights):
-            right = right[:, i * half : (i + 1) * half]
-            part = lax.dot_general(lhs[n], right, (((0,), (0,)), ((), ())), preferred_element_type=F32)
-            product = part if product is None else product + part
+        product, start = None, 0
+        for right in rights:
+            left = lhs[start : start + right.shape[0], :]
+            part = lax.dot_general(
+                left, right[:, i * half : (i + 1) * half], (((0,), (0,)), ((), ())), preferred_element_type=F32
+            )
+            product, start = part if product is None else product + part, start + right.shape[0]
         out[...] = (product * factor).astype(BF16)
 
 
@@ -158,32 +165,17 @@
         start = rows.stop
 
 
-def gradient_kernel(first, sizes, place, *refs):
-    pieces = len(sizes)
-    gate_hbm, up_hbm, mine = refs[:3]
-    sums = refs[3 : 3 + pieces]
-    outs_hbm, (loaded, stored, load_sem, store_sem) = refs[-6:-4], refs[-4:]
+def gradient_kernel(first, place, gate_factor, up_factor, mine, pair, *refs):
+    outs, (stored, sem) = refs[-4:-2], refs[-2:]
     rows = mine.shape[0] // 8
-    at_block = []
-    for piece, size in zip(sums, sizes):
-        at_block += [(piece, n) for n in range(size)]
-    blocks = [at(slot(place, *EIGHT[first + n]) * rows, rows, 64) for n in range(len(at_block))]
-    loads, stores = [], []
-    for n, block in enumerate(blocks):
-        for i, ref in enumerate((gate_hbm, up_hbm)):
-            loads.append(pltpu.make_async_copy(ref.at[block, :], loaded.at[n, i], load_sem.at[n, i]))
-            loads[-1].start()
-    for n, block in enumerate(blocks):
-        piece, m = at_block[n]
-        grad = mine[(first + n) * rows : (first + n + 1) * rows, :] + piece[m * rows : (m + 1) * rows, :].astype(F32)
-        for load in loads[2 * n : 2 * n + 2]:
-            load.wait()
-        gate, up = loaded[n, 0].astype(F32), loaded[n, 1].astype(F32)
-        sig = jax.nn.sigmoid(gate)
-        stored[n, 0] = (grad * up * sig * (1.0 + gate * (1.0 - sig))).astype(BF16)
-        stored[n, 1] = (grad * gate * sig).astype(BF16)
-        for i, ref in enumerate(outs_hbm):
-            stores.append(pltpu.make_async_copy(stored.at[n, i], ref.at[block, :], store_sem.at[n, i]))
+    stores = []
+    for n in range(pair.shape[0] // rows):
+        here = slice((first + n) * rows, (first + n + 1) * rows)
+        grad = mine[here, :] + pair[n * rows : (n + 1) * rows, :].astype(F32)
+        block = at(slot(place, *EIGHT[first + n]) * rows, rows, 64)
+        for i, (out, factor) in enumerate(zip(outs, (gate_factor, up_factor))):
+            stored[n, i] = (grad * factor[here, :].astype(F32)).astype(BF16)
+            stores.append(pltpu.make_async_copy(stored.at[n, i], out.at[block, :], sem.at[n, i]))
             stores[-1].start()
     for store in stores:
         store.wait()
@@ -215,40 +207,37 @@
     shard = down_weight.shape[0]
 
     packed = call(
-        pack_kernel, [shape(share, 2 * quarter)] * 2 + [shape(2 * shard, columns)] * 4, place, out_grad, down_weight
+        pack_kernel, [shape(share, 2 * quarter)] * 2 + [shape(2 * shard + 16, columns)] * 4, place, out_grad, down_weight
     )
     o_own, o_other, parts = packed[0], packed[1], packed[2:]
 
     parts = [parts[0]] + [send(parts[4 - k], z=4 - k) for k in (1, 2, 3)]
-    near, give = call(weight_kernel, [shape(4 * shard, columns)] * 2, place, *parts)
-    near, far = [near], [send(give, h=1)]
-    o_l, o_h, o_lh = send(o_other, l=1), send(o_own, h=1), send(o_other, l=1, h=1)
-    own, give = call(split_kernel, [shape(4 * share, quarter)] * 2, place, o_own, o_h, o_l, o_lh)
-
     block = pl.BlockSpec((share, columns), lambda n, place: (slot(place, n // 2, n % 2), 0))
     there = pl.BlockSpec((share, columns), lambda n, place: (n, 0))
-    (hid_own,) = call(
-        hidden_kernel, [shape(tokens, columns)], place, *tied((gate_pre, up_pre), o_own),
-        specs=[block] * 2, grid=(8,), to=[there],
+    hid_own, *factors = call(
+        hidden_kernel, [shape(tokens, columns)] * 3, place, *tied((gate_pre, up_pre), o_own),
+        specs=[block] * 2, grid=(8,), to=[there] * 3,
     )
-    hid_core = send(hid_own, c=1)
-    hid_pair = send(tied(hid_own, far[0], o_h, o_l, o_lh), l=1)
-
+    o_l, o_h, o_lh = send(o_other, l=1), send(tied(o_own, hid_own), h=1), send(o_other, l=1, h=1)
+    near, give_h = call(weight_kernel, [shape(4 * shard, columns)] * 2, place, *tied(parts, hid_own))
+    near, far = [near], [send(give_h, h=1)]
+    own, give = call(split_kernel, [shape(4 * share, quarter)] * 2, place, *tied((o_own, o_h, o_l, o_lh), hid_own, near[0]))
     near.append(ring_y(near[0]))
+    hid_pair = send(tied(hid_own, near[1], o_h, o_l, o_lh), l=1)
     own, core = [own], [send(give, c=1)]
     own.append(ring_z(own[0]))
     core.append(ring_z(core[0]))
     far.append(ring_y(far[0]))
     near.append(ring_y(near[1]))
-    own.append(ring_z(tied(own[1], near[2])))
-    core.append(ring_z(tied(core[1], far[1])))
+    own.append(ring_z(own[1]))
+    core.append(ring_z(core[1]))
     far.append(ring_y(far[1]))
     near.append(ring_y(near[2]))
-    own.append(ring_z(tied(own[2], near[3])))
-    core.append(ring_z(tied(core[2], far[2])))
+    own.append(ring_z(own[2]))
+    core.append(ring_z(core[2]))
     far.append(ring_y(far[2]))
     weights = near + far
-    hid_last = send(tied(hid_pair, hid_core, own[3], core[3], far[3]), c=1)
+    hid_core = [send(tied(x, far[3]), c=1) for x in (hid_own[: 2 * share], hid_own[2 * share :])]
 
     def hidden_grad(l, c, side, outs, *after, more=()):
         wide = slice(0, columns) if side is None else slice(side * half, (side + 1) * half)
@@ -269,44 +258,44 @@
             term_kernel(s, factor, *refs)
 
         return call(
-            kernel, [shape(cut, half)] * 2, place, *tied(own + core, *after), hid_own, hid_core, hid_pair, hid_last,
-            us=3.1, scratch=[pltpu.VMEM((4, tokens, cut), BF16)],
+            kernel, [shape(cut, half)] * 2, place, *tied(own + core, *after), hid_own, *hid_core, hid_pair, hid_last,
+            us=3.1, scratch=[pltpu.VMEM((4 * tokens, cut), BF16)],
         )
 
-    out, wide = [shape(tokens, half)], [shape(tokens, half, dtype=F32)]
-    out_0 = hidden_grad(1, 1, 0, out)[0]
-    pair_0 = hidden_grad(1, 0, 0, wide, out_0)[0]
-    out_1 = hidden_grad(1, 1, 1, out, pair_0)[0]
-    pair_1 = hidden_grad(1, 0, 1, wide, out_1)[0]
-    out_0, out_1 = send(out_0, c=1), send(out_1, c=1)
+    out = [shape(tokens, half)] * 2
+    outs = hidden_grad(1, 1, None, out, hid_core[0])
+    mine = hidden_grad(1, 0, None, [shape(tokens, half, dtype=F32)] * 2, outs[0])
+    hid_last = send(tied(hid_pair, own[3], core[3], near[3], hid_core[0]), c=1)
+    outs = [send(x, c=1) for x in outs]
     sizes = [6, 2]
-    pairs = call(chip_kernel, [shape(n * share, columns) for n in sizes], place, pair_0, pair_1, out_0, out_1)
-    first = term(1, pairs[0])
+    pairs = call(chip_kernel, [shape(n * share, columns) for n in sizes], place, *mine, *outs)
+    first = term(1, mine[0])
     second = term(2, first[0])
-    core_out = [send(x, c=1) for x in hidden_grad(0, 1, None, out * 2, second[0])]
+    core_out = [send(x, c=1) for x in hidden_grad(0, 1, None, out, second[0])]
     first = [ring_y(x) for x in first]
     second = [ring_y(added(a, b)) for a, b in zip(second, first)]
     third = term(3, first[0])
+    third_0 = third[0]
     (mine,) = hidden_grad(0, 0, None, [shape(tokens, columns, dtype=F32)], third[0], second[0], more=core_out)
     third = [ring_y(added(a, b)) for a, b in zip(third, second)]
     pairs = [send(x, l=1) for x in pairs]
-    def gradients(first, pieces, mine, before=()):
+    last = term(0, third_0)
+    (down_grad,) = call(join_kernel, [shape(cut, columns)], place, *last, *third)
+
+    def gradients(first, pair, mine, *before):
         def kernel(*refs):
-            gradient_kernel(first, [p.shape[0] // share for p in pieces], *refs)
-
-        count = sum(p.shape[0] for p in pieces) // share
+            gradient_kernel(first, *refs)
+
+        count = pair.shape[0] // share
         hbm = pl.BlockSpec(memory_space=pltpu.HBM)
         return call(
-            kernel, [shape(tokens, columns)] * 2, place, gate_pre, up_pre, mine, *pieces, *before,
-            specs=[hbm] * 2 + [VMEM] * (1 + len(pieces)) + [hbm] * len(before), to=[hbm] * 2,
-            alias={4 + len(pieces) + i: i for i in range(len(before))},
-            scratch=[pltpu.VMEM((count, 2, share, columns), BF16)] * 2 + [pltpu.SemaphoreType.DMA((count, 2))] * 2,
+            kernel, [shape(tokens, columns)] * 2, place, *factors, mine, pair, *before,
+            specs=[VMEM] * 4 + [hbm] * len(before), to=[hbm] * 2, alias={5 + i: i for i in range(len(before))},
+            scratch=[pltpu.VMEM((count, 2, share, columns), BF16), pltpu.SemaphoreType.DMA((count, 2))],
         )
 
-    gradient = gradients(0, pairs[:1], mine)
-    last = term(0, gradient[0])
-    (down_grad,) = call(join_kernel, [shape(cut, columns)], place, *last, *third)
-    gate_grad, up_grad = gradients(sizes[0], pairs[1:], mine, gradient)
+    gradient = gradients(0, pairs[0], mine)
+    gate_grad, up_grad = gradients(sizes[0], pairs[1], tied(mine, down_grad), *gradient)
     return (gate_grad, up_grad, down_grad)
 
 

time: 148 us -> 140 us (0.946)
  starting transfers between devices: 44.1 us -> 30.2 us
  waiting for transfers between devices: 54.9 us -> 65.4 us
  Pallas kernels: 42.5 us -> 36.9 us
  local copies, waits for them, and re-layouts: 3.92 us -> 5.42 us
    ppermute x35 -> x36, starting transfers between devices: 44.1 us -> 30.2 us  [permuted(): return lax.ppermute(x, ('dp', 'tensor'), pairs)]
    ppermute x35 -> x36, waiting for transfers between devices: 54.9 us -> 65.4 us  [permuted(): return lax.ppermute(x, ('dp', 'tensor'), pairs)]
    pallas_call x18 -> x16, Pallas kernels: 42.5 us -> 36.9 us  [call(): pl.pallas_call(kernel, out_shape=outs, input_output_aliases=alias or {},...]
    unnamed x10 -> x8, local copies, waits for them, and re-layouts: 3.84 us -> 5.22 us
  transfers between devices with their start and end apart: 35 -> 36, of which waited for: 16 -> 20; matrix products, arithmetic and copies ran while one was open for 0% -> 0% of each run, Pallas kernels for 27% -> 25%
where the time goes in v5:
time: 140 us; the launch traced here: 139 us
  waiting for transfers between devices  65.4 us (47%)
  Pallas kernels  36.9 us (26%)
  starting transfers between devices  30.2 us (22%)
  local copies, waits for them, and re-layouts  5.42 us (4%)
    ppermute x36, waiting for transfers between devices, permuted(): return lax.ppermute(x, ('dp', 'tensor'), pairs)  65.4 us
    pallas_call x16, Pallas kernels, call(): pl.pallas_call(kernel, out_shape=outs, input_output_aliases=alias or {},...  36.9 us
    ppermute x36, starting transfers between devices, permuted(): return lax.ppermute(x, ('dp', 'tensor'), pairs)  30.2 us
    unnamed x8, local copies, waits for them, and re-layouts  5.22 us
  transfers between devices with their start and end apart: 36, of which 20 were waited for; matrix products, arithmetic and copies ran while one was open for 0% of the time, Pallas kernels for 25%

profile of v5, /device:TPU:0, one launch (start us, length us, event | category | flops | bytes accessed | tf_op | source)
XLA Modules:
  0.0 139.4 jit_solution(11372053883396547552)
XLA Ops:
  3.7 4.2 %collective-permute-start.3 = (bf16[80,1792]{1,0:T(8,128)(2,1)S(1)}, bf16[80,1792]{1,0:T(8,128)(2,1)S(1)}, u32[]{:S(2)}, u32[]{:S(2)}) collective-permute-start(bf16[80,1792]{1,0:T(8,128)(2,1)S(1)} %get-tuple-element.109), channel_id=1, source_target_pairs={{0,6},{1,7},{2,0},{3,1},{4,2},{5,3},{6,4},{7,5},{8,14},{9,15},{10,... | collective-permute-start | bytes 860168 | tf_op jit(solution)/shard_map/ppermute | solution.py:22
  9.1 2.8 %collective-permute-start.2 = (bf16[64,2048]{1,0:T(8,128)(2,1)S(1)}, bf16[64,2048]{1,0:T(8,128)(2,1)S(1)}, u32[]{:S(2)}, u32[]{:S(2)}) collective-permute-start(bf16[64,2048]{1,0:T(8,128)(2,1)S(1)} %get-tuple-element.107), channel_id=1, source_target_pairs={{0,17},{1,16},{2,19},{3,18},{4,21},{5,20},{6,23},{7,22},{8,25},{9,... | collective-permute-start | bytes 786440 | tf_op jit(solution)/shard_map/ppermute | solution.py:22
  15.1 2.8 %shard_map.68 = (bf16[512,1792]{1,0:T(8,128)(2,1)S(1)}, bf16[512,1792]{1,0:T(8,128)(2,1)S(1)}, bf16[512,1792]{1,0:T(8,128)(2,1)S(1)}) custom-call(s32[5]{0:T(128)S(1)} %stack.23.place.refs_0_, bf16[512,1792]{1,0:T(8,128)(2,1)S(1)} %copy-done, bf16[512,1792]{1,0:T(8,128)(2,1)S(1)} %copy-done.1), custom_call_target="tpu_custom_call" | custom-call | tf_op jit(solution)/shard_map/pallas_call | solution.py:47
  20.1 3.0 %collective-permute-start = (bf16[64,2048]{1,0:T(8,128)(2,1)S(1)}, bf16[64,2048]{1,0:T(8,128)(2,1)S(1)}, u32[]{:S(2)}, u32[]{:S(2)}) collective-permute-start(bf16[64,2048]{1,0:T(8,128)(2,1)S(1)} %get-tuple-element.117.refs_0_), channel_id=1, source_target_pairs={{0,1},{1,0},{2,3},{3,2},{4,5},{5,4},{6,7},{7,6},{8,9},{9,8},{10,11... | collective-permute-start | bytes 786440 | tf_op jit(solution)/shard_map/ppermute | solution.py:22
  24.1 3.1 %collective-permute-start.13 = (bf16[128,1792]{1,0:T(8,128)(2,1)S(1)}, bf16[128,1792]{1,0:T(8,128)(2,1)S(1)}, u32[]{:S(2)}, u32[]{:S(2)}) collective-permute-start(bf16[128,1792]{1,0:T(8,128)(2,1)S(1)} %get-tuple-element.123), channel_id=1, source_target_pairs={{0,1},{1,0},{2,3},{3,2},{4,5},{5,4},{6,7},{7,6},{8,9},{9,8},{10,11... | collective-permute-start | bytes 1376264 | tf_op jit(solution)/shard_map/ppermute | solution.py:22
  30.1 8.4 %collective-permute-done.13.refs_9_ = bf16[128,1792]{1,0:T(8,128)(2,1)S(1)} collective-permute-done((bf16[128,1792]{1,0:T(8,128)(2,1)S(1)}, bf16[128,1792]{1,0:T(8,128)(2,1)S(1)}, u32[]{:S(2)}, u32[]{:S(2)}) %collective-permute-start.13) | collective-permute-done | bytes 458784 | tf_op jit(solution)/shard_map/ppermute | solution.py:22
  41.9 6.2 %collective-permute-done.14.refs_10_ = bf16[128,1792]{1,0:T(8,128)(2,1)S(1)} collective-permute-done((bf16[128,1792]{1,0:T(8,128)(2,1)S(1)}, bf16[128,1792]{1,0:T(8,128)(2,1)S(1)}, u32[]{:S(2)}, u32[]{:S(2)}) %collective-permute-start.14) | collective-permute-done | bytes 458784 | tf_op jit(solution)/shard_map/ppermute | solution.py:22
  48.5 4.0 %collective-permute-done.6.refs_2_ = bf16[256,1024]{1,0:T(8,128)(2,1)S(1)} collective-permute-done((bf16[256,1024]{1,0:T(8,128)(2,1)S(1)}, bf16[256,1024]{1,0:T(8,128)(2,1)S(1)}, u32[]{:S(2)}, u32[]{:S(2)}) %collective-permute-start.6) | collective-permute-done | bytes 524320 | tf_op jit(solution)/shard_map/ppermute | solution.py:22
  52.5 5.6 %collective-permute-done.10.refs_2_.refs_6_ = bf16[256,1024]{1,0:T(8,128)(2,1)S(1)} collective-permute-done((bf16[256,1024]{1,0:T(8,128)(2,1)S(1)}, bf16[256,1024]{1,0:T(8,128)(2,1)S(1)}, u32[]{:S(2)}, u32[]{:S(2)}) %collective-permute-start.10) | collective-permute-done | bytes 524320 | tf_op jit(solution)/shard_map/ppermute | solution.py:22
  61.0 2.7 %collective-permute-done.7.refs_3_ = bf16[256,1024]{1,0:T(8,128)(2,1)S(1)} collective-permute-done((bf16[256,1024]{1,0:T(8,128)(2,1)S(1)}, bf16[256,1024]{1,0:T(8,128)(2,1)S(1)}, u32[]{:S(2)}, u32[]{:S(2)}) %collective-permute-start.7) | collective-permute-done | bytes 524320 | tf_op jit(solution)/shard_map/ppermute | solution.py:22
  63.8 5.6 %collective-permute-done.11.refs_3_.refs_7_ = bf16[256,1024]{1,0:T(8,128)(2,1)S(1)} collective-permute-done((bf16[256,1024]{1,0:T(8,128)(2,1)S(1)}, bf16[256,1024]{1,0:T(8,128)(2,1)S(1)}, u32[]{:S(2)}, u32[]{:S(2)}) %collective-permute-start.11) | collective-permute-done | bytes 524320 | tf_op jit(solution)/shard_map/ppermute | solution.py:22
  72.8 6.4 %collective-permute-done.20.refs_8_ = bf16[128,1792]{1,0:T(8,128)(2,1)S(1)} collective-permute-done((bf16[128,1792]{1,0:T(8,128)(2,1)S(1)}, bf16[128,1792]{1,0:T(8,128)(2,1)S(1)}, u32[]{:S(2)}, u32[]{:S(2)}) %collective-permute-start.20) | collective-permute-done | bytes 458784 | tf_op jit(solution)/shard_map/ppermute | solution.py:22
  83.2 3.2 %shard_map.71 = (bf16[512,896]{1,0:T(8,128)(2,1)S(1)}, bf16[512,896]{1,0:T(8,128)(2,1)S(1)}) custom-call(s32[5]{0:T(128)S(1)} %stack.23.place.refs_0_, bf16[256,1024]{1,0:T(8,128)(2,1)S(1)} %collective-permute-done.9.refs_1_.refs_5_, bf16[256,1024]{1,0:T(8,128)(2,1)S(1)} %collective-permute-done.10.refs_2_.refs_6_, ...), custom_call_target="tpu_custom_call" | custom-call | flops 3520000000 | tf_op jit(solution)/shard_map/pallas_call | solution.py:47
  87.0 3.2 %shard_map.72 = (f32[512,896]{1,0:T(8,128)S(1)}, f32[512,896]{1,0:T(8,128)S(1)}) custom-call(s32[5]{0:T(128)S(1)} %stack.23.place.refs_0_, bf16[256,1024]{1,0:T(8,128)(2,1)S(1)} %get-tuple-element.175.refs_1_, bf16[256,1024]{1,0:T(8,128)(2,1)S(1)} %collective-permute-done.6.refs_2_, bf16[256,1024]{1,0:T(8,128)(2,1)S(1)} %collective-permute-done.7.refs_3_, ...), custom_call_target="tpu_custom_call" | custom-call | flops 3520000000 | tf_op jit(solution)/shard_map/pallas_call | solution.py:47
  93.4 3.3 %shard_map.73 = (bf16[256,896]{1,0:T(8,128)(2,1)S(1)}, bf16[256,896]{1,0:T(8,128)(2,1)S(1)}) custom-call(s32[5]{0:T(128)S(1)} %stack.23.place.refs_0_, bf16[256,1024]{1,0:T(8,128)(2,1)S(1)} %get-tuple-element.175.refs_1_, bf16[256,1024]{1,0:T(8,128)(2,1)S(1)} %collective-permute-done.6.refs_2_, bf16[256,1024]{1,0:T(8,128)(2,1)S(1)} %collective-permute-done.7.refs_3_, ...), custom_call_target="tpu_custom_call" | custom-call | flops 3409999872 | tf_op jit(solution)/shard_map/pallas_call | solution.py:47
  97.3 3.3 %shard_map.75 = (bf16[256,896]{1,0:T(8,128)(2,1)S(1)}, bf16[256,896]{1,0:T(8,128)(2,1)S(1)}) custom-call(s32[5]{0:T(128)S(1)} %stack.23.place.refs_0_, bf16[256,1024]{1,0:T(8,128)(2,1)S(1)} %get-tuple-element.175.refs_1_, bf16[256,1024]{1,0:T(8,128)(2,1)S(1)} %collective-permute-done.6.refs_2_, bf16[256,1024]{1,0:T(8,128)(2,1)S(1)} %collective-permute-done.7.refs_3_, ...), custom_call_target="tpu_custom_call" | custom-call | flops 3409999872 | tf_op jit(solution)/shard_map/pallas_call | solution.py:47
  100.6 3.2 %shard_map.76 = (bf16[512,896]{1,0:T(8,128)(2,1)S(1)}, bf16[512,896]{1,0:T(8,128)(2,1)S(1)}) custom-call(s32[5]{0:T(128)S(1)} %stack.23.place.refs_0_, bf16[256,1024]{1,0:T(8,128)(2,1)S(1)} %collective-permute-done.9.refs_1_.refs_5_, bf16[256,1024]{1,0:T(8,128)(2,1)S(1)} %collective-permute-done.10.refs_2_.refs_6_, ...), custom_call_target="tpu_custom_call" | custom-call | flops 3520000000 | tf_op jit(solution)/shard_map/pallas_call | solution.py:47
  106.6 4.7 %collective-permute-done.29 = bf16[256,896]{1,0:T(8,128)(2,1)S(1)} collective-permute-done((bf16[256,896]{1,0:T(8,128)(2,1)S(1)}, bf16[256,896]{1,0:T(8,128)(2,1)S(1)}, u32[]{:S(2)}, u32[]{:S(2)}) %collective-permute-start.29) | collective-permute-done | bytes 458784 | tf_op jit(solution)/shard_map/ppermute | solution.py:22
  111.7 3.3 %shard_map.74 = (bf16[256,896]{1,0:T(8,128)(2,1)S(1)}, bf16[256,896]{1,0:T(8,128)(2,1)S(1)}) custom-call(s32[5]{0:T(128)S(1)} %stack.23.place.refs_0_, bf16[256,1024]{1,0:T(8,128)(2,1)S(1)} %get-tuple-element.175.refs_1_, bf16[256,1024]{1,0:T(8,128)(2,1)S(1)} %collective-permute-done.6.refs_2_, bf16[256,1024]{1,0:T(8,128)(2,1)S(1)} %collective-permute-done.7.refs_3_, ...), custom_call_target="tpu_custom_call" | custom-call | flops 3409999872 | tf_op jit(solution)/shard_map/pallas_call | solution.py:47
  116.9 4.5 %collective-permute-done.30 = bf16[256,896]{1,0:T(8,128)(2,1)S(1)} collective-permute-done((bf16[256,896]{1,0:T(8,128)(2,1)S(1)}, bf16[256,896]{1,0:T(8,128)(2,1)S(1)}, u32[]{:S(2)}, u32[]{:S(2)}) %collective-permute-start.30) | collective-permute-done | bytes 458784 | tf_op jit(solution)/shard_map/ppermute | solution.py:22
  122.2 3.3 %shard_map.78 = (bf16[256,896]{1,0:T(8,128)(2,1)S(1)}, bf16[256,896]{1,0:T(8,128)(2,1)S(1)}) custom-call(s32[5]{0:T(128)S(1)} %stack.23.place.refs_0_, bf16[256,1024]{1,0:T(8,128)(2,1)S(1)} %get-tuple-element.175.refs_1_, bf16[256,1024]{1,0:T(8,128)(2,1)S(1)} %collective-permute-done.6.refs_2_, bf16[256,1024]{1,0:T(8,128)(2,1)S(1)} %collective-permute-done.7.refs_3_, ...), custom_call_target="tpu_custom_call" | custom-call | flops 3409999872 | tf_op jit(solution)/shard_map/pallas_call | solution.py:47
  125.5 3.2 %shard_map.77.refs_3_ = f32[512,1792]{1,0:T(8,128)S(1)} custom-call(s32[5]{0:T(128)S(1)} %stack.23.place.refs_0_, bf16[256,1024]{1,0:T(8,128)(2,1)S(1)} %get-tuple-element.175.refs_1_, bf16[256,1024]{1,0:T(8,128)(2,1)S(1)} %collective-permute-done.6.refs_2_, bf16[256,1024]{1,0:T(8,128)(2,1)S(1)} %collective-permute-done.7.refs_3_, ...), custom_call_target="tpu_custom_call" | custom-call | flops 3520000000 | tf_op jit(solution)/shard_map/pallas_call | solution.py:47
  128.7 2.2 %shard_map.81 = (bf16[512,1792]{1,0:T(8,128)(2,1)}, bf16[512,1792]{1,0:T(8,128)(2,1)}) custom-call(s32[5]{0:T(128)S(1)} %stack.23.place.refs_0_, bf16[512,1792]{1,0:T(8,128)(2,1)S(1)} %get-tuple-element.103.refs_1_, bf16[512,1792]{1,0:T(8,128)(2,1)S(1)} %get-tuple-element.104.refs_2_, f32[512,1792]{1,0:T(8,128)S(1)} %shard_map.77.refs_3_, ...), custom_call_target="tpu_custom_call" | custom-call | tf_op jit(solution)/shard_map/pallas_call | solution.py:47
  131.1 4.9 %collective-permute-done.31.refs_3_ = bf16[256,896]{1,0:T(8,128)(2,1)S(1)} collective-permute-done((bf16[256,896]{1,0:T(8,128)(2,1)S(1)}, bf16[256,896]{1,0:T(8,128)(2,1)S(1)}, u32[]{:S(2)}, u32[]{:S(2)}) %collective-permute-start.31) | collective-permute-done | bytes 458784 | tf_op jit(solution)/shard_map/ppermute | solution.py:22
  (79 shorter events, 41.2 us)
Async XLA Ops:
  3.7 16.4 %collective-permute-start.3 = (bf16[80,1792]{1,0:T(8,128)(2,1)S(1)}, bf16[80,1792]{1,0:T(8,128)(2,1)S(1)}, u32[]{:S(2)}, u32[]{:S(2)}) collective-permute-start(bf16[80,1792]{1,0:T(8,128)(2,1)S(1)} %get-tuple-element.109), channel_id=1, source_target_pairs={{0,6},{1,7},{2,0},{3,1},{4,2},{5,3},{6,4},{7,5},{8,14},{9,15},{10,... | collective-permute-start | bytes 860168 | tf_op jit(solution)/shard_map/ppermute | solution.py:22
  7.9 15.3 %collective-permute-start.4 = (bf16[80,1792]{1,0:T(8,128)(2,1)S(1)}, bf16[80,1792]{1,0:T(8,128)(2,1)S(1)}, u32[]{:S(2)}, u32[]{:S(2)}) collective-permute-start(bf16[80,1792]{1,0:T(8,128)(2,1)S(1)} %get-tuple-element.110), channel_id=1, source_target_pairs={{0,4},{1,5},{2,6},{3,7},{4,0},{5,1},{6,2},{7,3},{8,12},{9,13},{10,... | collective-permute-start | bytes 860168 | tf_op jit(solution)/shard_map/ppermute | solution.py:22
  7.9 15.6 %collective-permute-start.5 = (bf16[80,1792]{1,0:T(8,128)(2,1)S(1)}, bf16[80,1792]{1,0:T(8,128)(2,1)S(1)}, u32[]{:S(2)}, u32[]{:S(2)}) collective-permute-start(bf16[80,1792]{1,0:T(8,128)(2,1)S(1)} %get-tuple-element.111), channel_id=1, source_target_pairs={{0,2},{1,3},{2,4},{3,5},{4,6},{5,7},{6,0},{7,1},{8,10},{9,11},{10,... | collective-permute-start | bytes 860168 | tf_op jit(solution)/shard_map/ppermute | solution.py:22
  9.1 19.7 %collective-permute-start.2 = (bf16[64,2048]{1,0:T(8,128)(2,1)S(1)}, bf16[64,2048]{1,0:T(8,128)(2,1)S(1)}, u32[]{:S(2)}, u32[]{:S(2)}) collective-permute-start(bf16[64,2048]{1,0:T(8,128)(2,1)S(1)} %get-tuple-element.107), channel_id=1, source_target_pairs={{0,17},{1,16},{2,19},{3,18},{4,21},{5,20},{6,23},{7,22},{8,25},{9,... | collective-permute-start | bytes 786440 | tf_op jit(solution)/shard_map/ppermute | solution.py:22
  11.9 16.9 %collective-permute-start.1 = (bf16[64,2048]{1,0:T(8,128)(2,1)S(1)}, bf16[64,2048]{1,0:T(8,128)(2,1)S(1)}, u32[]{:S(2)}, u32[]{:S(2)}) collective-permute-start(bf16[64,2048]{1,0:T(8,128)(2,1)S(1)} %get-tuple-element.107), channel_id=1, source_target_pairs={{0,16},{1,17},{2,18},{3,19},{4,20},{5,21},{6,22},{7,23},{8,24},{9,... | collective-permute-start | bytes 786440 | tf_op jit(solution)/shard_map/ppermute | solution.py:22
  24.1 14.3 %collective-permute-start.13 = (bf16[128,1792]{1,0:T(8,128)(2,1)S(1)}, bf16[128,1792]{1,0:T(8,128)(2,1)S(1)}, u32[]{:S(2)}, u32[]{:S(2)}) collective-permute-start(bf16[128,1792]{1,0:T(8,128)(2,1)S(1)} %get-tuple-element.123), channel_id=1, source_target_pairs={{0,1},{1,0},{2,3},{3,2},{4,5},{5,4},{6,7},{7,6},{8,9},{9,8},{10,11... | collective-permute-start | bytes 1376264 | tf_op jit(solution)/shard_map/ppermute | solution.py:22
  27.2 12.8 %collective-permute-start.18 = (bf16[128,1792]{1,0:T(8,128)(2,1)S(1)}, bf16[128,1792]{1,0:T(8,128)(2,1)S(1)}, u32[]{:S(2)}, u32[]{:S(2)}) collective-permute-start(bf16[128,1792]{1,0:T(8,128)(2,1)S(1)} %get-tuple-element.116.refs_5_), channel_id=1, source_target_pairs={{0,32},{1,33},{2,34},{3,35},{4,36},{5,37},{6,38},{7,39},{8,104},{9... | collective-permute-start | bytes 1376264 | tf_op jit(solution)/shard_map/ppermute | solution.py:22
  29.8 11.8 %collective-permute-start.9 = (bf16[256,1024]{1,0:T(8,128)(2,1)S(1)}, bf16[256,1024]{1,0:T(8,128)(2,1)S(1)}, u32[]{:S(2)}, u32[]{:S(2)}) collective-permute-start(bf16[256,1024]{1,0:T(8,128)(2,1)S(1)} %get-tuple-element.122), channel_id=1, source_target_pairs={{0,8},{1,9},{2,10},{3,11},{4,12},{5,13},{6,14},{7,15},{8,0},{9,1},... | collective-permute-start | bytes 1572872 | tf_op jit(solution)/shard_map/ppermute | solution.py:22
  40.0 42.5 %collective-permute-start.22 = (bf16[512,1792]{1,0:T(8,128)(2,1)S(1)}, bf16[512,1792]{1,0:T(8,128)(2,1)S(1)}, u32[]{:S(2)}, u32[]{:S(2)}) collective-permute-start(bf16[512,1792]{1,0:T(8,128)(2,1)S(1)} %get-tuple-element.144.refs_9_), channel_id=1, source_target_pairs={{0,16},{1,17},{2,18},{3,19},{4,20},{5,21},{6,22},{7,23},{8,24},{9,... | collective-permute-start | bytes 5505032 | tf_op jit(solution)/shard_map/ppermute | solution.py:22
  41.5 11.0 %collective-permute-start.6 = (bf16[256,1024]{1,0:T(8,128)(2,1)S(1)}, bf16[256,1024]{1,0:T(8,128)(2,1)S(1)}, u32[]{:S(2)}, u32[]{:S(2)}) collective-permute-start(bf16[256,1024]{1,0:T(8,128)(2,1)S(1)} %get-tuple-element.175.refs_1_), channel_id=1, source_target_pairs={{0,2},{1,3},{2,4},{3,5},{4,6},{5,7},{6,0},{7,1},{8,14},{9,15},{10,... | collective-permute-start | bytes 1572872 | tf_op jit(solution)/shard_map/ppermute | solution.py:22
  41.6 16.5 %collective-permute-start.10 = (bf16[256,1024]{1,0:T(8,128)(2,1)S(1)}, bf16[256,1024]{1,0:T(8,128)(2,1)S(1)}, u32[]{:S(2)}, u32[]{:S(2)}) collective-permute-start(bf16[256,1024]{1,0:T(8,128)(2,1)S(1)} %collective-permute-done.9.refs_1_.refs_5_), channel_id=1, source_target_pairs={{0,2},{1,3},{2,4},{3,5},{4,6},{5,7},{6,0},{7,1},{8,14},{9,15},{10,... | collective-permute-start | bytes 1572872 | tf_op jit(solution)/shard_map/ppermute | solution.py:22
  48.2 11.6 %collective-permute-start.15 = (bf16[128,1792]{1,0:T(8,128)(2,1)S(1)}, bf16[128,1792]{1,0:T(8,128)(2,1)S(1)}, u32[]{:S(2)}, u32[]{:S(2)}) collective-permute-start(bf16[128,1792]{1,0:T(8,128)(2,1)S(1)} %collective-permute-done.14.refs_10_), channel_id=1, source_target_pairs={{0,32},{1,33},{2,34},{3,35},{4,36},{5,37},{6,38},{7,39},{8,104},{9... | collective-permute-start | bytes 1376264 | tf_op jit(solution)/shard_map/ppermute | solution.py:22
  52.5 11.2 %collective-permute-start.7 = (bf16[256,1024]{1,0:T(8,128)(2,1)S(1)}, bf16[256,1024]{1,0:T(8,128)(2,1)S(1)}, u32[]{:S(2)}, u32[]{:S(2)}) collective-permute-start(bf16[256,1024]{1,0:T(8,128)(2,1)S(1)} %collective-permute-done.6.refs_2_), channel_id=1, source_target_pairs={{0,2},{1,3},{2,4},{3,5},{4,6},{5,7},{6,0},{7,1},{8,14},{9,15},{10,... | collective-permute-start | bytes 1572872 | tf_op jit(solution)/shard_map/ppermute | solution.py:22
  58.2 11.2 %collective-permute-start.11 = (bf16[256,1024]{1,0:T(8,128)(2,1)S(1)}, bf16[256,1024]{1,0:T(8,128)(2,1)S(1)}, u32[]{:S(2)}, u32[]{:S(2)}) collective-permute-start(bf16[256,1024]{1,0:T(8,128)(2,1)S(1)} %collective-permute-done.10.refs_2_.refs_6_), channel_id=1, source_target_pairs={{0,2},{1,3},{2,4},{3,5},{4,6},{5,7},{6,0},{7,1},{8,14},{9,15},{10,... | collective-permute-start | bytes 1572872 | tf_op jit(solution)/shard_map/ppermute | solution.py:22
  58.2 11.3 %collective-permute-start.19 = (bf16[128,1792]{1,0:T(8,128)(2,1)S(1)}, bf16[128,1792]{1,0:T(8,128)(2,1)S(1)}, u32[]{:S(2)}, u32[]{:S(2)}) collective-permute-start(bf16[128,1792]{1,0:T(8,128)(2,1)S(1)} %collective-permute-done.18.refs_6_), channel_id=1, source_target_pairs={{0,32},{1,33},{2,34},{3,35},{4,36},{5,37},{6,38},{7,39},{8,104},{9... | collective-permute-start | bytes 1376264 | tf_op jit(solution)/shard_map/ppermute | solution.py:22
  59.7 13.0 %collective-permute-start.16 = (bf16[128,1792]{1,0:T(8,128)(2,1)S(1)}, bf16[128,1792]{1,0:T(8,128)(2,1)S(1)}, u32[]{:S(2)}, u32[]{:S(2)}) collective-permute-start(bf16[128,1792]{1,0:T(8,128)(2,1)S(1)} %collective-permute-done.15.refs_11_), channel_id=1, source_target_pairs={{0,32},{1,33},{2,34},{3,35},{4,36},{5,37},{6,38},{7,39},{8,104},{9... | collective-permute-start | bytes 1376264 | tf_op jit(solution)/shard_map/ppermute | solution.py:22
  63.8 15.4 %collective-permute-start.8 = (bf16[256,1024]{1,0:T(8,128)(2,1)S(1)}, bf16[256,1024]{1,0:T(8,128)(2,1)S(1)}, u32[]{:S(2)}, u32[]{:S(2)}) collective-permute-start(bf16[256,1024]{1,0:T(8,128)(2,1)S(1)} %collective-permute-done.7.refs_3_), channel_id=1, source_target_pairs={{0,2},{1,3},{2,4},{3,5},{4,6},{5,7},{6,0},{7,1},{8,14},{9,15},{10,... | collective-permute-start | bytes 1572872 | tf_op jit(solution)/shard_map/ppermute | solution.py:22
  69.4 11.2 %collective-permute-start.12 = (bf16[256,1024]{1,0:T(8,128)(2,1)S(1)}, bf16[256,1024]{1,0:T(8,128)(2,1)S(1)}, u32[]{:S(2)}, u32[]{:S(2)}) collective-permute-start(bf16[256,1024]{1,0:T(8,128)(2,1)S(1)} %collective-permute-done.11.refs_3_.refs_7_), channel_id=1, source_target_pairs={{0,2},{1,3},{2,4},{3,5},{4,6},{5,7},{6,0},{7,1},{8,14},{9,15},{10,... | collective-permute-start | bytes 1572872 | tf_op jit(solution)/shard_map/ppermute | solution.py:22
  91.8 36.9 %collective-permute-start.35 = (bf16[384,1792]{1,0:T(8,128)(2,1)S(1)}, bf16[384,1792]{1,0:T(8,128)(2,1)S(1)}, u32[]{:S(2)}, u32[]{:S(2)}) collective-permute-start(bf16[384,1792]{1,0:T(8,128)(2,1)S(1)} %get-tuple-element.192), channel_id=1, source_target_pairs={{0,16},{1,17},{2,18},{3,19},{4,20},{5,21},{6,22},{7,23},{8,24},{9,... | collective-permute-start | bytes 4128776 | tf_op jit(solution)/shard_map/ppermute | solution.py:22
  96.7 14.6 %collective-permute-start.29 = (bf16[256,896]{1,0:T(8,128)(2,1)S(1)}, bf16[256,896]{1,0:T(8,128)(2,1)S(1)}, u32[]{:S(2)}, u32[]{:S(2)}) collective-permute-start(bf16[256,896]{1,0:T(8,128)(2,1)S(1)} %get-tuple-element.187), channel_id=1, source_target_pairs={{0,32},{1,33},{2,34},{3,35},{4,36},{5,37},{6,38},{7,39},{8,104},{9... | collective-permute-start | bytes 1376264 | tf_op jit(solution)/shard_map/ppermute | solution.py:22
  103.8 17.8 %collective-permute-start.26 = (bf16[512,896]{1,0:T(8,128)(2,1)S(1)}, bf16[512,896]{1,0:T(8,128)(2,1)S(1)}, u32[]{:S(2)}, u32[]{:S(2)}) collective-permute-start(bf16[512,896]{1,0:T(8,128)(2,1)S(1)} %get-tuple-element.173), channel_id=1, source_target_pairs={{0,8},{1,9},{2,10},{3,11},{4,12},{5,13},{6,14},{7,15},{8,0},{9,1},... | collective-permute-start | bytes 2752520 | tf_op jit(solution)/shard_map/ppermute | solution.py:22
  103.9 21.6 %collective-permute-start.27 = (bf16[512,896]{1,0:T(8,128)(2,1)S(1)}, bf16[512,896]{1,0:T(8,128)(2,1)S(1)}, u32[]{:S(2)}, u32[]{:S(2)}) collective-permute-start(bf16[512,896]{1,0:T(8,128)(2,1)S(1)} %get-tuple-element.174), channel_id=1, source_target_pairs={{0,8},{1,9},{2,10},{3,11},{4,12},{5,13},{6,14},{7,15},{8,0},{9,1},... | collective-permute-start | bytes 2752520 | tf_op jit(solution)/shard_map/ppermute | solution.py:22
  116.3 21.4 %collective-permute-start.34 = (bf16[128,1792]{1,0:T(8,128)(2,1)S(1)}, bf16[128,1792]{1,0:T(8,128)(2,1)S(1)}, u32[]{:S(2)}, u32[]{:S(2)}) collective-permute-start(bf16[128,1792]{1,0:T(8,128)(2,1)S(1)} %get-tuple-element.191), channel_id=1, source_target_pairs={{0,16},{1,17},{2,18},{3,19},{4,20},{5,21},{6,22},{7,23},{8,24},{9,... | collective-permute-start | bytes 1376264 | tf_op jit(solution)/shard_map/ppermute | solution.py:22
  121.5 14.5 %collective-permute-start.31 = (bf16[256,896]{1,0:T(8,128)(2,1)S(1)}, bf16[256,896]{1,0:T(8,128)(2,1)S(1)}, u32[]{:S(2)}, u32[]{:S(2)}) collective-permute-start(bf16[256,896]{1,0:T(8,128)(2,1)S(1)} %add_convert_fusion), channel_id=1, source_target_pairs={{0,32},{1,33},{2,34},{3,35},{4,36},{5,37},{6,38},{7,39},{8,104},{9... | collective-permute-start | bytes 1376264 | tf_op jit(solution)/shard_map/ppermute | solution.py:22
  (16 other events, 110.5 us)

commit v6 on v5

--- a/solution.py
+++ b/solution.py
@@ -83,8 +83,6 @@
                 to = pl.ds((i * 4 + k) * stripe, stripe)
                 out[:, to] = grad[:, at((k * 4 + side * 2 + core) * stripe, stripe)]
     rows, columns = weight.shape[0], parts[0].shape[1]
-    for k in range(4):
-        parts[k][2 * rows :, :] = jnp.zeros_like(parts[k][2 * rows :, :])
     for n, (k, j) in enumerate(EIGHT):
         parts[k][j * rows : (j + 1) * rows, :] = weight[:, at(slot(place, k, j) * columns, columns)]
 
@@ -207,7 +205,7 @@
     shard = down_weight.shape[0]
 
     packed = call(
-        pack_kernel, [shape(share, 2 * quarter)] * 2 + [shape(2 * shard + 16, columns)] * 4, place, out_grad, down_weight
+        pack_kernel, [shape(share, 2 * quarter)] * 2 + [shape(2 * shard, columns)] * 4, place, out_grad, down_weight
     )
     o_own, o_other, parts = packed[0], packed[1], packed[2:]
 
@@ -218,7 +216,7 @@
         hidden_kernel, [shape(tokens, columns)] * 3, place, *tied((gate_pre, up_pre), o_own),
         specs=[block] * 2, grid=(8,), to=[there] * 3,
     )
-    o_l, o_h, o_lh = send(o_other, l=1), send(tied(o_own, hid_own), h=1), send(o_other, l=1, h=1)
+    o_l, o_h, o_lh = send(tied(o_other, hid_own), l=1), send(o_own, h=1), send(o_other, l=1, h=1)
     near, give_h = call(weight_kernel, [shape(4 * shard, columns)] * 2, place, *tied(parts, hid_own))
     near, far = [near], [send(give_h, h=1)]
     own, give = call(split_kernel, [shape(4 * share, quarter)] * 2, place, *tied((o_own, o_h, o_l, o_lh), hid_own, near[0]))

time: 140 us -> 137 us (0.979)
  waiting for transfers between devices: 65.4 us -> 59.1 us
  starting transfers between devices: 30.2 us -> 33.4 us
    ppermute x36, waiting for transfers between devices: 65.4 us -> 59.1 us  [permuted(): return lax.ppermute(x, ('dp', 'tensor'), pairs)]
    ppermute x36, starting transfers between devices: 30.2 us -> 33.4 us  [permuted(): return lax.ppermute(x, ('dp', 'tensor'), pairs)]
  transfers between devices with their start and end apart: 36 -> 36, of which waited for: 20 -> 18; matrix products, arithmetic and copies ran while one was open for 0% -> 0% of each run, Pallas kernels for 25% -> 25%
where the time goes in v6:
time: 137 us; the launch traced here: 136 us
  waiting for transfers between devices  59.1 us (43%)
  Pallas kernels  36.9 us (27%)
  starting transfers between devices  33.4 us (24%)
  local copies, waits for them, and re-layouts  5.42 us (4%)
    ppermute x36, waiting for transfers between devices, permuted(): return lax.ppermute(x, ('dp', 'tensor'), pairs)  59.1 us
    pallas_call x16, Pallas kernels, call(): pl.pallas_call(kernel, out_shape=outs, input_output_aliases=alias or {},...  36.9 us
    ppermute x36, starting transfers between devices, permuted(): return lax.ppermute(x, ('dp', 'tensor'), pairs)  33.4 us
    unnamed x8, local copies, waits for them, and re-layouts  5.22 us
  transfers between devices with their start and end apart: 36, of which 18 were waited for; matrix products, arithmetic and copies ran while one was open for 0% of the time, Pallas kernels for 25%

profile of v6, /device:TPU:0, one launch (start us, length us, event | category | flops | bytes accessed | tf_op | source)
XLA Modules:
  0.0 136.4 jit_solution(14328190120683024306)
XLA Ops:
  3.7 4.2 %collective-permute-start.3 = (bf16[64,1792]{1,0:T(8,128)(2,1)S(1)}, bf16[64,1792]{1,0:T(8,128)(2,1)S(1)}, u32[]{:S(2)}, u32[]{:S(2)}) collective-permute-start(bf16[64,1792]{1,0:T(8,128)(2,1)S(1)} %get-tuple-element.109), channel_id=1, source_target_pairs={{0,6},{1,7},{2,0},{3,1},{4,2},{5,3},{6,4},{7,5},{8,14},{9,15},{10,... | collective-permute-start | bytes 688136 | tf_op jit(solution)/shard_map/ppermute | solution.py:22
  9.1 2.8 %collective-permute-start.2 = (bf16[64,2048]{1,0:T(8,128)(2,1)S(1)}, bf16[64,2048]{1,0:T(8,128)(2,1)S(1)}, u32[]{:S(2)}, u32[]{:S(2)}) collective-permute-start(bf16[64,2048]{1,0:T(8,128)(2,1)S(1)} %get-tuple-element.107), channel_id=1, source_target_pairs={{0,17},{1,16},{2,19},{3,18},{4,21},{5,20},{6,23},{7,22},{8,25},{9,... | collective-permute-start | bytes 786440 | tf_op jit(solution)/shard_map/ppermute | solution.py:22
  15.7 2.8 %shard_map.68 = (bf16[512,1792]{1,0:T(8,128)(2,1)S(1)}, bf16[512,1792]{1,0:T(8,128)(2,1)S(1)}, bf16[512,1792]{1,0:T(8,128)(2,1)S(1)}) custom-call(s32[5]{0:T(128)S(1)} %stack.23.place.refs_0_, bf16[512,1792]{1,0:T(8,128)(2,1)S(1)} %copy-done, bf16[512,1792]{1,0:T(8,128)(2,1)S(1)} %copy-done.1), custom_call_target="tpu_custom_call" | custom-call | tf_op jit(solution)/shard_map/pallas_call | solution.py:47
  21.7 3.1 %collective-permute-start.13 = (bf16[128,1792]{1,0:T(8,128)(2,1)S(1)}, bf16[128,1792]{1,0:T(8,128)(2,1)S(1)}, u32[]{:S(2)}, u32[]{:S(2)}) collective-permute-start(bf16[128,1792]{1,0:T(8,128)(2,1)S(1)} %get-tuple-element.123), channel_id=1, source_target_pairs={{0,1},{1,0},{2,3},{3,2},{4,5},{5,4},{6,7},{7,6},{8,9},{9,8},{10,11... | collective-permute-start | bytes 1376264 | tf_op jit(solution)/shard_map/ppermute | solution.py:22
  27.6 9.1 %collective-permute-done.13.refs_9_ = bf16[128,1792]{1,0:T(8,128)(2,1)S(1)} collective-permute-done((bf16[128,1792]{1,0:T(8,128)(2,1)S(1)}, bf16[128,1792]{1,0:T(8,128)(2,1)S(1)}, u32[]{:S(2)}, u32[]{:S(2)}) %collective-permute-start.13) | collective-permute-done | bytes 458784 | tf_op jit(solution)/shard_map/ppermute | solution.py:22
  38.8 2.2 %collective-permute-start.6 = (bf16[256,1024]{1,0:T(8,128)(2,1)S(1)}, bf16[256,1024]{1,0:T(8,128)(2,1)S(1)}, u32[]{:S(2)}, u32[]{:S(2)}) collective-permute-start(bf16[256,1024]{1,0:T(8,128)(2,1)S(1)} %get-tuple-element.175.refs_1_), channel_id=1, source_target_pairs={{0,2},{1,3},{2,4},{3,5},{4,6},{5,7},{6,0},{7,1},{8,14},{9,15},{10,... | collective-permute-start | bytes 1572872 | tf_op jit(solution)/shard_map/ppermute | solution.py:22
  41.3 5.1 %collective-permute-done.14.refs_10_ = bf16[128,1792]{1,0:T(8,128)(2,1)S(1)} collective-permute-done((bf16[128,1792]{1,0:T(8,128)(2,1)S(1)}, bf16[128,1792]{1,0:T(8,128)(2,1)S(1)}, u32[]{:S(2)}, u32[]{:S(2)}) %collective-permute-start.14) | collective-permute-done | bytes 458784 | tf_op jit(solution)/shard_map/ppermute | solution.py:22
  46.8 2.7 %collective-permute-done.6.refs_2_ = bf16[256,1024]{1,0:T(8,128)(2,1)S(1)} collective-permute-done((bf16[256,1024]{1,0:T(8,128)(2,1)S(1)}, bf16[256,1024]{1,0:T(8,128)(2,1)S(1)}, u32[]{:S(2)}, u32[]{:S(2)}) %collective-permute-start.6) | collective-permute-done | bytes 524320 | tf_op jit(solution)/shard_map/ppermute | solution.py:22
  50.2 4.9 %collective-permute-done.10.refs_2_.refs_6_ = bf16[256,1024]{1,0:T(8,128)(2,1)S(1)} collective-permute-done((bf16[256,1024]{1,0:T(8,128)(2,1)S(1)}, bf16[256,1024]{1,0:T(8,128)(2,1)S(1)}, u32[]{:S(2)}, u32[]{:S(2)}) %collective-permute-start.10) | collective-permute-done | bytes 524320 | tf_op jit(solution)/shard_map/ppermute | solution.py:22
  61.4 4.9 %collective-permute-done.11.refs_3_.refs_7_ = bf16[256,1024]{1,0:T(8,128)(2,1)S(1)} collective-permute-done((bf16[256,1024]{1,0:T(8,128)(2,1)S(1)}, bf16[256,1024]{1,0:T(8,128)(2,1)S(1)}, u32[]{:S(2)}, u32[]{:S(2)}) %collective-permute-start.11) | collective-permute-done | bytes 524320 | tf_op jit(solution)/shard_map/ppermute | solution.py:22
  70.4 6.4 %collective-permute-done.20.refs_8_ = bf16[128,1792]{1,0:T(8,128)(2,1)S(1)} collective-permute-done((bf16[128,1792]{1,0:T(8,128)(2,1)S(1)}, bf16[128,1792]{1,0:T(8,128)(2,1)S(1)}, u32[]{:S(2)}, u32[]{:S(2)}) %collective-permute-start.20) | collective-permute-done | bytes 458784 | tf_op jit(solution)/shard_map/ppermute | solution.py:22
  77.6 2.6 %collective-permute-done.22.refs_12_ = bf16[512,1792]{1,0:T(8,128)(2,1)S(1)} collective-permute-done((bf16[512,1792]{1,0:T(8,128)(2,1)S(1)}, bf16[512,1792]{1,0:T(8,128)(2,1)S(1)}, u32[]{:S(2)}, u32[]{:S(2)}) %collective-permute-start.22) | collective-permute-done | bytes 1835040 | tf_op jit(solution)/shard_map/ppermute | solution.py:22
  80.9 3.2 %shard_map.71 = (bf16[512,896]{1,0:T(8,128)(2,1)S(1)}, bf16[512,896]{1,0:T(8,128)(2,1)S(1)}) custom-call(s32[5]{0:T(128)S(1)} %stack.23.place.refs_0_, bf16[256,1024]{1,0:T(8,128)(2,1)S(1)} %collective-permute-done.9.refs_1_.refs_5_, bf16[256,1024]{1,0:T(8,128)(2,1)S(1)} %collective-permute-done.10.refs_2_.refs_6_, ...), custom_call_target="tpu_custom_call" | custom-call | flops 3520000000 | tf_op jit(solution)/shard_map/pallas_call | solution.py:47
  84.7 3.2 %shard_map.72 = (f32[512,896]{1,0:T(8,128)S(1)}, f32[512,896]{1,0:T(8,128)S(1)}) custom-call(s32[5]{0:T(128)S(1)} %stack.23.place.refs_0_, bf16[256,1024]{1,0:T(8,128)(2,1)S(1)} %get-tuple-element.175.refs_1_, bf16[256,1024]{1,0:T(8,128)(2,1)S(1)} %collective-permute-done.6.refs_2_, bf16[256,1024]{1,0:T(8,128)(2,1)S(1)} %collective-permute-done.7.refs_3_, ...), custom_call_target="tpu_custom_call" | custom-call | flops 3520000000 | tf_op jit(solution)/shard_map/pallas_call | solution.py:47
  90.3 3.3 %shard_map.73 = (bf16[256,896]{1,0:T(8,128)(2,1)S(1)}, bf16[256,896]{1,0:T(8,128)(2,1)S(1)}) custom-call(s32[5]{0:T(128)S(1)} %stack.23.place.refs_0_, bf16[256,1024]{1,0:T(8,128)(2,1)S(1)} %get-tuple-element.175.refs_1_, bf16[256,1024]{1,0:T(8,128)(2,1)S(1)} %collective-permute-done.6.refs_2_, bf16[256,1024]{1,0:T(8,128)(2,1)S(1)} %collective-permute-done.7.refs_3_, ...), custom_call_target="tpu_custom_call" | custom-call | flops 3409999872 | tf_op jit(solution)/shard_map/pallas_call | solution.py:47
  94.9 3.3 %shard_map.75 = (bf16[256,896]{1,0:T(8,128)(2,1)S(1)}, bf16[256,896]{1,0:T(8,128)(2,1)S(1)}) custom-call(s32[5]{0:T(128)S(1)} %stack.23.place.refs_0_, bf16[256,1024]{1,0:T(8,128)(2,1)S(1)} %get-tuple-element.175.refs_1_, bf16[256,1024]{1,0:T(8,128)(2,1)S(1)} %collective-permute-done.6.refs_2_, bf16[256,1024]{1,0:T(8,128)(2,1)S(1)} %collective-permute-done.7.refs_3_, ...), custom_call_target="tpu_custom_call" | custom-call | flops 3409999872 | tf_op jit(solution)/shard_map/pallas_call | solution.py:47
  98.2 3.2 %shard_map.76 = (bf16[512,896]{1,0:T(8,128)(2,1)S(1)}, bf16[512,896]{1,0:T(8,128)(2,1)S(1)}) custom-call(s32[5]{0:T(128)S(1)} %stack.23.place.refs_0_, bf16[256,1024]{1,0:T(8,128)(2,1)S(1)} %collective-permute-done.9.refs_1_.refs_5_, bf16[256,1024]{1,0:T(8,128)(2,1)S(1)} %collective-permute-done.10.refs_2_.refs_6_, ...), custom_call_target="tpu_custom_call" | custom-call | flops 3520000000 | tf_op jit(solution)/shard_map/pallas_call | solution.py:47
  103.6 4.7 %collective-permute-done.29 = bf16[256,896]{1,0:T(8,128)(2,1)S(1)} collective-permute-done((bf16[256,896]{1,0:T(8,128)(2,1)S(1)}, bf16[256,896]{1,0:T(8,128)(2,1)S(1)}, u32[]{:S(2)}, u32[]{:S(2)}) %collective-permute-start.29) | collective-permute-done | bytes 458784 | tf_op jit(solution)/shard_map/ppermute | solution.py:22
  108.7 3.3 %shard_map.74 = (bf16[256,896]{1,0:T(8,128)(2,1)S(1)}, bf16[256,896]{1,0:T(8,128)(2,1)S(1)}) custom-call(s32[5]{0:T(128)S(1)} %stack.23.place.refs_0_, bf16[256,1024]{1,0:T(8,128)(2,1)S(1)} %get-tuple-element.175.refs_1_, bf16[256,1024]{1,0:T(8,128)(2,1)S(1)} %collective-permute-done.6.refs_2_, bf16[256,1024]{1,0:T(8,128)(2,1)S(1)} %collective-permute-done.7.refs_3_, ...), custom_call_target="tpu_custom_call" | custom-call | flops 3409999872 | tf_op jit(solution)/shard_map/pallas_call | solution.py:47
  114.6 3.8 %collective-permute-done.30 = bf16[256,896]{1,0:T(8,128)(2,1)S(1)} collective-permute-done((bf16[256,896]{1,0:T(8,128)(2,1)S(1)}, bf16[256,896]{1,0:T(8,128)(2,1)S(1)}, u32[]{:S(2)}, u32[]{:S(2)}) %collective-permute-start.30) | collective-permute-done | bytes 458784 | tf_op jit(solution)/shard_map/ppermute | solution.py:22
  119.2 3.3 %shard_map.78 = (bf16[256,896]{1,0:T(8,128)(2,1)S(1)}, bf16[256,896]{1,0:T(8,128)(2,1)S(1)}) custom-call(s32[5]{0:T(128)S(1)} %stack.23.place.refs_0_, bf16[256,1024]{1,0:T(8,128)(2,1)S(1)} %get-tuple-element.175.refs_1_, bf16[256,1024]{1,0:T(8,128)(2,1)S(1)} %collective-permute-done.6.refs_2_, bf16[256,1024]{1,0:T(8,128)(2,1)S(1)} %collective-permute-done.7.refs_3_, ...), custom_call_target="tpu_custom_call" | custom-call | flops 3409999872 | tf_op jit(solution)/shard_map/pallas_call | solution.py:47
  122.5 3.2 %shard_map.77.refs_3_ = f32[512,1792]{1,0:T(8,128)S(1)} custom-call(s32[5]{0:T(128)S(1)} %stack.23.place.refs_0_, bf16[256,1024]{1,0:T(8,128)(2,1)S(1)} %get-tuple-element.175.refs_1_, bf16[256,1024]{1,0:T(8,128)(2,1)S(1)} %collective-permute-done.6.refs_2_, bf16[256,1024]{1,0:T(8,128)(2,1)S(1)} %collective-permute-done.7.refs_3_, ...), custom_call_target="tpu_custom_call" | custom-call | flops 3520000000 | tf_op jit(solution)/shard_map/pallas_call | solution.py:47
  125.7 2.2 %shard_map.81 = (bf16[512,1792]{1,0:T(8,128)(2,1)}, bf16[512,1792]{1,0:T(8,128)(2,1)}) custom-call(s32[5]{0:T(128)S(1)} %stack.23.place.refs_0_, bf16[512,1792]{1,0:T(8,128)(2,1)S(1)} %get-tuple-element.103.refs_1_, bf16[512,1792]{1,0:T(8,128)(2,1)S(1)} %get-tuple-element.104.refs_2_, f32[512,1792]{1,0:T(8,128)S(1)} %shard_map.77.refs_3_, ...), custom_call_target="tpu_custom_call" | custom-call | tf_op jit(solution)/shard_map/pallas_call | solution.py:47
  128.1 4.9 %collective-permute-done.31.refs_3_ = bf16[256,896]{1,0:T(8,128)(2,1)S(1)} collective-permute-done((bf16[256,896]{1,0:T(8,128)(2,1)S(1)}, bf16[256,896]{1,0:T(8,128)(2,1)S(1)}, u32[]{:S(2)}, u32[]{:S(2)}) %collective-permute-start.31) | collective-permute-done | bytes 458784 | tf_op jit(solution)/shard_map/ppermute | solution.py:22
  (79 shorter events, 42.9 us)
Async XLA Ops:
  3.7 14.8 %collective-permute-start.3 = (bf16[64,1792]{1,0:T(8,128)(2,1)S(1)}, bf16[64,1792]{1,0:T(8,128)(2,1)S(1)}, u32[]{:S(2)}, u32[]{:S(2)}) collective-permute-start(bf16[64,1792]{1,0:T(8,128)(2,1)S(1)} %get-tuple-element.109), channel_id=1, source_target_pairs={{0,6},{1,7},{2,0},{3,1},{4,2},{5,3},{6,4},{7,5},{8,14},{9,15},{10,... | collective-permute-start | bytes 688136 | tf_op jit(solution)/shard_map/ppermute | solution.py:22
  7.9 11.3 %collective-permute-start.4 = (bf16[64,1792]{1,0:T(8,128)(2,1)S(1)}, bf16[64,1792]{1,0:T(8,128)(2,1)S(1)}, u32[]{:S(2)}, u32[]{:S(2)}) collective-permute-start(bf16[64,1792]{1,0:T(8,128)(2,1)S(1)} %get-tuple-element.110), channel_id=1, source_target_pairs={{0,4},{1,5},{2,6},{3,7},{4,0},{5,1},{6,2},{7,3},{8,12},{9,13},{10,... | collective-permute-start | bytes 688136 | tf_op jit(solution)/shard_map/ppermute | solution.py:22
  7.9 13.2 %collective-permute-start.5 = (bf16[64,1792]{1,0:T(8,128)(2,1)S(1)}, bf16[64,1792]{1,0:T(8,128)(2,1)S(1)}, u32[]{:S(2)}, u32[]{:S(2)}) collective-permute-start(bf16[64,1792]{1,0:T(8,128)(2,1)S(1)} %get-tuple-element.111), channel_id=1, source_target_pairs={{0,2},{1,3},{2,4},{3,5},{4,6},{5,7},{6,0},{7,1},{8,10},{9,11},{10,... | collective-permute-start | bytes 688136 | tf_op jit(solution)/shard_map/ppermute | solution.py:22
  9.1 17.2 %collective-permute-start.2 = (bf16[64,2048]{1,0:T(8,128)(2,1)S(1)}, bf16[64,2048]{1,0:T(8,128)(2,1)S(1)}, u32[]{:S(2)}, u32[]{:S(2)}) collective-permute-start(bf16[64,2048]{1,0:T(8,128)(2,1)S(1)} %get-tuple-element.107), channel_id=1, source_target_pairs={{0,17},{1,16},{2,19},{3,18},{4,21},{5,20},{6,23},{7,22},{8,25},{9,... | collective-permute-start | bytes 786440 | tf_op jit(solution)/shard_map/ppermute | solution.py:22
  11.9 14.5 %collective-permute-start = (bf16[64,2048]{1,0:T(8,128)(2,1)S(1)}, bf16[64,2048]{1,0:T(8,128)(2,1)S(1)}, u32[]{:S(2)}, u32[]{:S(2)}) collective-permute-start(bf16[64,2048]{1,0:T(8,128)(2,1)S(1)} %get-tuple-element.117.refs_0_), channel_id=1, source_target_pairs={{0,1},{1,0},{2,3},{3,2},{4,5},{5,4},{6,7},{7,6},{8,9},{9,8},{10,11... | collective-permute-start | bytes 786440 | tf_op jit(solution)/shard_map/ppermute | solution.py:22
  21.7 15.0 %collective-permute-start.13 = (bf16[128,1792]{1,0:T(8,128)(2,1)S(1)}, bf16[128,1792]{1,0:T(8,128)(2,1)S(1)}, u32[]{:S(2)}, u32[]{:S(2)}) collective-permute-start(bf16[128,1792]{1,0:T(8,128)(2,1)S(1)} %get-tuple-element.123), channel_id=1, source_target_pairs={{0,1},{1,0},{2,3},{3,2},{4,5},{5,4},{6,7},{7,6},{8,9},{9,8},{10,11... | collective-permute-start | bytes 1376264 | tf_op jit(solution)/shard_map/ppermute | solution.py:22
  24.8 13.5 %collective-permute-start.18 = (bf16[128,1792]{1,0:T(8,128)(2,1)S(1)}, bf16[128,1792]{1,0:T(8,128)(2,1)S(1)}, u32[]{:S(2)}, u32[]{:S(2)}) collective-permute-start(bf16[128,1792]{1,0:T(8,128)(2,1)S(1)} %get-tuple-element.116.refs_5_), channel_id=1, source_target_pairs={{0,32},{1,33},{2,34},{3,35},{4,36},{5,37},{6,38},{7,39},{8,104},{9... | collective-permute-start | bytes 1376264 | tf_op jit(solution)/shard_map/ppermute | solution.py:22
  27.0 14.0 %collective-permute-start.9 = (bf16[256,1024]{1,0:T(8,128)(2,1)S(1)}, bf16[256,1024]{1,0:T(8,128)(2,1)S(1)}, u32[]{:S(2)}, u32[]{:S(2)}) collective-permute-start(bf16[256,1024]{1,0:T(8,128)(2,1)S(1)} %get-tuple-element.122), channel_id=1, source_target_pairs={{0,8},{1,9},{2,10},{3,11},{4,12},{5,13},{6,14},{7,15},{8,0},{9,1},... | collective-permute-start | bytes 1572872 | tf_op jit(solution)/shard_map/ppermute | solution.py:22
  38.3 41.9 %collective-permute-start.22 = (bf16[512,1792]{1,0:T(8,128)(2,1)S(1)}, bf16[512,1792]{1,0:T(8,128)(2,1)S(1)}, u32[]{:S(2)}, u32[]{:S(2)}) collective-permute-start(bf16[512,1792]{1,0:T(8,128)(2,1)S(1)} %get-tuple-element.144.refs_9_), channel_id=1, source_target_pairs={{0,16},{1,17},{2,18},{3,19},{4,20},{5,21},{6,22},{7,23},{8,24},{9,... | collective-permute-start | bytes 5505032 | tf_op jit(solution)/shard_map/ppermute | solution.py:22
  38.8 10.7 %collective-permute-start.6 = (bf16[256,1024]{1,0:T(8,128)(2,1)S(1)}, bf16[256,1024]{1,0:T(8,128)(2,1)S(1)}, u32[]{:S(2)}, u32[]{:S(2)}) collective-permute-start(bf16[256,1024]{1,0:T(8,128)(2,1)S(1)} %get-tuple-element.175.refs_1_), channel_id=1, source_target_pairs={{0,2},{1,3},{2,4},{3,5},{4,6},{5,7},{6,0},{7,1},{8,14},{9,15},{10,... | collective-permute-start | bytes 1572872 | tf_op jit(solution)/shard_map/ppermute | solution.py:22
  41.0 14.1 %collective-permute-start.10 = (bf16[256,1024]{1,0:T(8,128)(2,1)S(1)}, bf16[256,1024]{1,0:T(8,128)(2,1)S(1)}, u32[]{:S(2)}, u32[]{:S(2)}) collective-permute-start(bf16[256,1024]{1,0:T(8,128)(2,1)S(1)} %collective-permute-done.9.refs_1_.refs_5_), channel_id=1, source_target_pairs={{0,2},{1,3},{2,4},{3,5},{4,6},{5,7},{6,0},{7,1},{8,14},{9,15},{10,... | collective-permute-start | bytes 1572872 | tf_op jit(solution)/shard_map/ppermute | solution.py:22
  46.4 11.0 %collective-permute-start.15 = (bf16[128,1792]{1,0:T(8,128)(2,1)S(1)}, bf16[128,1792]{1,0:T(8,128)(2,1)S(1)}, u32[]{:S(2)}, u32[]{:S(2)}) collective-permute-start(bf16[128,1792]{1,0:T(8,128)(2,1)S(1)} %collective-permute-done.14.refs_10_), channel_id=1, source_target_pairs={{0,32},{1,33},{2,34},{3,35},{4,36},{5,37},{6,38},{7,39},{8,104},{9... | collective-permute-start | bytes 1376264 | tf_op jit(solution)/shard_map/ppermute | solution.py:22
  49.5 11.2 %collective-permute-start.7 = (bf16[256,1024]{1,0:T(8,128)(2,1)S(1)}, bf16[256,1024]{1,0:T(8,128)(2,1)S(1)}, u32[]{:S(2)}, u32[]{:S(2)}) collective-permute-start(bf16[256,1024]{1,0:T(8,128)(2,1)S(1)} %collective-permute-done.6.refs_2_), channel_id=1, source_target_pairs={{0,2},{1,3},{2,4},{3,5},{4,6},{5,7},{6,0},{7,1},{8,14},{9,15},{10,... | collective-permute-start | bytes 1572872 | tf_op jit(solution)/shard_map/ppermute | solution.py:22
  55.1 11.2 %collective-permute-start.11 = (bf16[256,1024]{1,0:T(8,128)(2,1)S(1)}, bf16[256,1024]{1,0:T(8,128)(2,1)S(1)}, u32[]{:S(2)}, u32[]{:S(2)}) collective-permute-start(bf16[256,1024]{1,0:T(8,128)(2,1)S(1)} %collective-permute-done.10.refs_2_.refs_6_), channel_id=1, source_target_pairs={{0,2},{1,3},{2,4},{3,5},{4,6},{5,7},{6,0},{7,1},{8,14},{9,15},{10,... | collective-permute-start | bytes 1572872 | tf_op jit(solution)/shard_map/ppermute | solution.py:22
  55.8 11.3 %collective-permute-start.19 = (bf16[128,1792]{1,0:T(8,128)(2,1)S(1)}, bf16[128,1792]{1,0:T(8,128)(2,1)S(1)}, u32[]{:S(2)}, u32[]{:S(2)}) collective-permute-start(bf16[128,1792]{1,0:T(8,128)(2,1)S(1)} %collective-permute-done.18.refs_6_), channel_id=1, source_target_pairs={{0,32},{1,33},{2,34},{3,35},{4,36},{5,37},{6,38},{7,39},{8,104},{9... | collective-permute-start | bytes 1376264 | tf_op jit(solution)/shard_map/ppermute | solution.py:22
  57.4 13.0 %collective-permute-start.16 = (bf16[128,1792]{1,0:T(8,128)(2,1)S(1)}, bf16[128,1792]{1,0:T(8,128)(2,1)S(1)}, u32[]{:S(2)}, u32[]{:S(2)}) collective-permute-start(bf16[128,1792]{1,0:T(8,128)(2,1)S(1)} %collective-permute-done.15.refs_11_), channel_id=1, source_target_pairs={{0,32},{1,33},{2,34},{3,35},{4,36},{5,37},{6,38},{7,39},{8,104},{9... | collective-permute-start | bytes 1376264 | tf_op jit(solution)/shard_map/ppermute | solution.py:22
  60.7 16.1 %collective-permute-start.8 = (bf16[256,1024]{1,0:T(8,128)(2,1)S(1)}, bf16[256,1024]{1,0:T(8,128)(2,1)S(1)}, u32[]{:S(2)}, u32[]{:S(2)}) collective-permute-start(bf16[256,1024]{1,0:T(8,128)(2,1)S(1)} %collective-permute-done.7.refs_3_), channel_id=1, source_target_pairs={{0,2},{1,3},{2,4},{3,5},{4,6},{5,7},{6,0},{7,1},{8,14},{9,15},{10,... | collective-permute-start | bytes 1572872 | tf_op jit(solution)/shard_map/ppermute | solution.py:22
  66.4 11.2 %collective-permute-start.12 = (bf16[256,1024]{1,0:T(8,128)(2,1)S(1)}, bf16[256,1024]{1,0:T(8,128)(2,1)S(1)}, u32[]{:S(2)}, u32[]{:S(2)}) collective-permute-start(bf16[256,1024]{1,0:T(8,128)(2,1)S(1)} %collective-permute-done.11.refs_3_.refs_7_), channel_id=1, source_target_pairs={{0,2},{1,3},{2,4},{3,5},{4,6},{5,7},{6,0},{7,1},{8,14},{9,15},{10,... | collective-permute-start | bytes 1572872 | tf_op jit(solution)/shard_map/ppermute | solution.py:22
  89.4 36.2 %collective-permute-start.35 = (bf16[384,1792]{1,0:T(8,128)(2,1)S(1)}, bf16[384,1792]{1,0:T(8,128)(2,1)S(1)}, u32[]{:S(2)}, u32[]{:S(2)}) collective-permute-start(bf16[384,1792]{1,0:T(8,128)(2,1)S(1)} %get-tuple-element.192), channel_id=1, source_target_pairs={{0,16},{1,17},{2,18},{3,19},{4,20},{5,21},{6,22},{7,23},{8,24},{9,... | collective-permute-start | bytes 4128776 | tf_op jit(solution)/shard_map/ppermute | solution.py:22
  93.7 14.6 %collective-permute-start.29 = (bf16[256,896]{1,0:T(8,128)(2,1)S(1)}, bf16[256,896]{1,0:T(8,128)(2,1)S(1)}, u32[]{:S(2)}, u32[]{:S(2)}) collective-permute-start(bf16[256,896]{1,0:T(8,128)(2,1)S(1)} %get-tuple-element.187), channel_id=1, source_target_pairs={{0,32},{1,33},{2,34},{3,35},{4,36},{5,37},{6,38},{7,39},{8,104},{9... | collective-permute-start | bytes 1376264 | tf_op jit(solution)/shard_map/ppermute | solution.py:22
  101.4 17.1 %collective-permute-start.26 = (bf16[512,896]{1,0:T(8,128)(2,1)S(1)}, bf16[512,896]{1,0:T(8,128)(2,1)S(1)}, u32[]{:S(2)}, u32[]{:S(2)}) collective-permute-start(bf16[512,896]{1,0:T(8,128)(2,1)S(1)} %get-tuple-element.173), channel_id=1, source_target_pairs={{0,8},{1,9},{2,10},{3,11},{4,12},{5,13},{6,14},{7,15},{8,0},{9,1},... | collective-permute-start | bytes 2752520 | tf_op jit(solution)/shard_map/ppermute | solution.py:22
  101.5 20.9 %collective-permute-start.27 = (bf16[512,896]{1,0:T(8,128)(2,1)S(1)}, bf16[512,896]{1,0:T(8,128)(2,1)S(1)}, u32[]{:S(2)}, u32[]{:S(2)}) collective-permute-start(bf16[512,896]{1,0:T(8,128)(2,1)S(1)} %get-tuple-element.174), channel_id=1, source_target_pairs={{0,8},{1,9},{2,10},{3,11},{4,12},{5,13},{6,14},{7,15},{8,0},{9,1},... | collective-permute-start | bytes 2752520 | tf_op jit(solution)/shard_map/ppermute | solution.py:22
  113.2 21.4 %collective-permute-start.34 = (bf16[128,1792]{1,0:T(8,128)(2,1)S(1)}, bf16[128,1792]{1,0:T(8,128)(2,1)S(1)}, u32[]{:S(2)}, u32[]{:S(2)}) collective-permute-start(bf16[128,1792]{1,0:T(8,128)(2,1)S(1)} %get-tuple-element.191), channel_id=1, source_target_pairs={{0,16},{1,17},{2,18},{3,19},{4,20},{5,21},{6,22},{7,23},{8,24},{9,... | collective-permute-start | bytes 1376264 | tf_op jit(solution)/shard_map/ppermute | solution.py:22
  118.5 14.5 %collective-permute-start.31 = (bf16[256,896]{1,0:T(8,128)(2,1)S(1)}, bf16[256,896]{1,0:T(8,128)(2,1)S(1)}, u32[]{:S(2)}, u32[]{:S(2)}) collective-permute-start(bf16[256,896]{1,0:T(8,128)(2,1)S(1)} %add_convert_fusion), channel_id=1, source_target_pairs={{0,32},{1,33},{2,34},{3,35},{4,36},{5,37},{6,38},{7,39},{8,104},{9... | collective-permute-start | bytes 1376264 | tf_op jit(solution)/shard_map/ppermute | solution.py:22
  (16 other events, 109.8 us)

commit v7 on v6

--- a/solution.py
+++ b/solution.py
@@ -153,13 +153,11 @@
         out[...] = (product * factor).astype(BF16)
 
 
-def chip_kernel(place, *refs):
-    half, start = refs[0].shape[1], 0
-    for out in refs[4:]:
+def chip_kernel(place, mine, core, *outs):
+    start = 0
+    for out in outs:
         rows = slice(start, start + out.shape[0])
-        for i in range(2):
-            total = refs[i][rows, :] + refs[2 + i][rows, :].astype(F32)
-            out[:, i * half : (i + 1) * half] = total.astype(BF16)
+        out[...] = (mine[rows, :] + core[rows, :].astype(F32)).astype(BF16)
         start = rows.stop
 
 
@@ -235,7 +233,7 @@
     core.append(ring_z(core[2]))
     far.append(ring_y(far[2]))
     weights = near + far
-    hid_core = [send(tied(x, far[3]), c=1) for x in (hid_own[: 2 * share], hid_own[2 * share :])]
+    hid_core = [send(tied(hid_own[: 2 * share], far[3], near[3]), c=1), send(tied(hid_own[2 * share :], far[3]), c=1)]
 
     def hidden_grad(l, c, side, outs, *after, more=()):
         wide = slice(0, columns) if side is None else slice(side * half, (side + 1) * half)
@@ -246,7 +244,7 @@
 
         return call(
             kernel, outs, place, *tied((own, core)[c], *after), *weights, *more,
-            us=size / half * 1.6, scratch=[pltpu.VMEM((tokens, quarter), BF16), pltpu.VMEM((quarter, size), BF16)],
+            us=0.0 if l else 3.2, scratch=[pltpu.VMEM((tokens, quarter), BF16), pltpu.VMEM((quarter, size), BF16)],
         )
 
     factor = 1.0 / float(np.sqrt(np.float32(tokens * 16)))
@@ -261,13 +259,13 @@
         )
 
     out = [shape(tokens, half)] * 2
-    outs = hidden_grad(1, 1, None, out, hid_core[0])
-    mine = hidden_grad(1, 0, None, [shape(tokens, half, dtype=F32)] * 2, outs[0])
-    hid_last = send(tied(hid_pair, own[3], core[3], near[3], hid_core[0]), c=1)
-    outs = [send(x, c=1) for x in outs]
-    sizes = [6, 2]
-    pairs = call(chip_kernel, [shape(n * share, columns) for n in sizes], place, *mine, *outs)
-    first = term(1, mine[0])
+    (chip_out,) = hidden_grad(1, 1, None, [shape(tokens, columns)], hid_core[0])
+    (mine,) = hidden_grad(1, 0, None, [shape(tokens, columns, dtype=F32)], chip_out)
+    chip_out = send(chip_out, c=1)
+    hid_last = send(tied(hid_pair, mine, hid_core[0]), c=1)
+    sizes = [8]
+    pairs = call(chip_kernel, [shape(n * share, columns) for n in sizes], place, mine, chip_out)
+    first = term(1, pairs[0])
     second = term(2, first[0])
     core_out = [send(x, c=1) for x in hidden_grad(0, 1, None, out, second[0])]
     first = [ring_y(x) for x in first]
@@ -292,8 +290,7 @@
             scratch=[pltpu.VMEM((count, 2, share, columns), BF16), pltpu.SemaphoreType.DMA((count, 2))],
         )
 
-    gradient = gradients(0, pairs[0], mine)
-    gate_grad, up_grad = gradients(sizes[0], pairs[1], tied(mine, down_grad), *gradient)
+    gate_grad, up_grad = gradients(0, pairs[0], tied(mine, down_grad))
     return (gate_grad, up_grad, down_grad)
 
 

time: 137 us -> 129 us (0.942)
  waiting for transfers between devices: 59.1 us -> 51.5 us
  starting transfers between devices: 33.4 us -> 34.9 us
    ppermute x36 -> x34, waiting for transfers between devices: 59.1 us -> 51.5 us  [permuted(): return lax.ppermute(x, ('dp', 'tensor'), pairs)]
    ppermute x36 -> x34, starting transfers between devices: 33.4 us -> 34.9 us  [permuted(): return lax.ppermute(x, ('dp', 'tensor'), pairs)]
    pallas_call x16 -> x15, Pallas kernels: 36.9 us -> 35.6 us  [call(): pl.pallas_call(kernel, out_shape=outs, input_output_aliases=alias or {},...]
  transfers between devices with their start and end apart: 36 -> 34, of which waited for: 18 -> 16; matrix products, arithmetic and copies ran while one was open for 0% -> 0% of each run, Pallas kernels for 25% -> 25%
where the time goes in v7:
time: 129 us
  waiting for transfers between devices  51.5 us (40%)
  Pallas kernels  35.6 us (28%)
  starting transfers between devices  34.9 us (27%)
  local copies, waits for them, and re-layouts  5.42 us (4%)
    ppermute x34, waiting for transfers between devices, permuted(): return lax.ppermute(x, ('dp', 'tensor'), pairs)  51.5 us
    pallas_call x15, Pallas kernels, call(): pl.pallas_call(kernel, out_shape=outs, input_output_aliases=alias or {},...  35.6 us
    ppermute x34, starting transfers between devices, permuted(): return lax.ppermute(x, ('dp', 'tensor'), pairs)  34.9 us
    unnamed x8, local copies, waits for them, and re-layouts  5.22 us
  transfers between devices with their start and end apart: 34, of which 16 were waited for; matrix products, arithmetic and copies ran while one was open for 0% of the time, Pallas kernels for 25%

profile of v7, /device:TPU:0, one launch (start us, length us, event | category | flops | bytes accessed | tf_op | source)
XLA Modules:
  0.0 129.0 jit_solution(6309979229501656149)
XLA Ops:
  3.7 4.2 %collective-permute-start.3 = (bf16[64,1792]{1,0:T(8,128)(2,1)S(1)}, bf16[64,1792]{1,0:T(8,128)(2,1)S(1)}, u32[]{:S(2)}, u32[]{:S(2)}) collective-permute-start(bf16[64,1792]{1,0:T(8,128)(2,1)S(1)} %get-tuple-element.101), channel_id=1, source_target_pairs={{0,6},{1,7},{2,0},{3,1},{4,2},{5,3},{6,4},{7,5},{8,14},{9,15},{10,... | collective-permute-start | bytes 688136 | tf_op jit(solution)/shard_map/ppermute | solution.py:22
  9.1 2.8 %collective-permute-start.2 = (bf16[64,2048]{1,0:T(8,128)(2,1)S(1)}, bf16[64,2048]{1,0:T(8,128)(2,1)S(1)}, u32[]{:S(2)}, u32[]{:S(2)}) collective-permute-start(bf16[64,2048]{1,0:T(8,128)(2,1)S(1)} %get-tuple-element.99), channel_id=1, source_target_pairs={{0,17},{1,16},{2,19},{3,18},{4,21},{5,20},{6,23},{7,22},{8,25},{9,... | collective-permute-start | bytes 786440 | tf_op jit(solution)/shard_map/ppermute | solution.py:22
  15.7 2.8 %shard_map.68 = (bf16[512,1792]{1,0:T(8,128)(2,1)S(1)}, bf16[512,1792]{1,0:T(8,128)(2,1)S(1)}, bf16[512,1792]{1,0:T(8,128)(2,1)S(1)}) custom-call(s32[5]{0:T(128)S(1)} %stack.23.place.refs_0_, bf16[512,1792]{1,0:T(8,128)(2,1)S(1)} %copy-done, bf16[512,1792]{1,0:T(8,128)(2,1)S(1)} %copy-done.1), custom_call_target="tpu_custom_call" | custom-call | tf_op jit(solution)/shard_map/pallas_call | solution.py:47
  21.7 3.1 %collective-permute-start.13 = (bf16[128,1792]{1,0:T(8,128)(2,1)S(1)}, bf16[128,1792]{1,0:T(8,128)(2,1)S(1)}, u32[]{:S(2)}, u32[]{:S(2)}) collective-permute-start(bf16[128,1792]{1,0:T(8,128)(2,1)S(1)} %get-tuple-element.115), channel_id=1, source_target_pairs={{0,1},{1,0},{2,3},{3,2},{4,5},{5,4},{6,7},{7,6},{8,9},{9,8},{10,11... | collective-permute-start | bytes 1376264 | tf_op jit(solution)/shard_map/ppermute | solution.py:22
  27.6 9.1 %collective-permute-done.13.refs_9_ = bf16[128,1792]{1,0:T(8,128)(2,1)S(1)} collective-permute-done((bf16[128,1792]{1,0:T(8,128)(2,1)S(1)}, bf16[128,1792]{1,0:T(8,128)(2,1)S(1)}, u32[]{:S(2)}, u32[]{:S(2)}) %collective-permute-start.13) | collective-permute-done | bytes 458784 | tf_op jit(solution)/shard_map/ppermute | solution.py:22
  38.8 2.2 %collective-permute-start.10 = (bf16[256,1024]{1,0:T(8,128)(2,1)S(1)}, bf16[256,1024]{1,0:T(8,128)(2,1)S(1)}, u32[]{:S(2)}, u32[]{:S(2)}) collective-permute-start(bf16[256,1024]{1,0:T(8,128)(2,1)S(1)} %collective-permute-done.9.refs_1_.refs_5_), channel_id=1, source_target_pairs={{0,2},{1,3},{2,4},{3,5},{4,6},{5,7},{6,0},{7,1},{8,14},{9,15},{10,... | collective-permute-start | bytes 1572872 | tf_op jit(solution)/shard_map/ppermute | solution.py:22
  42.9 3.5 %collective-permute-done.14.refs_10_ = bf16[128,1792]{1,0:T(8,128)(2,1)S(1)} collective-permute-done((bf16[128,1792]{1,0:T(8,128)(2,1)S(1)}, bf16[128,1792]{1,0:T(8,128)(2,1)S(1)}, u32[]{:S(2)}, u32[]{:S(2)}) %collective-permute-start.14) | collective-permute-done | bytes 458784 | tf_op jit(solution)/shard_map/ppermute | solution.py:22
  46.8 2.7 %collective-permute-done.10.refs_2_.refs_6_ = bf16[256,1024]{1,0:T(8,128)(2,1)S(1)} collective-permute-done((bf16[256,1024]{1,0:T(8,128)(2,1)S(1)}, bf16[256,1024]{1,0:T(8,128)(2,1)S(1)}, u32[]{:S(2)}, u32[]{:S(2)}) %collective-permute-start.10) | collective-permute-done | bytes 524320 | tf_op jit(solution)/shard_map/ppermute | solution.py:22
  50.2 4.9 %collective-permute-done.6.refs_2_ = bf16[256,1024]{1,0:T(8,128)(2,1)S(1)} collective-permute-done((bf16[256,1024]{1,0:T(8,128)(2,1)S(1)}, bf16[256,1024]{1,0:T(8,128)(2,1)S(1)}, u32[]{:S(2)}, u32[]{:S(2)}) %collective-permute-start.6) | collective-permute-done | bytes 524320 | tf_op jit(solution)/shard_map/ppermute | solution.py:22
  61.4 4.9 %collective-permute-done.7.refs_3_ = bf16[256,1024]{1,0:T(8,128)(2,1)S(1)} collective-permute-done((bf16[256,1024]{1,0:T(8,128)(2,1)S(1)}, bf16[256,1024]{1,0:T(8,128)(2,1)S(1)}, u32[]{:S(2)}, u32[]{:S(2)}) %collective-permute-start.7) | collective-permute-done | bytes 524320 | tf_op jit(solution)/shard_map/ppermute | solution.py:22
  67.1 3.3 %collective-permute-done.16.refs_12_ = bf16[128,1792]{1,0:T(8,128)(2,1)S(1)} collective-permute-done((bf16[128,1792]{1,0:T(8,128)(2,1)S(1)}, bf16[128,1792]{1,0:T(8,128)(2,1)S(1)}, u32[]{:S(2)}, u32[]{:S(2)}) %collective-permute-start.16) | collective-permute-done | bytes 458784 | tf_op jit(solution)/shard_map/ppermute | solution.py:22
  72.2 3.2 %shard_map.71 = bf16[512,1792]{1,0:T(8,128)(2,1)S(1)} custom-call(s32[5]{0:T(128)S(1)} %stack.23.place.refs_0_, bf16[256,1024]{1,0:T(8,128)(2,1)S(1)} %collective-permute-done.9.refs_1_.refs_5_, bf16[256,1024]{1,0:T(8,128)(2,1)S(1)} %collective-permute-done.10.refs_2_.refs_6_, bf16[256,1024]{1,0:T(8,128)(2,1)S(1)} %collective-permute-done.11.refs_3_.refs_7_, ...), custom_call_target="tpu_custom_call" | custom-call | tf_op jit(solution)/shard_map/pallas_call | solution.py:47
  77.6 3.2 %shard_map.72.mine = f32[512,1792]{1,0:T(8,128)S(1)} custom-call(s32[5]{0:T(128)S(1)} %stack.23.place.refs_0_, bf16[256,1024]{1,0:T(8,128)(2,1)S(1)} %get-tuple-element.165.refs_1_, bf16[256,1024]{1,0:T(8,128)(2,1)S(1)} %collective-permute-done.6.refs_2_, bf16[256,1024]{1,0:T(8,128)(2,1)S(1)} %collective-permute-done.7.refs_3_, ...), custom_call_target="tpu_custom_call" | custom-call | tf_op jit(solution)/shard_map/pallas_call | solution.py:47
  84.3 2.3 %collective-permute-done.22.refs_11_ = bf16[384,1792]{1,0:T(8,128)(2,1)S(1)} collective-permute-done((bf16[384,1792]{1,0:T(8,128)(2,1)S(1)}, bf16[384,1792]{1,0:T(8,128)(2,1)S(1)}, u32[]{:S(2)}, u32[]{:S(2)}) %collective-permute-start.22) | collective-permute-done | bytes 1376288 | tf_op jit(solution)/shard_map/ppermute | solution.py:22
  86.6 3.3 %shard_map.74 = (bf16[256,896]{1,0:T(8,128)(2,1)S(1)}, bf16[256,896]{1,0:T(8,128)(2,1)S(1)}) custom-call(s32[5]{0:T(128)S(1)} %stack.23.place.refs_0_, bf16[256,1024]{1,0:T(8,128)(2,1)S(1)} %get-tuple-element.165.refs_1_, bf16[256,1024]{1,0:T(8,128)(2,1)S(1)} %collective-permute-done.6.refs_2_, bf16[256,1024]{1,0:T(8,128)(2,1)S(1)} %collective-permute-done.7.refs_3_, ...), custom_call_target="tpu_custom_call" | custom-call | flops 3409999872 | tf_op jit(solution)/shard_map/pallas_call | solution.py:47
  92.8 3.3 %shard_map.76 = (bf16[256,896]{1,0:T(8,128)(2,1)S(1)}, bf16[256,896]{1,0:T(8,128)(2,1)S(1)}) custom-call(s32[5]{0:T(128)S(1)} %stack.23.place.refs_0_, bf16[256,1024]{1,0:T(8,128)(2,1)S(1)} %get-tuple-element.165.refs_1_, bf16[256,1024]{1,0:T(8,128)(2,1)S(1)} %collective-permute-done.6.refs_2_, bf16[256,1024]{1,0:T(8,128)(2,1)S(1)} %collective-permute-done.7.refs_3_, ...), custom_call_target="tpu_custom_call" | custom-call | flops 3409999872 | tf_op jit(solution)/shard_map/pallas_call | solution.py:47
  96.1 3.2 %shard_map.77 = (bf16[512,896]{1,0:T(8,128)(2,1)S(1)}, bf16[512,896]{1,0:T(8,128)(2,1)S(1)}) custom-call(s32[5]{0:T(128)S(1)} %stack.23.place.refs_0_, bf16[256,1024]{1,0:T(8,128)(2,1)S(1)} %collective-permute-done.9.refs_1_.refs_5_, bf16[256,1024]{1,0:T(8,128)(2,1)S(1)} %collective-permute-done.10.refs_2_.refs_6_, ...), custom_call_target="tpu_custom_call" | custom-call | flops 3520000000 | tf_op jit(solution)/shard_map/pallas_call | solution.py:47
  100.3 4.3 %collective-permute-done.30 = bf16[256,896]{1,0:T(8,128)(2,1)S(1)} collective-permute-done((bf16[256,896]{1,0:T(8,128)(2,1)S(1)}, bf16[256,896]{1,0:T(8,128)(2,1)S(1)}, u32[]{:S(2)}, u32[]{:S(2)}) %collective-permute-start.30) | collective-permute-done | bytes 458784 | tf_op jit(solution)/shard_map/ppermute | solution.py:22
  105.3 3.3 %shard_map.75 = (bf16[256,896]{1,0:T(8,128)(2,1)S(1)}, bf16[256,896]{1,0:T(8,128)(2,1)S(1)}) custom-call(s32[5]{0:T(128)S(1)} %stack.23.place.refs_0_, bf16[256,1024]{1,0:T(8,128)(2,1)S(1)} %get-tuple-element.165.refs_1_, bf16[256,1024]{1,0:T(8,128)(2,1)S(1)} %collective-permute-done.6.refs_2_, bf16[256,1024]{1,0:T(8,128)(2,1)S(1)} %collective-permute-done.7.refs_3_, ...), custom_call_target="tpu_custom_call" | custom-call | flops 3409999872 | tf_op jit(solution)/shard_map/pallas_call | solution.py:47
  110.1 4.6 %collective-permute-done.31 = bf16[256,896]{1,0:T(8,128)(2,1)S(1)} collective-permute-done((bf16[256,896]{1,0:T(8,128)(2,1)S(1)}, bf16[256,896]{1,0:T(8,128)(2,1)S(1)}, u32[]{:S(2)}, u32[]{:S(2)}) %collective-permute-start.31) | collective-permute-done | bytes 458784 | tf_op jit(solution)/shard_map/ppermute | solution.py:22
  115.0 3.3 %shard_map.79 = (bf16[256,896]{1,0:T(8,128)(2,1)S(1)}, bf16[256,896]{1,0:T(8,128)(2,1)S(1)}) custom-call(s32[5]{0:T(128)S(1)} %stack.23.place.refs_0_, bf16[256,1024]{1,0:T(8,128)(2,1)S(1)} %get-tuple-element.165.refs_1_, bf16[256,1024]{1,0:T(8,128)(2,1)S(1)} %collective-permute-done.6.refs_2_, bf16[256,1024]{1,0:T(8,128)(2,1)S(1)} %collective-permute-done.7.refs_3_, ...), custom_call_target="tpu_custom_call" | custom-call | flops 3409999872 | tf_op jit(solution)/shard_map/pallas_call | solution.py:47
  118.2 3.2 %shard_map.78.refs_3_ = f32[512,1792]{1,0:T(8,128)S(1)} custom-call(s32[5]{0:T(128)S(1)} %stack.23.place.refs_0_, bf16[256,1024]{1,0:T(8,128)(2,1)S(1)} %get-tuple-element.165.refs_1_, bf16[256,1024]{1,0:T(8,128)(2,1)S(1)} %collective-permute-done.6.refs_2_, bf16[256,1024]{1,0:T(8,128)(2,1)S(1)} %collective-permute-done.7.refs_3_, ...), custom_call_target="tpu_custom_call" | custom-call | flops 3520000000 | tf_op jit(solution)/shard_map/pallas_call | solution.py:47
  121.5 3.1 %collective-permute-done.32.refs_3_ = bf16[256,896]{1,0:T(8,128)(2,1)S(1)} collective-permute-done((bf16[256,896]{1,0:T(8,128)(2,1)S(1)}, bf16[256,896]{1,0:T(8,128)(2,1)S(1)}, u32[]{:S(2)}, u32[]{:S(2)}) %collective-permute-start.32) | collective-permute-done | bytes 458784 | tf_op jit(solution)/shard_map/ppermute | solution.py:22
  126.2 2.6 %shard_map.81 = (bf16[512,1792]{1,0:T(8,128)(2,1)}, bf16[512,1792]{1,0:T(8,128)(2,1)}) custom-call(s32[5]{0:T(128)S(1)} %stack.23.place.refs_0_, bf16[512,1792]{1,0:T(8,128)(2,1)S(1)} %get-tuple-element.95.refs_1_, bf16[512,1792]{1,0:T(8,128)(2,1)S(1)} %get-tuple-element.96.refs_2_, f32[512,1792]{1,0:T(8,128)S(1)} %shard_map.78.refs_3_, ...), custom_call_target="tpu_custom_call" | custom-call | tf_op jit(solution)/shard_map/pallas_call | solution.py:47
  (74 shorter events, 41.6 us)
Async XLA Ops:
  3.7 14.8 %collective-permute-start.3 = (bf16[64,1792]{1,0:T(8,128)(2,1)S(1)}, bf16[64,1792]{1,0:T(8,128)(2,1)S(1)}, u32[]{:S(2)}, u32[]{:S(2)}) collective-permute-start(bf16[64,1792]{1,0:T(8,128)(2,1)S(1)} %get-tuple-element.101), channel_id=1, source_target_pairs={{0,6},{1,7},{2,0},{3,1},{4,2},{5,3},{6,4},{7,5},{8,14},{9,15},{10,... | collective-permute-start | bytes 688136 | tf_op jit(solution)/shard_map/ppermute | solution.py:22
  7.9 11.3 %collective-permute-start.4 = (bf16[64,1792]{1,0:T(8,128)(2,1)S(1)}, bf16[64,1792]{1,0:T(8,128)(2,1)S(1)}, u32[]{:S(2)}, u32[]{:S(2)}) collective-permute-start(bf16[64,1792]{1,0:T(8,128)(2,1)S(1)} %get-tuple-element.102), channel_id=1, source_target_pairs={{0,4},{1,5},{2,6},{3,7},{4,0},{5,1},{6,2},{7,3},{8,12},{9,13},{10,... | collective-permute-start | bytes 688136 | tf_op jit(solution)/shard_map/ppermute | solution.py:22
  7.9 13.2 %collective-permute-start.5 = (bf16[64,1792]{1,0:T(8,128)(2,1)S(1)}, bf16[64,1792]{1,0:T(8,128)(2,1)S(1)}, u32[]{:S(2)}, u32[]{:S(2)}) collective-permute-start(bf16[64,1792]{1,0:T(8,128)(2,1)S(1)} %get-tuple-element.103), channel_id=1, source_target_pairs={{0,2},{1,3},{2,4},{3,5},{4,6},{5,7},{6,0},{7,1},{8,10},{9,11},{10,... | collective-permute-start | bytes 688136 | tf_op jit(solution)/shard_map/ppermute | solution.py:22
  9.1 17.2 %collective-permute-start.2 = (bf16[64,2048]{1,0:T(8,128)(2,1)S(1)}, bf16[64,2048]{1,0:T(8,128)(2,1)S(1)}, u32[]{:S(2)}, u32[]{:S(2)}) collective-permute-start(bf16[64,2048]{1,0:T(8,128)(2,1)S(1)} %get-tuple-element.99), channel_id=1, source_target_pairs={{0,17},{1,16},{2,19},{3,18},{4,21},{5,20},{6,23},{7,22},{8,25},{9,... | collective-permute-start | bytes 786440 | tf_op jit(solution)/shard_map/ppermute | solution.py:22
  11.9 14.5 %collective-permute-start = (bf16[64,2048]{1,0:T(8,128)(2,1)S(1)}, bf16[64,2048]{1,0:T(8,128)(2,1)S(1)}, u32[]{:S(2)}, u32[]{:S(2)}) collective-permute-start(bf16[64,2048]{1,0:T(8,128)(2,1)S(1)} %get-tuple-element.109.refs_0_), channel_id=1, source_target_pairs={{0,1},{1,0},{2,3},{3,2},{4,5},{5,4},{6,7},{7,6},{8,9},{9,8},{10,11... | collective-permute-start | bytes 786440 | tf_op jit(solution)/shard_map/ppermute | solution.py:22
  21.7 15.0 %collective-permute-start.13 = (bf16[128,1792]{1,0:T(8,128)(2,1)S(1)}, bf16[128,1792]{1,0:T(8,128)(2,1)S(1)}, u32[]{:S(2)}, u32[]{:S(2)}) collective-permute-start(bf16[128,1792]{1,0:T(8,128)(2,1)S(1)} %get-tuple-element.115), channel_id=1, source_target_pairs={{0,1},{1,0},{2,3},{3,2},{4,5},{5,4},{6,7},{7,6},{8,9},{9,8},{10,11... | collective-permute-start | bytes 1376264 | tf_op jit(solution)/shard_map/ppermute | solution.py:22
  24.8 13.5 %collective-permute-start.17 = (bf16[128,1792]{1,0:T(8,128)(2,1)S(1)}, bf16[128,1792]{1,0:T(8,128)(2,1)S(1)}, u32[]{:S(2)}, u32[]{:S(2)}) collective-permute-start(bf16[128,1792]{1,0:T(8,128)(2,1)S(1)} %get-tuple-element.108.refs_5_), channel_id=1, source_target_pairs={{0,32},{1,33},{2,34},{3,35},{4,36},{5,37},{6,38},{7,39},{8,104},{9... | collective-permute-start | bytes 1376264 | tf_op jit(solution)/shard_map/ppermute | solution.py:22
  27.0 11.8 %collective-permute-start.9 = (bf16[256,1024]{1,0:T(8,128)(2,1)S(1)}, bf16[256,1024]{1,0:T(8,128)(2,1)S(1)}, u32[]{:S(2)}, u32[]{:S(2)}) collective-permute-start(bf16[256,1024]{1,0:T(8,128)(2,1)S(1)} %get-tuple-element.114), channel_id=1, source_target_pairs={{0,8},{1,9},{2,10},{3,11},{4,12},{5,13},{6,14},{7,15},{8,0},{9,1},... | collective-permute-start | bytes 1572872 | tf_op jit(solution)/shard_map/ppermute | solution.py:22
  38.3 42.5 %collective-permute-start.23 = (bf16[512,1792]{1,0:T(8,128)(2,1)S(1)}, bf16[512,1792]{1,0:T(8,128)(2,1)S(1)}, u32[]{:S(2)}, u32[]{:S(2)}) collective-permute-start(bf16[512,1792]{1,0:T(8,128)(2,1)S(1)} %get-tuple-element.134.refs_9_), channel_id=1, source_target_pairs={{0,16},{1,17},{2,18},{3,19},{4,20},{5,21},{6,22},{7,23},{8,24},{9,... | collective-permute-start | bytes 5505032 | tf_op jit(solution)/shard_map/ppermute | solution.py:22
  38.8 10.7 %collective-permute-start.10 = (bf16[256,1024]{1,0:T(8,128)(2,1)S(1)}, bf16[256,1024]{1,0:T(8,128)(2,1)S(1)}, u32[]{:S(2)}, u32[]{:S(2)}) collective-permute-start(bf16[256,1024]{1,0:T(8,128)(2,1)S(1)} %collective-permute-done.9.refs_1_.refs_5_), channel_id=1, source_target_pairs={{0,2},{1,3},{2,4},{3,5},{4,6},{5,7},{6,0},{7,1},{8,14},{9,15},{10,... | collective-permute-start | bytes 1572872 | tf_op jit(solution)/shard_map/ppermute | solution.py:22
  41.0 14.1 %collective-permute-start.6 = (bf16[256,1024]{1,0:T(8,128)(2,1)S(1)}, bf16[256,1024]{1,0:T(8,128)(2,1)S(1)}, u32[]{:S(2)}, u32[]{:S(2)}) collective-permute-start(bf16[256,1024]{1,0:T(8,128)(2,1)S(1)} %get-tuple-element.165.refs_1_), channel_id=1, source_target_pairs={{0,2},{1,3},{2,4},{3,5},{4,6},{5,7},{6,0},{7,1},{8,14},{9,15},{10,... | collective-permute-start | bytes 1572872 | tf_op jit(solution)/shard_map/ppermute | solution.py:22
  41.3 14.5 %collective-permute-start.18 = (bf16[128,1792]{1,0:T(8,128)(2,1)S(1)}, bf16[128,1792]{1,0:T(8,128)(2,1)S(1)}, u32[]{:S(2)}, u32[]{:S(2)}) collective-permute-start(bf16[128,1792]{1,0:T(8,128)(2,1)S(1)} %collective-permute-done.17.refs_6_), channel_id=1, source_target_pairs={{0,32},{1,33},{2,34},{3,35},{4,36},{5,37},{6,38},{7,39},{8,104},{9... | collective-permute-start | bytes 1376264 | tf_op jit(solution)/shard_map/ppermute | solution.py:22
  46.4 11.0 %collective-permute-start.15 = (bf16[128,1792]{1,0:T(8,128)(2,1)S(1)}, bf16[128,1792]{1,0:T(8,128)(2,1)S(1)}, u32[]{:S(2)}, u32[]{:S(2)}) collective-permute-start(bf16[128,1792]{1,0:T(8,128)(2,1)S(1)} %collective-permute-done.14.refs_10_), channel_id=1, source_target_pairs={{0,32},{1,33},{2,34},{3,35},{4,36},{5,37},{6,38},{7,39},{8,104},{9... | collective-permute-start | bytes 1376264 | tf_op jit(solution)/shard_map/ppermute | solution.py:22
  49.5 11.2 %collective-permute-start.11 = (bf16[256,1024]{1,0:T(8,128)(2,1)S(1)}, bf16[256,1024]{1,0:T(8,128)(2,1)S(1)}, u32[]{:S(2)}, u32[]{:S(2)}) collective-permute-start(bf16[256,1024]{1,0:T(8,128)(2,1)S(1)} %collective-permute-done.10.refs_2_.refs_6_), channel_id=1, source_target_pairs={{0,2},{1,3},{2,4},{3,5},{4,6},{5,7},{6,0},{7,1},{8,14},{9,15},{10,... | collective-permute-start | bytes 1572872 | tf_op jit(solution)/shard_map/ppermute | solution.py:22
  55.1 11.2 %collective-permute-start.7 = (bf16[256,1024]{1,0:T(8,128)(2,1)S(1)}, bf16[256,1024]{1,0:T(8,128)(2,1)S(1)}, u32[]{:S(2)}, u32[]{:S(2)}) collective-permute-start(bf16[256,1024]{1,0:T(8,128)(2,1)S(1)} %collective-permute-done.6.refs_2_), channel_id=1, source_target_pairs={{0,2},{1,3},{2,4},{3,5},{4,6},{5,7},{6,0},{7,1},{8,14},{9,15},{10,... | collective-permute-start | bytes 1572872 | tf_op jit(solution)/shard_map/ppermute | solution.py:22
  55.8 11.3 %collective-permute-start.19 = (bf16[128,1792]{1,0:T(8,128)(2,1)S(1)}, bf16[128,1792]{1,0:T(8,128)(2,1)S(1)}, u32[]{:S(2)}, u32[]{:S(2)}) collective-permute-start(bf16[128,1792]{1,0:T(8,128)(2,1)S(1)} %collective-permute-done.18.refs_7_), channel_id=1, source_target_pairs={{0,32},{1,33},{2,34},{3,35},{4,36},{5,37},{6,38},{7,39},{8,104},{9... | collective-permute-start | bytes 1376264 | tf_op jit(solution)/shard_map/ppermute | solution.py:22
  57.4 13.0 %collective-permute-start.16 = (bf16[128,1792]{1,0:T(8,128)(2,1)S(1)}, bf16[128,1792]{1,0:T(8,128)(2,1)S(1)}, u32[]{:S(2)}, u32[]{:S(2)}) collective-permute-start(bf16[128,1792]{1,0:T(8,128)(2,1)S(1)} %collective-permute-done.15.refs_11_), channel_id=1, source_target_pairs={{0,32},{1,33},{2,34},{3,35},{4,36},{5,37},{6,38},{7,39},{8,104},{9... | collective-permute-start | bytes 1376264 | tf_op jit(solution)/shard_map/ppermute | solution.py:22
  60.7 11.2 %collective-permute-start.12 = (bf16[256,1024]{1,0:T(8,128)(2,1)S(1)}, bf16[256,1024]{1,0:T(8,128)(2,1)S(1)}, u32[]{:S(2)}, u32[]{:S(2)}) collective-permute-start(bf16[256,1024]{1,0:T(8,128)(2,1)S(1)} %collective-permute-done.11.refs_3_.refs_7_), channel_id=1, source_target_pairs={{0,2},{1,3},{2,4},{3,5},{4,6},{5,7},{6,0},{7,1},{8,14},{9,15},{10,... | collective-permute-start | bytes 1572872 | tf_op jit(solution)/shard_map/ppermute | solution.py:22
  66.4 11.2 %collective-permute-start.8 = (bf16[256,1024]{1,0:T(8,128)(2,1)S(1)}, bf16[256,1024]{1,0:T(8,128)(2,1)S(1)}, u32[]{:S(2)}, u32[]{:S(2)}) collective-permute-start(bf16[256,1024]{1,0:T(8,128)(2,1)S(1)} %collective-permute-done.7.refs_3_), channel_id=1, source_target_pairs={{0,2},{1,3},{2,4},{3,5},{4,6},{5,7},{6,0},{7,1},{8,14},{9,15},{10,... | collective-permute-start | bytes 1572872 | tf_op jit(solution)/shard_map/ppermute | solution.py:22
  82.4 43.8 %collective-permute-start.33 = (bf16[512,1792]{1,0:T(8,128)(2,1)S(1)}, bf16[512,1792]{1,0:T(8,128)(2,1)S(1)}, u32[]{:S(2)}, u32[]{:S(2)}) collective-permute-start(bf16[512,1792]{1,0:T(8,128)(2,1)S(1)} %shard_map.73), channel_id=1, source_target_pairs={{0,16},{1,17},{2,18},{3,19},{4,20},{5,21},{6,22},{7,23},{8,24},{9,... | collective-permute-start | bytes 5505032 | tf_op jit(solution)/shard_map/ppermute | solution.py:22
  91.5 13.0 %collective-permute-start.30 = (bf16[256,896]{1,0:T(8,128)(2,1)S(1)}, bf16[256,896]{1,0:T(8,128)(2,1)S(1)}, u32[]{:S(2)}, u32[]{:S(2)}) collective-permute-start(bf16[256,896]{1,0:T(8,128)(2,1)S(1)} %get-tuple-element.177), channel_id=1, source_target_pairs={{0,32},{1,33},{2,34},{3,35},{4,36},{5,37},{6,38},{7,39},{8,104},{9... | collective-permute-start | bytes 1376264 | tf_op jit(solution)/shard_map/ppermute | solution.py:22
  99.3 18.9 %collective-permute-start.27 = (bf16[512,896]{1,0:T(8,128)(2,1)S(1)}, bf16[512,896]{1,0:T(8,128)(2,1)S(1)}, u32[]{:S(2)}, u32[]{:S(2)}) collective-permute-start(bf16[512,896]{1,0:T(8,128)(2,1)S(1)} %get-tuple-element.163), channel_id=1, source_target_pairs={{0,8},{1,9},{2,10},{3,11},{4,12},{5,13},{6,14},{7,15},{8,0},{9,1},... | collective-permute-start | bytes 2752520 | tf_op jit(solution)/shard_map/ppermute | solution.py:22
  99.6 18.7 %collective-permute-start.28 = (bf16[512,896]{1,0:T(8,128)(2,1)S(1)}, bf16[512,896]{1,0:T(8,128)(2,1)S(1)}, u32[]{:S(2)}, u32[]{:S(2)}) collective-permute-start(bf16[512,896]{1,0:T(8,128)(2,1)S(1)} %get-tuple-element.164), channel_id=1, source_target_pairs={{0,8},{1,9},{2,10},{3,11},{4,12},{5,13},{6,14},{7,15},{8,0},{9,1},... | collective-permute-start | bytes 2752520 | tf_op jit(solution)/shard_map/ppermute | solution.py:22
  109.9 11.6 %collective-permute-start.29 = (bf16[256,896]{1,0:T(8,128)(2,1)S(1)}, bf16[256,896]{1,0:T(8,128)(2,1)S(1)}, u32[]{:S(2)}, u32[]{:S(2)}) collective-permute-start(bf16[256,896]{1,0:T(8,128)(2,1)S(1)} %add_convert_fusion.2), channel_id=1, source_target_pairs={{0,32},{1,33},{2,34},{3,35},{4,36},{5,37},{6,38},{7,39},{8,104},{9... | collective-permute-start | bytes 1376264 | tf_op jit(solution)/shard_map/ppermute | solution.py:22
  (14 other events, 81.7 us)

commit v8 on v7

--- a/solution.py
+++ b/solution.py
@@ -112,19 +112,25 @@
     up_factor[...] = (gate * sig).astype(BF16)
 
 
-def product_kernel(l, columns, count, place, *refs):
-    chunks, weights, more, outs, (rows_of, all_of) = refs[:4], refs[4:12], refs[12 : -2 - count], refs[-2 - count : -2], refs[-2:]
-    rows, cut = chunks[0].shape[0] // 2, weights[0].shape[0] // 4
+def rows_kernel(place, *refs):
+    weights, out = refs[:8], refs[8]
+    cut = weights[0].shape[0] // 4
     for s in range(4):
-        rows_of[chunk_rows(place, s, rows), :] = chunks[s][l * rows : (l + 1) * rows, :]
         for j in range(2):
             for z in range(4):
                 to = ((behind(place, 0, s) * 4 + z) * 2 + (place[4] + j) % 2) * cut
-                all_of[at(to, cut, 32), :] = weights[4 * j + s][z * cut : (z + 1) * cut, columns]
-    half = weights[0].shape[1] // 2
-    for i in range(all_of.shape[1] // half):
+                out[at(to, cut, 32), :] = weights[4 * j + s][z * cut : (z + 1) * cut, :]
+
+
+def product_kernel(l, count, place, *refs):
+    chunks, weight, more, outs, rows_of = refs[:4], refs[4], refs[5 : -1 - count], refs[-1 - count : -1], refs[-1]
+    rows = chunks[0].shape[0] // 2
+    for s in range(4):
+        rows_of[chunk_rows(place, s, rows), :] = chunks[s][l * rows : (l + 1) * rows, :]
+    half = weight.shape[1] // 2
+    for i in range(2):
         part = slice(i * half, (i + 1) * half)
-        product = jnp.dot(rows_of[...], all_of[:, part], preferred_element_type=F32)
+        product = jnp.dot(rows_of[...], weight[:, part], preferred_element_type=F32)
         if more:
             product = product + more[i][...].astype(F32)
         if count == 1:
@@ -233,18 +239,17 @@
     core.append(ring_z(core[2]))
     far.append(ring_y(far[2]))
     weights = near + far
-    hid_core = [send(tied(hid_own[: 2 * share], far[3], near[3]), c=1), send(tied(hid_own[2 * share :], far[3]), c=1)]
-
-    def hidden_grad(l, c, side, outs, *after, more=()):
-        wide = slice(0, columns) if side is None else slice(side * half, (side + 1) * half)
-        size = wide.stop - wide.start
-
+    hid_core = [send(tied(hid_own[: 2 * share], far[3], near[3], own[3]), c=1), send(tied(hid_own[2 * share :], far[3]), c=1)]
+
+    (weight,) = call(rows_kernel, [shape(quarter, columns)], place, *weights)
+
+    def hidden_grad(l, c, outs, *after, more=()):
         def kernel(*refs):
-            product_kernel(l, wide, len(outs), *refs)
+            product_kernel(l, len(outs), *refs)
 
         return call(
-            kernel, outs, place, *tied((own, core)[c], *after), *weights, *more,
-            us=0.0 if l else 3.2, scratch=[pltpu.VMEM((tokens, quarter), BF16), pltpu.VMEM((quarter, size), BF16)],
+            kernel, outs, place, *tied((own, core)[c], *after), weight, *more,
+            us=0.0 if l else 3.2, scratch=[pltpu.VMEM((tokens, quarter), BF16)],
         )
 
     factor = 1.0 / float(np.sqrt(np.float32(tokens * 16)))
@@ -259,20 +264,20 @@
         )
 
     out = [shape(tokens, half)] * 2
-    (chip_out,) = hidden_grad(1, 1, None, [shape(tokens, columns)], hid_core[0])
-    (mine,) = hidden_grad(1, 0, None, [shape(tokens, columns, dtype=F32)], chip_out)
+    (chip_out,) = hidden_grad(1, 1, [shape(tokens, columns)], hid_core[0])
+    (mine,) = hidden_grad(1, 0, [shape(tokens, columns, dtype=F32)], chip_out)
     chip_out = send(chip_out, c=1)
     hid_last = send(tied(hid_pair, mine, hid_core[0]), c=1)
     sizes = [8]
     pairs = call(chip_kernel, [shape(n * share, columns) for n in sizes], place, mine, chip_out)
     first = term(1, pairs[0])
     second = term(2, first[0])
-    core_out = [send(x, c=1) for x in hidden_grad(0, 1, None, out, second[0])]
+    core_out = [send(x, c=1) for x in hidden_grad(0, 1, out, second[0])]
     first = [ring_y(x) for x in first]
     second = [ring_y(added(a, b)) for a, b in zip(second, first)]
     third = term(3, first[0])
     third_0 = third[0]
-    (mine,) = hidden_grad(0, 0, None, [shape(tokens, columns, dtype=F32)], third[0], second[0], more=core_out)
+    (mine,) = hidden_grad(0, 0, [shape(tokens, columns, dtype=F32)], third[0], second[0], more=core_out)
     third = [ring_y(added(a, b)) for a, b in zip(third, second)]
     pairs = [send(x, l=1) for x in pairs]
     last = term(0, third_0)

time: 129 us -> 129 us (level)
  starting transfers between devices: 34.9 us -> 33.6 us
    ppermute x34, starting transfers between devices: 34.9 us -> 33.6 us  [permuted(): return lax.ppermute(x, ('dp', 'tensor'), pairs)]
    pallas_call x15 -> x16, Pallas kernels: 35.6 us -> 35.4 us  [call(): pl.pallas_call(kernel, out_shape=outs, input_output_aliases=alias or {},...]
  transfers between devices with their start and end apart: 34 -> 34, of which waited for: 16 -> 18; matrix products, arithmetic and copies ran while one was open for 0% -> 0% of each run, Pallas kernels for 25% -> 25%
where the time goes in v8:
time: 129 us; the launch traced here: 128 us
  waiting for transfers between devices  52.3 us (41%)
  Pallas kernels  35.4 us (27%)
  starting transfers between devices  33.6 us (26%)
  local copies, waits for them, and re-layouts  5.42 us (4%)
    ppermute x34, waiting for transfers between devices, permuted(): return lax.ppermute(x, ('dp', 'tensor'), pairs)  52.3 us
    pallas_call x16, Pallas kernels, call(): pl.pallas_call(kernel, out_shape=outs, input_output_aliases=alias or {},...  35.4 us
    ppermute x34, starting transfers between devices, permuted(): return lax.ppermute(x, ('dp', 'tensor'), pairs)  33.6 us
    unnamed x8, local copies, waits for them, and re-layouts  5.22 us
  transfers between devices with their start and end apart: 34, of which 18 were waited for; matrix products, arithmetic and copies ran while one was open for 0% of the time, Pallas kernels for 25%

profile of v8, /device:TPU:0, one launch (start us, length us, event | category | flops | bytes accessed | tf_op | source)
XLA Modules:
  0.0 128.3 jit_solution(8579722319643810059)
XLA Ops:
  3.7 4.2 %collective-permute-start.3 = (bf16[64,1792]{1,0:T(8,128)(2,1)S(1)}, bf16[64,1792]{1,0:T(8,128)(2,1)S(1)}, u32[]{:S(2)}, u32[]{:S(2)}) collective-permute-start(bf16[64,1792]{1,0:T(8,128)(2,1)S(1)} %get-tuple-element.101), channel_id=1, source_target_pairs={{0,6},{1,7},{2,0},{3,1},{4,2},{5,3},{6,4},{7,5},{8,14},{9,15},{10,... | collective-permute-start | bytes 688136 | tf_op jit(solution)/shard_map/ppermute | solution.py:22
  9.1 2.8 %collective-permute-start.2 = (bf16[64,2048]{1,0:T(8,128)(2,1)S(1)}, bf16[64,2048]{1,0:T(8,128)(2,1)S(1)}, u32[]{:S(2)}, u32[]{:S(2)}) collective-permute-start(bf16[64,2048]{1,0:T(8,128)(2,1)S(1)} %get-tuple-element.99), channel_id=1, source_target_pairs={{0,17},{1,16},{2,19},{3,18},{4,21},{5,20},{6,23},{7,22},{8,25},{9,... | collective-permute-start | bytes 786440 | tf_op jit(solution)/shard_map/ppermute | solution.py:22
  15.7 2.8 %shard_map.68 = (bf16[512,1792]{1,0:T(8,128)(2,1)S(1)}, bf16[512,1792]{1,0:T(8,128)(2,1)S(1)}, bf16[512,1792]{1,0:T(8,128)(2,1)S(1)}) custom-call(s32[5]{0:T(128)S(1)} %stack.23.place.refs_0_, bf16[512,1792]{1,0:T(8,128)(2,1)S(1)} %copy-done, bf16[512,1792]{1,0:T(8,128)(2,1)S(1)} %copy-done.1), custom_call_target="tpu_custom_call" | custom-call | tf_op jit(solution)/shard_map/pallas_call | solution.py:47
  21.7 3.1 %collective-permute-start.13 = (bf16[128,1792]{1,0:T(8,128)(2,1)S(1)}, bf16[128,1792]{1,0:T(8,128)(2,1)S(1)}, u32[]{:S(2)}, u32[]{:S(2)}) collective-permute-start(bf16[128,1792]{1,0:T(8,128)(2,1)S(1)} %get-tuple-element.115), channel_id=1, source_target_pairs={{0,1},{1,0},{2,3},{3,2},{4,5},{5,4},{6,7},{7,6},{8,9},{9,8},{10,11... | collective-permute-start | bytes 1376264 | tf_op jit(solution)/shard_map/ppermute | solution.py:22
  27.6 3.2 %collective-permute-start.6 = (bf16[256,1024]{1,0:T(8,128)(2,1)S(1)}, bf16[256,1024]{1,0:T(8,128)(2,1)S(1)}, u32[]{:S(2)}, u32[]{:S(2)}) collective-permute-start(bf16[256,1024]{1,0:T(8,128)(2,1)S(1)} %get-tuple-element.165.refs_1_), channel_id=1, source_target_pairs={{0,2},{1,3},{2,4},{3,5},{4,6},{5,7},{6,0},{7,1},{8,14},{9,15},{10,... | collective-permute-start | bytes 1572872 | tf_op jit(solution)/shard_map/ppermute | solution.py:22
  30.9 5.8 %collective-permute-done.13.refs_4_ = bf16[128,1792]{1,0:T(8,128)(2,1)S(1)} collective-permute-done((bf16[128,1792]{1,0:T(8,128)(2,1)S(1)}, bf16[128,1792]{1,0:T(8,128)(2,1)S(1)}, u32[]{:S(2)}, u32[]{:S(2)}) %collective-permute-start.13) | collective-permute-done | bytes 458784 | tf_op jit(solution)/shard_map/ppermute | solution.py:22
  42.9 3.5 %collective-permute-done.14.refs_5_ = bf16[128,1792]{1,0:T(8,128)(2,1)S(1)} collective-permute-done((bf16[128,1792]{1,0:T(8,128)(2,1)S(1)}, bf16[128,1792]{1,0:T(8,128)(2,1)S(1)}, u32[]{:S(2)}, u32[]{:S(2)}) %collective-permute-start.14) | collective-permute-done | bytes 458784 | tf_op jit(solution)/shard_map/ppermute | solution.py:22
  46.8 2.7 %collective-permute-done.10.refs_2_.refs_6_ = bf16[256,1024]{1,0:T(8,128)(2,1)S(1)} collective-permute-done((bf16[256,1024]{1,0:T(8,128)(2,1)S(1)}, bf16[256,1024]{1,0:T(8,128)(2,1)S(1)}, u32[]{:S(2)}, u32[]{:S(2)}) %collective-permute-start.10) | collective-permute-done | bytes 524320 | tf_op jit(solution)/shard_map/ppermute | solution.py:22
  50.2 4.9 %collective-permute-done.7.refs_3_ = bf16[256,1024]{1,0:T(8,128)(2,1)S(1)} collective-permute-done((bf16[256,1024]{1,0:T(8,128)(2,1)S(1)}, bf16[256,1024]{1,0:T(8,128)(2,1)S(1)}, u32[]{:S(2)}, u32[]{:S(2)}) %collective-permute-start.7) | collective-permute-done | bytes 524320 | tf_op jit(solution)/shard_map/ppermute | solution.py:22
  61.5 4.0 %collective-permute-done.19.refs_3_ = bf16[128,1792]{1,0:T(8,128)(2,1)S(1)} collective-permute-done((bf16[128,1792]{1,0:T(8,128)(2,1)S(1)}, bf16[128,1792]{1,0:T(8,128)(2,1)S(1)}, u32[]{:S(2)}, u32[]{:S(2)}) %collective-permute-start.19) | collective-permute-done | bytes 458784 | tf_op jit(solution)/shard_map/ppermute | solution.py:22
  66.4 4.1 %collective-permute-done.16.refs_7_ = bf16[128,1792]{1,0:T(8,128)(2,1)S(1)} collective-permute-done((bf16[128,1792]{1,0:T(8,128)(2,1)S(1)}, bf16[128,1792]{1,0:T(8,128)(2,1)S(1)}, u32[]{:S(2)}, u32[]{:S(2)}) %collective-permute-start.16) | collective-permute-done | bytes 458784 | tf_op jit(solution)/shard_map/ppermute | solution.py:22
  72.2 2.9 %shard_map.72 = bf16[512,1792]{1,0:T(8,128)(2,1)S(1)} custom-call(s32[5]{0:T(128)S(1)} %stack.23.place.refs_0_, bf16[256,1024]{1,0:T(8,128)(2,1)S(1)} %collective-permute-done.9.refs_1_.refs_5_, bf16[256,1024]{1,0:T(8,128)(2,1)S(1)} %collective-permute-done.10.refs_2_.refs_6_, bf16[256,1024]{1,0:T(8,128)(2,1)S(1)} %collective-permute-done.11.refs_3_.refs_7_, ...), custom_call_target="tpu_custom_call" | custom-call | tf_op jit(solution)/shard_map/pallas_call | solution.py:47
  75.4 2.9 %shard_map.73.mine = f32[512,1792]{1,0:T(8,128)S(1)} custom-call(s32[5]{0:T(128)S(1)} %stack.23.place.refs_0_, bf16[256,1024]{1,0:T(8,128)(2,1)S(1)} %get-tuple-element.165.refs_1_, bf16[256,1024]{1,0:T(8,128)(2,1)S(1)} %collective-permute-done.6.refs_2_, bf16[256,1024]{1,0:T(8,128)(2,1)S(1)} %collective-permute-done.7.refs_3_, ...), custom_call_target="tpu_custom_call" | custom-call | tf_op jit(solution)/shard_map/pallas_call | solution.py:47
  82.6 3.3 %collective-permute-done.22.refs_11_ = bf16[384,1792]{1,0:T(8,128)(2,1)S(1)} collective-permute-done((bf16[384,1792]{1,0:T(8,128)(2,1)S(1)}, bf16[384,1792]{1,0:T(8,128)(2,1)S(1)}, u32[]{:S(2)}, u32[]{:S(2)}) %collective-permute-start.22) | collective-permute-done | bytes 1376288 | tf_op jit(solution)/shard_map/ppermute | solution.py:22
  85.9 3.3 %shard_map.75 = (bf16[256,896]{1,0:T(8,128)(2,1)S(1)}, bf16[256,896]{1,0:T(8,128)(2,1)S(1)}) custom-call(s32[5]{0:T(128)S(1)} %stack.23.place.refs_0_, bf16[256,1024]{1,0:T(8,128)(2,1)S(1)} %get-tuple-element.165.refs_1_, bf16[256,1024]{1,0:T(8,128)(2,1)S(1)} %collective-permute-done.6.refs_2_, bf16[256,1024]{1,0:T(8,128)(2,1)S(1)} %collective-permute-done.7.refs_3_, ...), custom_call_target="tpu_custom_call" | custom-call | flops 3409999872 | tf_op jit(solution)/shard_map/pallas_call | solution.py:47
  90.3 3.3 %shard_map.77 = (bf16[256,896]{1,0:T(8,128)(2,1)S(1)}, bf16[256,896]{1,0:T(8,128)(2,1)S(1)}) custom-call(s32[5]{0:T(128)S(1)} %stack.23.place.refs_0_, bf16[256,1024]{1,0:T(8,128)(2,1)S(1)} %get-tuple-element.165.refs_1_, bf16[256,1024]{1,0:T(8,128)(2,1)S(1)} %collective-permute-done.6.refs_2_, bf16[256,1024]{1,0:T(8,128)(2,1)S(1)} %collective-permute-done.7.refs_3_, ...), custom_call_target="tpu_custom_call" | custom-call | flops 3409999872 | tf_op jit(solution)/shard_map/pallas_call | solution.py:47
  93.6 2.9 %shard_map.78 = (bf16[512,896]{1,0:T(8,128)(2,1)S(1)}, bf16[512,896]{1,0:T(8,128)(2,1)S(1)}) custom-call(s32[5]{0:T(128)S(1)} %stack.23.place.refs_0_, bf16[256,1024]{1,0:T(8,128)(2,1)S(1)} %collective-permute-done.9.refs_1_.refs_5_, bf16[256,1024]{1,0:T(8,128)(2,1)S(1)} %collective-permute-done.10.refs_2_.refs_6_, ...), custom_call_target="tpu_custom_call" | custom-call | flops 3520000000 | tf_op jit(solution)/shard_map/pallas_call | solution.py:47
  99.2 4.7 %collective-permute-done.30 = bf16[256,896]{1,0:T(8,128)(2,1)S(1)} collective-permute-done((bf16[256,896]{1,0:T(8,128)(2,1)S(1)}, bf16[256,896]{1,0:T(8,128)(2,1)S(1)}, u32[]{:S(2)}, u32[]{:S(2)}) %collective-permute-start.30) | collective-permute-done | bytes 458784 | tf_op jit(solution)/shard_map/ppermute | solution.py:22
  104.3 3.3 %shard_map.76 = (bf16[256,896]{1,0:T(8,128)(2,1)S(1)}, bf16[256,896]{1,0:T(8,128)(2,1)S(1)}) custom-call(s32[5]{0:T(128)S(1)} %stack.23.place.refs_0_, bf16[256,1024]{1,0:T(8,128)(2,1)S(1)} %get-tuple-element.165.refs_1_, bf16[256,1024]{1,0:T(8,128)(2,1)S(1)} %collective-permute-done.6.refs_2_, bf16[256,1024]{1,0:T(8,128)(2,1)S(1)} %collective-permute-done.7.refs_3_, ...), custom_call_target="tpu_custom_call" | custom-call | flops 3409999872 | tf_op jit(solution)/shard_map/pallas_call | solution.py:47
  109.1 4.9 %collective-permute-done.31 = bf16[256,896]{1,0:T(8,128)(2,1)S(1)} collective-permute-done((bf16[256,896]{1,0:T(8,128)(2,1)S(1)}, bf16[256,896]{1,0:T(8,128)(2,1)S(1)}, u32[]{:S(2)}, u32[]{:S(2)}) %collective-permute-start.31) | collective-permute-done | bytes 458784 | tf_op jit(solution)/shard_map/ppermute | solution.py:22
  114.2 3.3 %shard_map.80 = (bf16[256,896]{1,0:T(8,128)(2,1)S(1)}, bf16[256,896]{1,0:T(8,128)(2,1)S(1)}) custom-call(s32[5]{0:T(128)S(1)} %stack.23.place.refs_0_, bf16[256,1024]{1,0:T(8,128)(2,1)S(1)} %get-tuple-element.165.refs_1_, bf16[256,1024]{1,0:T(8,128)(2,1)S(1)} %collective-permute-done.6.refs_2_, bf16[256,1024]{1,0:T(8,128)(2,1)S(1)} %collective-permute-done.7.refs_3_, ...), custom_call_target="tpu_custom_call" | custom-call | flops 3409999872 | tf_op jit(solution)/shard_map/pallas_call | solution.py:47
  117.5 2.9 %shard_map.79.refs_3_ = f32[512,1792]{1,0:T(8,128)S(1)} custom-call(s32[5]{0:T(128)S(1)} %stack.23.place.refs_0_, bf16[256,1024]{1,0:T(8,128)(2,1)S(1)} %get-tuple-element.165.refs_1_, bf16[256,1024]{1,0:T(8,128)(2,1)S(1)} %collective-permute-done.6.refs_2_, bf16[256,1024]{1,0:T(8,128)(2,1)S(1)} %collective-permute-done.7.refs_3_, ...), custom_call_target="tpu_custom_call" | custom-call | flops 3520000000 | tf_op jit(solution)/shard_map/pallas_call | solution.py:47
  120.5 3.4 %collective-permute-done.32.refs_3_ = bf16[256,896]{1,0:T(8,128)(2,1)S(1)} collective-permute-done((bf16[256,896]{1,0:T(8,128)(2,1)S(1)}, bf16[256,896]{1,0:T(8,128)(2,1)S(1)}, u32[]{:S(2)}, u32[]{:S(2)}) %collective-permute-start.32) | collective-permute-done | bytes 458784 | tf_op jit(solution)/shard_map/ppermute | solution.py:22
  125.6 2.6 %shard_map.82 = (bf16[512,1792]{1,0:T(8,128)(2,1)}, bf16[512,1792]{1,0:T(8,128)(2,1)}) custom-call(s32[5]{0:T(128)S(1)} %stack.23.place.refs_0_, bf16[512,1792]{1,0:T(8,128)(2,1)S(1)} %get-tuple-element.95.refs_1_, bf16[512,1792]{1,0:T(8,128)(2,1)S(1)} %get-tuple-element.96.refs_2_, f32[512,1792]{1,0:T(8,128)S(1)} %shard_map.79.refs_3_, ...), custom_call_target="tpu_custom_call" | custom-call | tf_op jit(solution)/shard_map/pallas_call | solution.py:47
  (75 shorter events, 42.2 us)
Async XLA Ops:
  3.7 14.8 %collective-permute-start.3 = (bf16[64,1792]{1,0:T(8,128)(2,1)S(1)}, bf16[64,1792]{1,0:T(8,128)(2,1)S(1)}, u32[]{:S(2)}, u32[]{:S(2)}) collective-permute-start(bf16[64,1792]{1,0:T(8,128)(2,1)S(1)} %get-tuple-element.101), channel_id=1, source_target_pairs={{0,6},{1,7},{2,0},{3,1},{4,2},{5,3},{6,4},{7,5},{8,14},{9,15},{10,... | collective-permute-start | bytes 688136 | tf_op jit(solution)/shard_map/ppermute | solution.py:22
  7.9 11.3 %collective-permute-start.4 = (bf16[64,1792]{1,0:T(8,128)(2,1)S(1)}, bf16[64,1792]{1,0:T(8,128)(2,1)S(1)}, u32[]{:S(2)}, u32[]{:S(2)}) collective-permute-start(bf16[64,1792]{1,0:T(8,128)(2,1)S(1)} %get-tuple-element.102), channel_id=1, source_target_pairs={{0,4},{1,5},{2,6},{3,7},{4,0},{5,1},{6,2},{7,3},{8,12},{9,13},{10,... | collective-permute-start | bytes 688136 | tf_op jit(solution)/shard_map/ppermute | solution.py:22
  7.9 13.2 %collective-permute-start.5 = (bf16[64,1792]{1,0:T(8,128)(2,1)S(1)}, bf16[64,1792]{1,0:T(8,128)(2,1)S(1)}, u32[]{:S(2)}, u32[]{:S(2)}) collective-permute-start(bf16[64,1792]{1,0:T(8,128)(2,1)S(1)} %get-tuple-element.103), channel_id=1, source_target_pairs={{0,2},{1,3},{2,4},{3,5},{4,6},{5,7},{6,0},{7,1},{8,10},{9,11},{10,... | collective-permute-start | bytes 688136 | tf_op jit(solution)/shard_map/ppermute | solution.py:22
  9.1 17.2 %collective-permute-start.2 = (bf16[64,2048]{1,0:T(8,128)(2,1)S(1)}, bf16[64,2048]{1,0:T(8,128)(2,1)S(1)}, u32[]{:S(2)}, u32[]{:S(2)}) collective-permute-start(bf16[64,2048]{1,0:T(8,128)(2,1)S(1)} %get-tuple-element.99), channel_id=1, source_target_pairs={{0,17},{1,16},{2,19},{3,18},{4,21},{5,20},{6,23},{7,22},{8,25},{9,... | collective-permute-start | bytes 786440 | tf_op jit(solution)/shard_map/ppermute | solution.py:22
  11.9 14.5 %collective-permute-start = (bf16[64,2048]{1,0:T(8,128)(2,1)S(1)}, bf16[64,2048]{1,0:T(8,128)(2,1)S(1)}, u32[]{:S(2)}, u32[]{:S(2)}) collective-permute-start(bf16[64,2048]{1,0:T(8,128)(2,1)S(1)} %get-tuple-element.109.refs_0_), channel_id=1, source_target_pairs={{0,1},{1,0},{2,3},{3,2},{4,5},{5,4},{6,7},{7,6},{8,9},{9,8},{10,11... | collective-permute-start | bytes 786440 | tf_op jit(solution)/shard_map/ppermute | solution.py:22
  21.7 15.0 %collective-permute-start.13 = (bf16[128,1792]{1,0:T(8,128)(2,1)S(1)}, bf16[128,1792]{1,0:T(8,128)(2,1)S(1)}, u32[]{:S(2)}, u32[]{:S(2)}) collective-permute-start(bf16[128,1792]{1,0:T(8,128)(2,1)S(1)} %get-tuple-element.115), channel_id=1, source_target_pairs={{0,1},{1,0},{2,3},{3,2},{4,5},{5,4},{6,7},{7,6},{8,9},{9,8},{10,11... | collective-permute-start | bytes 1376264 | tf_op jit(solution)/shard_map/ppermute | solution.py:22
  24.8 13.5 %collective-permute-start.17 = (bf16[128,1792]{1,0:T(8,128)(2,1)S(1)}, bf16[128,1792]{1,0:T(8,128)(2,1)S(1)}, u32[]{:S(2)}, u32[]{:S(2)}) collective-permute-start(bf16[128,1792]{1,0:T(8,128)(2,1)S(1)} %get-tuple-element.108.refs_0_), channel_id=1, source_target_pairs={{0,32},{1,33},{2,34},{3,35},{4,36},{5,37},{6,38},{7,39},{8,104},{9... | collective-permute-start | bytes 1376264 | tf_op jit(solution)/shard_map/ppermute | solution.py:22
  27.0 11.8 %collective-permute-start.9 = (bf16[256,1024]{1,0:T(8,128)(2,1)S(1)}, bf16[256,1024]{1,0:T(8,128)(2,1)S(1)}, u32[]{:S(2)}, u32[]{:S(2)}) collective-permute-start(bf16[256,1024]{1,0:T(8,128)(2,1)S(1)} %get-tuple-element.114), channel_id=1, source_target_pairs={{0,8},{1,9},{2,10},{3,11},{4,12},{5,13},{6,14},{7,15},{8,0},{9,1},... | collective-permute-start | bytes 1572872 | tf_op jit(solution)/shard_map/ppermute | solution.py:22
  27.6 13.4 %collective-permute-start.6 = (bf16[256,1024]{1,0:T(8,128)(2,1)S(1)}, bf16[256,1024]{1,0:T(8,128)(2,1)S(1)}, u32[]{:S(2)}, u32[]{:S(2)}) collective-permute-start(bf16[256,1024]{1,0:T(8,128)(2,1)S(1)} %get-tuple-element.165.refs_1_), channel_id=1, source_target_pairs={{0,2},{1,3},{2,4},{3,5},{4,6},{5,7},{6,0},{7,1},{8,14},{9,15},{10,... | collective-permute-start | bytes 1572872 | tf_op jit(solution)/shard_map/ppermute | solution.py:22
  38.3 41.9 %collective-permute-start.23 = (bf16[512,1792]{1,0:T(8,128)(2,1)S(1)}, bf16[512,1792]{1,0:T(8,128)(2,1)S(1)}, u32[]{:S(2)}, u32[]{:S(2)}) collective-permute-start(bf16[512,1792]{1,0:T(8,128)(2,1)S(1)} %get-tuple-element.134.refs_9_), channel_id=1, source_target_pairs={{0,16},{1,17},{2,18},{3,19},{4,20},{5,21},{6,22},{7,23},{8,24},{9,... | collective-permute-start | bytes 5505032 | tf_op jit(solution)/shard_map/ppermute | solution.py:22
  38.8 10.7 %collective-permute-start.10 = (bf16[256,1024]{1,0:T(8,128)(2,1)S(1)}, bf16[256,1024]{1,0:T(8,128)(2,1)S(1)}, u32[]{:S(2)}, u32[]{:S(2)}) collective-permute-start(bf16[256,1024]{1,0:T(8,128)(2,1)S(1)} %collective-permute-done.9.refs_1_.refs_5_), channel_id=1, source_target_pairs={{0,2},{1,3},{2,4},{3,5},{4,6},{5,7},{6,0},{7,1},{8,14},{9,15},{10,... | collective-permute-start | bytes 1572872 | tf_op jit(solution)/shard_map/ppermute | solution.py:22
  41.0 14.1 %collective-permute-start.7 = (bf16[256,1024]{1,0:T(8,128)(2,1)S(1)}, bf16[256,1024]{1,0:T(8,128)(2,1)S(1)}, u32[]{:S(2)}, u32[]{:S(2)}) collective-permute-start(bf16[256,1024]{1,0:T(8,128)(2,1)S(1)} %collective-permute-done.6.refs_2_), channel_id=1, source_target_pairs={{0,2},{1,3},{2,4},{3,5},{4,6},{5,7},{6,0},{7,1},{8,14},{9,15},{10,... | collective-permute-start | bytes 1572872 | tf_op jit(solution)/shard_map/ppermute | solution.py:22
  41.3 14.5 %collective-permute-start.18 = (bf16[128,1792]{1,0:T(8,128)(2,1)S(1)}, bf16[128,1792]{1,0:T(8,128)(2,1)S(1)}, u32[]{:S(2)}, u32[]{:S(2)}) collective-permute-start(bf16[128,1792]{1,0:T(8,128)(2,1)S(1)} %collective-permute-done.17.refs_1_), channel_id=1, source_target_pairs={{0,32},{1,33},{2,34},{3,35},{4,36},{5,37},{6,38},{7,39},{8,104},{9... | collective-permute-start | bytes 1376264 | tf_op jit(solution)/shard_map/ppermute | solution.py:22
  46.4 11.0 %collective-permute-start.15 = (bf16[128,1792]{1,0:T(8,128)(2,1)S(1)}, bf16[128,1792]{1,0:T(8,128)(2,1)S(1)}, u32[]{:S(2)}, u32[]{:S(2)}) collective-permute-start(bf16[128,1792]{1,0:T(8,128)(2,1)S(1)} %collective-permute-done.14.refs_5_), channel_id=1, source_target_pairs={{0,32},{1,33},{2,34},{3,35},{4,36},{5,37},{6,38},{7,39},{8,104},{9... | collective-permute-start | bytes 1376264 | tf_op jit(solution)/shard_map/ppermute | solution.py:22
  49.5 11.2 %collective-permute-start.11 = (bf16[256,1024]{1,0:T(8,128)(2,1)S(1)}, bf16[256,1024]{1,0:T(8,128)(2,1)S(1)}, u32[]{:S(2)}, u32[]{:S(2)}) collective-permute-start(bf16[256,1024]{1,0:T(8,128)(2,1)S(1)} %collective-permute-done.10.refs_2_.refs_6_), channel_id=1, source_target_pairs={{0,2},{1,3},{2,4},{3,5},{4,6},{5,7},{6,0},{7,1},{8,14},{9,15},{10,... | collective-permute-start | bytes 1572872 | tf_op jit(solution)/shard_map/ppermute | solution.py:22
  55.1 11.2 %collective-permute-start.8 = (bf16[256,1024]{1,0:T(8,128)(2,1)S(1)}, bf16[256,1024]{1,0:T(8,128)(2,1)S(1)}, u32[]{:S(2)}, u32[]{:S(2)}) collective-permute-start(bf16[256,1024]{1,0:T(8,128)(2,1)S(1)} %collective-permute-done.7.refs_3_), channel_id=1, source_target_pairs={{0,2},{1,3},{2,4},{3,5},{4,6},{5,7},{6,0},{7,1},{8,14},{9,15},{10,... | collective-permute-start | bytes 1572872 | tf_op jit(solution)/shard_map/ppermute | solution.py:22
  57.4 13.0 %collective-permute-start.16 = (bf16[128,1792]{1,0:T(8,128)(2,1)S(1)}, bf16[128,1792]{1,0:T(8,128)(2,1)S(1)}, u32[]{:S(2)}, u32[]{:S(2)}) collective-permute-start(bf16[128,1792]{1,0:T(8,128)(2,1)S(1)} %collective-permute-done.15.refs_6_), channel_id=1, source_target_pairs={{0,32},{1,33},{2,34},{3,35},{4,36},{5,37},{6,38},{7,39},{8,104},{9... | collective-permute-start | bytes 1376264 | tf_op jit(solution)/shard_map/ppermute | solution.py:22
  60.7 11.2 %collective-permute-start.12 = (bf16[256,1024]{1,0:T(8,128)(2,1)S(1)}, bf16[256,1024]{1,0:T(8,128)(2,1)S(1)}, u32[]{:S(2)}, u32[]{:S(2)}) collective-permute-start(bf16[256,1024]{1,0:T(8,128)(2,1)S(1)} %collective-permute-done.11.refs_3_.refs_7_), channel_id=1, source_target_pairs={{0,2},{1,3},{2,4},{3,5},{4,6},{5,7},{6,0},{7,1},{8,14},{9,15},{10,... | collective-permute-start | bytes 1572872 | tf_op jit(solution)/shard_map/ppermute | solution.py:22
  81.7 43.8 %collective-permute-start.33 = (bf16[512,1792]{1,0:T(8,128)(2,1)S(1)}, bf16[512,1792]{1,0:T(8,128)(2,1)S(1)}, u32[]{:S(2)}, u32[]{:S(2)}) collective-permute-start(bf16[512,1792]{1,0:T(8,128)(2,1)S(1)} %shard_map.74), channel_id=1, source_target_pairs={{0,16},{1,17},{2,18},{3,19},{4,20},{5,21},{6,22},{7,23},{8,24},{9,... | collective-permute-start | bytes 5505032 | tf_op jit(solution)/shard_map/ppermute | solution.py:22
  89.3 14.6 %collective-permute-start.30 = (bf16[256,896]{1,0:T(8,128)(2,1)S(1)}, bf16[256,896]{1,0:T(8,128)(2,1)S(1)}, u32[]{:S(2)}, u32[]{:S(2)}) collective-permute-start(bf16[256,896]{1,0:T(8,128)(2,1)S(1)} %get-tuple-element.177), channel_id=1, source_target_pairs={{0,32},{1,33},{2,34},{3,35},{4,36},{5,37},{6,38},{7,39},{8,104},{9... | collective-permute-start | bytes 1376264 | tf_op jit(solution)/shard_map/ppermute | solution.py:22
  96.5 20.9 %collective-permute-start.27 = (bf16[512,896]{1,0:T(8,128)(2,1)S(1)}, bf16[512,896]{1,0:T(8,128)(2,1)S(1)}, u32[]{:S(2)}, u32[]{:S(2)}) collective-permute-start(bf16[512,896]{1,0:T(8,128)(2,1)S(1)} %get-tuple-element.163), channel_id=1, source_target_pairs={{0,8},{1,9},{2,10},{3,11},{4,12},{5,13},{6,14},{7,15},{8,0},{9,1},... | collective-permute-start | bytes 2752520 | tf_op jit(solution)/shard_map/ppermute | solution.py:22
  97.0 20.5 %collective-permute-start.28 = (bf16[512,896]{1,0:T(8,128)(2,1)S(1)}, bf16[512,896]{1,0:T(8,128)(2,1)S(1)}, u32[]{:S(2)}, u32[]{:S(2)}) collective-permute-start(bf16[512,896]{1,0:T(8,128)(2,1)S(1)} %get-tuple-element.164), channel_id=1, source_target_pairs={{0,8},{1,9},{2,10},{3,11},{4,12},{5,13},{6,14},{7,15},{8,0},{9,1},... | collective-permute-start | bytes 2752520 | tf_op jit(solution)/shard_map/ppermute | solution.py:22
  104.0 10.0 %collective-permute-start.31 = (bf16[256,896]{1,0:T(8,128)(2,1)S(1)}, bf16[256,896]{1,0:T(8,128)(2,1)S(1)}, u32[]{:S(2)}, u32[]{:S(2)}) collective-permute-start(bf16[256,896]{1,0:T(8,128)(2,1)S(1)} %add_convert_fusion.1), channel_id=1, source_target_pairs={{0,32},{1,33},{2,34},{3,35},{4,36},{5,37},{6,38},{7,39},{8,104},{9... | collective-permute-start | bytes 1376264 | tf_op jit(solution)/shard_map/ppermute | solution.py:22
  109.0 11.5 %collective-permute-start.29 = (bf16[256,896]{1,0:T(8,128)(2,1)S(1)}, bf16[256,896]{1,0:T(8,128)(2,1)S(1)}, u32[]{:S(2)}, u32[]{:S(2)}) collective-permute-start(bf16[256,896]{1,0:T(8,128)(2,1)S(1)} %add_convert_fusion.2), channel_id=1, source_target_pairs={{0,32},{1,33},{2,34},{3,35},{4,36},{5,37},{6,38},{7,39},{8,104},{9... | collective-permute-start | bytes 1376264 | tf_op jit(solution)/shard_map/ppermute | solution.py:22
  (14 other events, 80.6 us)

commit v9 on v8

--- a/solution.py
+++ b/solution.py
@@ -74,7 +74,7 @@
     return at((4 + (2 * place[2] - 1) * s) % 4 * rows, rows, 128)
 
 
-def pack_kernel(place, grad, weight, own, other, *parts):
+def grad_kernel(place, grad, own, other):
     l, c = place[1], place[2]
     stripe = own.shape[1] // 8
     for out, side in ((own, l), (other, 1 - l)):
@@ -82,6 +82,9 @@
             for k in range(4):
                 to = pl.ds((i * 4 + k) * stripe, stripe)
                 out[:, to] = grad[:, at((k * 4 + side * 2 + core) * stripe, stripe)]
+
+
+def pack_kernel(place, weight, *parts):
     rows, columns = weight.shape[0], parts[0].shape[1]
     for n, (k, j) in enumerate(EIGHT):
         parts[k][j * rows : (j + 1) * rows, :] = weight[:, at(slot(place, k, j) * columns, columns)]
@@ -208,10 +211,8 @@
     cut = quarter // 4
     shard = down_weight.shape[0]
 
-    packed = call(
-        pack_kernel, [shape(share, 2 * quarter)] * 2 + [shape(2 * shard, columns)] * 4, place, out_grad, down_weight
-    )
-    o_own, o_other, parts = packed[0], packed[1], packed[2:]
+    parts = call(pack_kernel, [shape(2 * shard, columns)] * 4, place, down_weight)
+    o_own, o_other = call(grad_kernel, [shape(share, 2 * quarter)] * 2, place, tied(out_grad, parts[0]))
 
     parts = [parts[0]] + [send(parts[4 - k], z=4 - k) for k in (1, 2, 3)]
     block = pl.BlockSpec((share, columns), lambda n, place: (slot(place, n // 2, n % 2), 0))

time: 129 us -> 128 us (level)
  waiting for transfers between devices: 52.3 us -> 48.5 us
  starting transfers between devices: 33.6 us -> 36 us
    ppermute x34, waiting for transfers between devices: 52.3 us -> 48.5 us  [permuted(): return lax.ppermute(x, ('dp', 'tensor'), pairs)]
    ppermute x34, starting transfers between devices: 33.6 us -> 36 us  [permuted(): return lax.ppermute(x, ('dp', 'tensor'), pairs)]
    pallas_call x16 -> x17, Pallas kernels: 35.4 us -> 36 us  [call(): pl.pallas_call(kernel, out_shape=outs, input_output_aliases=alias or {},...]
  transfers between devices with their start and end apart: 34 -> 34, of which waited for: 18 -> 19; matrix products, arithmetic and copies ran while one was open for 0% -> 0% of each run, Pallas kernels for 25% -> 26%
where the time goes in v9:
time: 128 us
  waiting for transfers between devices  48.5 us (38%)
  Pallas kernels  36 us (28%)
  starting transfers between devices  36 us (28%)
  local copies, waits for them, and re-layouts  5.42 us (4%)
    ppermute x34, waiting for transfers between devices, permuted(): return lax.ppermute(x, ('dp', 'tensor'), pairs)  48.5 us
    ppermute x34, starting transfers between devices, permuted(): return lax.ppermute(x, ('dp', 'tensor'), pairs)  36 us
    pallas_call x17, Pallas kernels, call(): pl.pallas_call(kernel, out_shape=outs, input_output_aliases=alias or {},...  36 us
    unnamed x8, local copies, waits for them, and re-layouts  5.22 us
  transfers between devices with their start and end apart: 34, of which 19 were waited for; matrix products, arithmetic and copies ran while one was open for 0% of the time, Pallas kernels for 26%

profile of v9, /device:TPU:0, one launch (start us, length us, event | category | flops | bytes accessed | tf_op | source)
XLA Modules:
  0.0 127.5 jit_solution(9803045716044616215)
XLA Ops:
  2.6 4.2 %collective-permute-start.3 = (bf16[64,1792]{1,0:T(8,128)(2,1)S(1)}, bf16[64,1792]{1,0:T(8,128)(2,1)S(1)}, u32[]{:S(2)}, u32[]{:S(2)}) collective-permute-start(bf16[64,1792]{1,0:T(8,128)(2,1)S(1)} %get-tuple-element.103), channel_id=1, source_target_pairs={{0,6},{1,7},{2,0},{3,1},{4,2},{5,3},{6,4},{7,5},{8,14},{9,15},{10,... | collective-permute-start | bytes 688136 | tf_op jit(solution)/shard_map/ppermute | solution.py:22
  9.7 2.8 %collective-permute-start.2 = (bf16[64,2048]{1,0:T(8,128)(2,1)S(1)}, bf16[64,2048]{1,0:T(8,128)(2,1)S(1)}, u32[]{:S(2)}, u32[]{:S(2)}) collective-permute-start(bf16[64,2048]{1,0:T(8,128)(2,1)S(1)} %get-tuple-element.102), channel_id=1, source_target_pairs={{0,17},{1,16},{2,19},{3,18},{4,21},{5,20},{6,23},{7,22},{8,25},{9,... | collective-permute-start | bytes 786440 | tf_op jit(solution)/shard_map/ppermute | solution.py:22
  16.3 2.8 %shard_map.69 = (bf16[512,1792]{1,0:T(8,128)(2,1)S(1)}, bf16[512,1792]{1,0:T(8,128)(2,1)S(1)}, bf16[512,1792]{1,0:T(8,128)(2,1)S(1)}) custom-call(s32[5]{0:T(128)S(1)} %stack.23.place.refs_0_, bf16[512,1792]{1,0:T(8,128)(2,1)S(1)} %copy-done, bf16[512,1792]{1,0:T(8,128)(2,1)S(1)} %copy-done.1), custom_call_target="tpu_custom_call" | custom-call | tf_op jit(solution)/shard_map/pallas_call | solution.py:47
  20.6 3.1 %collective-permute-start.13 = (bf16[128,1792]{1,0:T(8,128)(2,1)S(1)}, bf16[128,1792]{1,0:T(8,128)(2,1)S(1)}, u32[]{:S(2)}, u32[]{:S(2)}) collective-permute-start(bf16[128,1792]{1,0:T(8,128)(2,1)S(1)} %get-tuple-element.117), channel_id=1, source_target_pairs={{0,1},{1,0},{2,3},{3,2},{4,5},{5,4},{6,7},{7,6},{8,9},{9,8},{10,11... | collective-permute-start | bytes 1376264 | tf_op jit(solution)/shard_map/ppermute | solution.py:22
  27.9 3.6 %collective-permute-start.6 = (bf16[256,1024]{1,0:T(8,128)(2,1)S(1)}, bf16[256,1024]{1,0:T(8,128)(2,1)S(1)}, u32[]{:S(2)}, u32[]{:S(2)}) collective-permute-start(bf16[256,1024]{1,0:T(8,128)(2,1)S(1)} %get-tuple-element.167.refs_1_), channel_id=1, source_target_pairs={{0,2},{1,3},{2,4},{3,5},{4,6},{5,7},{6,0},{7,1},{8,14},{9,15},{10,... | collective-permute-start | bytes 1572872 | tf_op jit(solution)/shard_map/ppermute | solution.py:22
  31.5 5.8 %collective-permute-done.13.refs_4_ = bf16[128,1792]{1,0:T(8,128)(2,1)S(1)} collective-permute-done((bf16[128,1792]{1,0:T(8,128)(2,1)S(1)}, bf16[128,1792]{1,0:T(8,128)(2,1)S(1)}, u32[]{:S(2)}, u32[]{:S(2)}) %collective-permute-start.13) | collective-permute-done | bytes 458784 | tf_op jit(solution)/shard_map/ppermute | solution.py:22
  43.5 3.4 %collective-permute-done.14.refs_5_ = bf16[128,1792]{1,0:T(8,128)(2,1)S(1)} collective-permute-done((bf16[128,1792]{1,0:T(8,128)(2,1)S(1)}, bf16[128,1792]{1,0:T(8,128)(2,1)S(1)}, u32[]{:S(2)}, u32[]{:S(2)}) %collective-permute-start.14) | collective-permute-done | bytes 458784 | tf_op jit(solution)/shard_map/ppermute | solution.py:22
  47.3 2.5 %collective-permute-done.10.refs_2_.refs_6_ = bf16[256,1024]{1,0:T(8,128)(2,1)S(1)} collective-permute-done((bf16[256,1024]{1,0:T(8,128)(2,1)S(1)}, bf16[256,1024]{1,0:T(8,128)(2,1)S(1)}, u32[]{:S(2)}, u32[]{:S(2)}) %collective-permute-start.10) | collective-permute-done | bytes 524320 | tf_op jit(solution)/shard_map/ppermute | solution.py:22
  50.8 4.6 %collective-permute-done.7.refs_3_ = bf16[256,1024]{1,0:T(8,128)(2,1)S(1)} collective-permute-done((bf16[256,1024]{1,0:T(8,128)(2,1)S(1)}, bf16[256,1024]{1,0:T(8,128)(2,1)S(1)}, u32[]{:S(2)}, u32[]{:S(2)}) %collective-permute-start.7) | collective-permute-done | bytes 524320 | tf_op jit(solution)/shard_map/ppermute | solution.py:22
  62.1 4.0 %collective-permute-done.19.refs_3_ = bf16[128,1792]{1,0:T(8,128)(2,1)S(1)} collective-permute-done((bf16[128,1792]{1,0:T(8,128)(2,1)S(1)}, bf16[128,1792]{1,0:T(8,128)(2,1)S(1)}, u32[]{:S(2)}, u32[]{:S(2)}) %collective-permute-start.19) | collective-permute-done | bytes 458784 | tf_op jit(solution)/shard_map/ppermute | solution.py:22
  66.7 4.4 %collective-permute-done.16.refs_7_ = bf16[128,1792]{1,0:T(8,128)(2,1)S(1)} collective-permute-done((bf16[128,1792]{1,0:T(8,128)(2,1)S(1)}, bf16[128,1792]{1,0:T(8,128)(2,1)S(1)}, u32[]{:S(2)}, u32[]{:S(2)}) %collective-permute-start.16) | collective-permute-done | bytes 458784 | tf_op jit(solution)/shard_map/ppermute | solution.py:22
  72.9 2.9 %shard_map.73 = bf16[512,1792]{1,0:T(8,128)(2,1)S(1)} custom-call(s32[5]{0:T(128)S(1)} %stack.23.place.refs_0_, bf16[256,1024]{1,0:T(8,128)(2,1)S(1)} %collective-permute-done.9.refs_1_.refs_5_, bf16[256,1024]{1,0:T(8,128)(2,1)S(1)} %collective-permute-done.10.refs_2_.refs_6_, bf16[256,1024]{1,0:T(8,128)(2,1)S(1)} %collective-permute-done.11.refs_3_.refs_7_, ...), custom_call_target="tpu_custom_call" | custom-call | tf_op jit(solution)/shard_map/pallas_call | solution.py:47
  76.0 2.9 %shard_map.74.mine = f32[512,1792]{1,0:T(8,128)S(1)} custom-call(s32[5]{0:T(128)S(1)} %stack.23.place.refs_0_, bf16[256,1024]{1,0:T(8,128)(2,1)S(1)} %get-tuple-element.167.refs_1_, bf16[256,1024]{1,0:T(8,128)(2,1)S(1)} %collective-permute-done.6.refs_2_, bf16[256,1024]{1,0:T(8,128)(2,1)S(1)} %collective-permute-done.7.refs_3_, ...), custom_call_target="tpu_custom_call" | custom-call | tf_op jit(solution)/shard_map/pallas_call | solution.py:47
  82.3 2.9 %collective-permute-done.22.refs_11_ = bf16[384,1792]{1,0:T(8,128)(2,1)S(1)} collective-permute-done((bf16[384,1792]{1,0:T(8,128)(2,1)S(1)}, bf16[384,1792]{1,0:T(8,128)(2,1)S(1)}, u32[]{:S(2)}, u32[]{:S(2)}) %collective-permute-start.22) | collective-permute-done | bytes 1376288 | tf_op jit(solution)/shard_map/ppermute | solution.py:22
  85.2 3.3 %shard_map.76 = (bf16[256,896]{1,0:T(8,128)(2,1)S(1)}, bf16[256,896]{1,0:T(8,128)(2,1)S(1)}) custom-call(s32[5]{0:T(128)S(1)} %stack.23.place.refs_0_, bf16[256,1024]{1,0:T(8,128)(2,1)S(1)} %get-tuple-element.167.refs_1_, bf16[256,1024]{1,0:T(8,128)(2,1)S(1)} %collective-permute-done.6.refs_2_, bf16[256,1024]{1,0:T(8,128)(2,1)S(1)} %collective-permute-done.7.refs_3_, ...), custom_call_target="tpu_custom_call" | custom-call | flops 3409999872 | tf_op jit(solution)/shard_map/pallas_call | solution.py:47
  90.6 3.3 %shard_map.78 = (bf16[256,896]{1,0:T(8,128)(2,1)S(1)}, bf16[256,896]{1,0:T(8,128)(2,1)S(1)}) custom-call(s32[5]{0:T(128)S(1)} %stack.23.place.refs_0_, bf16[256,1024]{1,0:T(8,128)(2,1)S(1)} %get-tuple-element.167.refs_1_, bf16[256,1024]{1,0:T(8,128)(2,1)S(1)} %collective-permute-done.6.refs_2_, bf16[256,1024]{1,0:T(8,128)(2,1)S(1)} %collective-permute-done.7.refs_3_, ...), custom_call_target="tpu_custom_call" | custom-call | flops 3409999872 | tf_op jit(solution)/shard_map/pallas_call | solution.py:47
  93.9 2.9 %shard_map.79 = (bf16[512,896]{1,0:T(8,128)(2,1)S(1)}, bf16[512,896]{1,0:T(8,128)(2,1)S(1)}) custom-call(s32[5]{0:T(128)S(1)} %stack.23.place.refs_0_, bf16[256,1024]{1,0:T(8,128)(2,1)S(1)} %collective-permute-done.9.refs_1_.refs_5_, bf16[256,1024]{1,0:T(8,128)(2,1)S(1)} %collective-permute-done.10.refs_2_.refs_6_, ...), custom_call_target="tpu_custom_call" | custom-call | flops 3520000000 | tf_op jit(solution)/shard_map/pallas_call | solution.py:47
  98.4 4.7 %collective-permute-done.30 = bf16[256,896]{1,0:T(8,128)(2,1)S(1)} collective-permute-done((bf16[256,896]{1,0:T(8,128)(2,1)S(1)}, bf16[256,896]{1,0:T(8,128)(2,1)S(1)}, u32[]{:S(2)}, u32[]{:S(2)}) %collective-permute-start.30) | collective-permute-done | bytes 458784 | tf_op jit(solution)/shard_map/ppermute | solution.py:22
  103.6 3.3 %shard_map.77 = (bf16[256,896]{1,0:T(8,128)(2,1)S(1)}, bf16[256,896]{1,0:T(8,128)(2,1)S(1)}) custom-call(s32[5]{0:T(128)S(1)} %stack.23.place.refs_0_, bf16[256,1024]{1,0:T(8,128)(2,1)S(1)} %get-tuple-element.167.refs_1_, bf16[256,1024]{1,0:T(8,128)(2,1)S(1)} %collective-permute-done.6.refs_2_, bf16[256,1024]{1,0:T(8,128)(2,1)S(1)} %collective-permute-done.7.refs_3_, ...), custom_call_target="tpu_custom_call" | custom-call | flops 3409999872 | tf_op jit(solution)/shard_map/pallas_call | solution.py:47
  108.3 4.9 %collective-permute-done.31 = bf16[256,896]{1,0:T(8,128)(2,1)S(1)} collective-permute-done((bf16[256,896]{1,0:T(8,128)(2,1)S(1)}, bf16[256,896]{1,0:T(8,128)(2,1)S(1)}, u32[]{:S(2)}, u32[]{:S(2)}) %collective-permute-start.31) | collective-permute-done | bytes 458784 | tf_op jit(solution)/shard_map/ppermute | solution.py:22
  113.4 3.3 %shard_map.81 = (bf16[256,896]{1,0:T(8,128)(2,1)S(1)}, bf16[256,896]{1,0:T(8,128)(2,1)S(1)}) custom-call(s32[5]{0:T(128)S(1)} %stack.23.place.refs_0_, bf16[256,1024]{1,0:T(8,128)(2,1)S(1)} %get-tuple-element.167.refs_1_, bf16[256,1024]{1,0:T(8,128)(2,1)S(1)} %collective-permute-done.6.refs_2_, bf16[256,1024]{1,0:T(8,128)(2,1)S(1)} %collective-permute-done.7.refs_3_, ...), custom_call_target="tpu_custom_call" | custom-call | flops 3409999872 | tf_op jit(solution)/shard_map/pallas_call | solution.py:47
  116.7 2.9 %shard_map.80.refs_3_ = f32[512,1792]{1,0:T(8,128)S(1)} custom-call(s32[5]{0:T(128)S(1)} %stack.23.place.refs_0_, bf16[256,1024]{1,0:T(8,128)(2,1)S(1)} %get-tuple-element.167.refs_1_, bf16[256,1024]{1,0:T(8,128)(2,1)S(1)} %collective-permute-done.6.refs_2_, bf16[256,1024]{1,0:T(8,128)(2,1)S(1)} %collective-permute-done.7.refs_3_, ...), custom_call_target="tpu_custom_call" | custom-call | flops 3520000000 | tf_op jit(solution)/shard_map/pallas_call | solution.py:47
  119.7 3.4 %collective-permute-done.32.refs_3_ = bf16[256,896]{1,0:T(8,128)(2,1)S(1)} collective-permute-done((bf16[256,896]{1,0:T(8,128)(2,1)S(1)}, bf16[256,896]{1,0:T(8,128)(2,1)S(1)}, u32[]{:S(2)}, u32[]{:S(2)}) %collective-permute-start.32) | collective-permute-done | bytes 458784 | tf_op jit(solution)/shard_map/ppermute | solution.py:22
  124.8 2.6 %shard_map.83 = (bf16[512,1792]{1,0:T(8,128)(2,1)}, bf16[512,1792]{1,0:T(8,128)(2,1)}) custom-call(s32[5]{0:T(128)S(1)} %stack.23.place.refs_0_, bf16[512,1792]{1,0:T(8,128)(2,1)S(1)} %get-tuple-element.98.refs_1_, bf16[512,1792]{1,0:T(8,128)(2,1)S(1)} %get-tuple-element.99.refs_2_, f32[512,1792]{1,0:T(8,128)S(1)} %shard_map.80.refs_3_, ...), custom_call_target="tpu_custom_call" | custom-call | tf_op jit(solution)/shard_map/pallas_call | solution.py:47
  (76 shorter events, 41.9 us)
Async XLA Ops:
  2.6 16.6 %collective-permute-start.3 = (bf16[64,1792]{1,0:T(8,128)(2,1)S(1)}, bf16[64,1792]{1,0:T(8,128)(2,1)S(1)}, u32[]{:S(2)}, u32[]{:S(2)}) collective-permute-start(bf16[64,1792]{1,0:T(8,128)(2,1)S(1)} %get-tuple-element.103), channel_id=1, source_target_pairs={{0,6},{1,7},{2,0},{3,1},{4,2},{5,3},{6,4},{7,5},{8,14},{9,15},{10,... | collective-permute-start | bytes 688136 | tf_op jit(solution)/shard_map/ppermute | solution.py:22
  6.8 13.0 %collective-permute-start.4 = (bf16[64,1792]{1,0:T(8,128)(2,1)S(1)}, bf16[64,1792]{1,0:T(8,128)(2,1)S(1)}, u32[]{:S(2)}, u32[]{:S(2)}) collective-permute-start(bf16[64,1792]{1,0:T(8,128)(2,1)S(1)} %get-tuple-element.104), channel_id=1, source_target_pairs={{0,4},{1,5},{2,6},{3,7},{4,0},{5,1},{6,2},{7,3},{8,12},{9,13},{10,... | collective-permute-start | bytes 688136 | tf_op jit(solution)/shard_map/ppermute | solution.py:22
  6.8 13.2 %collective-permute-start.5 = (bf16[64,1792]{1,0:T(8,128)(2,1)S(1)}, bf16[64,1792]{1,0:T(8,128)(2,1)S(1)}, u32[]{:S(2)}, u32[]{:S(2)}) collective-permute-start(bf16[64,1792]{1,0:T(8,128)(2,1)S(1)} %get-tuple-element.105), channel_id=1, source_target_pairs={{0,2},{1,3},{2,4},{3,5},{4,6},{5,7},{6,0},{7,1},{8,10},{9,11},{10,... | collective-permute-start | bytes 688136 | tf_op jit(solution)/shard_map/ppermute | solution.py:22
  9.7 15.6 %collective-permute-start.2 = (bf16[64,2048]{1,0:T(8,128)(2,1)S(1)}, bf16[64,2048]{1,0:T(8,128)(2,1)S(1)}, u32[]{:S(2)}, u32[]{:S(2)}) collective-permute-start(bf16[64,2048]{1,0:T(8,128)(2,1)S(1)} %get-tuple-element.102), channel_id=1, source_target_pairs={{0,17},{1,16},{2,19},{3,18},{4,21},{5,20},{6,23},{7,22},{8,25},{9,... | collective-permute-start | bytes 786440 | tf_op jit(solution)/shard_map/ppermute | solution.py:22
  12.5 12.7 %collective-permute-start = (bf16[64,2048]{1,0:T(8,128)(2,1)S(1)}, bf16[64,2048]{1,0:T(8,128)(2,1)S(1)}, u32[]{:S(2)}, u32[]{:S(2)}) collective-permute-start(bf16[64,2048]{1,0:T(8,128)(2,1)S(1)} %get-tuple-element.111.refs_0_), channel_id=1, source_target_pairs={{0,1},{1,0},{2,3},{3,2},{4,5},{5,4},{6,7},{7,6},{8,9},{9,8},{10,11... | collective-permute-start | bytes 786440 | tf_op jit(solution)/shard_map/ppermute | solution.py:22
  20.6 16.7 %collective-permute-start.13 = (bf16[128,1792]{1,0:T(8,128)(2,1)S(1)}, bf16[128,1792]{1,0:T(8,128)(2,1)S(1)}, u32[]{:S(2)}, u32[]{:S(2)}) collective-permute-start(bf16[128,1792]{1,0:T(8,128)(2,1)S(1)} %get-tuple-element.117), channel_id=1, source_target_pairs={{0,1},{1,0},{2,3},{3,2},{4,5},{5,4},{6,7},{7,6},{8,9},{9,8},{10,11... | collective-permute-start | bytes 1376264 | tf_op jit(solution)/shard_map/ppermute | solution.py:22
  23.7 15.2 %collective-permute-start.17 = (bf16[128,1792]{1,0:T(8,128)(2,1)S(1)}, bf16[128,1792]{1,0:T(8,128)(2,1)S(1)}, u32[]{:S(2)}, u32[]{:S(2)}) collective-permute-start(bf16[128,1792]{1,0:T(8,128)(2,1)S(1)} %get-tuple-element.110.refs_0_), channel_id=1, source_target_pairs={{0,32},{1,33},{2,34},{3,35},{4,36},{5,37},{6,38},{7,39},{8,104},{9... | collective-permute-start | bytes 1376264 | tf_op jit(solution)/shard_map/ppermute | solution.py:22
  27.8 11.6 %collective-permute-start.9 = (bf16[256,1024]{1,0:T(8,128)(2,1)S(1)}, bf16[256,1024]{1,0:T(8,128)(2,1)S(1)}, u32[]{:S(2)}, u32[]{:S(2)}) collective-permute-start(bf16[256,1024]{1,0:T(8,128)(2,1)S(1)} %get-tuple-element.116), channel_id=1, source_target_pairs={{0,8},{1,9},{2,10},{3,11},{4,12},{5,13},{6,14},{7,15},{8,0},{9,1},... | collective-permute-start | bytes 1572872 | tf_op jit(solution)/shard_map/ppermute | solution.py:22
  27.9 13.7 %collective-permute-start.6 = (bf16[256,1024]{1,0:T(8,128)(2,1)S(1)}, bf16[256,1024]{1,0:T(8,128)(2,1)S(1)}, u32[]{:S(2)}, u32[]{:S(2)}) collective-permute-start(bf16[256,1024]{1,0:T(8,128)(2,1)S(1)} %get-tuple-element.167.refs_1_), channel_id=1, source_target_pairs={{0,2},{1,3},{2,4},{3,5},{4,6},{5,7},{6,0},{7,1},{8,14},{9,15},{10,... | collective-permute-start | bytes 1572872 | tf_op jit(solution)/shard_map/ppermute | solution.py:22
  38.8 40.6 %collective-permute-start.23 = (bf16[512,1792]{1,0:T(8,128)(2,1)S(1)}, bf16[512,1792]{1,0:T(8,128)(2,1)S(1)}, u32[]{:S(2)}, u32[]{:S(2)}) collective-permute-start(bf16[512,1792]{1,0:T(8,128)(2,1)S(1)} %get-tuple-element.136.refs_9_), channel_id=1, source_target_pairs={{0,16},{1,17},{2,18},{3,19},{4,20},{5,21},{6,22},{7,23},{8,24},{9,... | collective-permute-start | bytes 5505032 | tf_op jit(solution)/shard_map/ppermute | solution.py:22
  39.4 10.4 %collective-permute-start.10 = (bf16[256,1024]{1,0:T(8,128)(2,1)S(1)}, bf16[256,1024]{1,0:T(8,128)(2,1)S(1)}, u32[]{:S(2)}, u32[]{:S(2)}) collective-permute-start(bf16[256,1024]{1,0:T(8,128)(2,1)S(1)} %collective-permute-done.9.refs_1_.refs_5_), channel_id=1, source_target_pairs={{0,2},{1,3},{2,4},{3,5},{4,6},{5,7},{6,0},{7,1},{8,14},{9,15},{10,... | collective-permute-start | bytes 1572872 | tf_op jit(solution)/shard_map/ppermute | solution.py:22
  41.7 13.8 %collective-permute-start.7 = (bf16[256,1024]{1,0:T(8,128)(2,1)S(1)}, bf16[256,1024]{1,0:T(8,128)(2,1)S(1)}, u32[]{:S(2)}, u32[]{:S(2)}) collective-permute-start(bf16[256,1024]{1,0:T(8,128)(2,1)S(1)} %collective-permute-done.6.refs_2_), channel_id=1, source_target_pairs={{0,2},{1,3},{2,4},{3,5},{4,6},{5,7},{6,0},{7,1},{8,14},{9,15},{10,... | collective-permute-start | bytes 1572872 | tf_op jit(solution)/shard_map/ppermute | solution.py:22
  41.9 14.5 %collective-permute-start.18 = (bf16[128,1792]{1,0:T(8,128)(2,1)S(1)}, bf16[128,1792]{1,0:T(8,128)(2,1)S(1)}, u32[]{:S(2)}, u32[]{:S(2)}) collective-permute-start(bf16[128,1792]{1,0:T(8,128)(2,1)S(1)} %collective-permute-done.17.refs_1_), channel_id=1, source_target_pairs={{0,32},{1,33},{2,34},{3,35},{4,36},{5,37},{6,38},{7,39},{8,104},{9... | collective-permute-start | bytes 1376264 | tf_op jit(solution)/shard_map/ppermute | solution.py:22
  46.9 11.1 %collective-permute-start.15 = (bf16[128,1792]{1,0:T(8,128)(2,1)S(1)}, bf16[128,1792]{1,0:T(8,128)(2,1)S(1)}, u32[]{:S(2)}, u32[]{:S(2)}) collective-permute-start(bf16[128,1792]{1,0:T(8,128)(2,1)S(1)} %collective-permute-done.14.refs_5_), channel_id=1, source_target_pairs={{0,32},{1,33},{2,34},{3,35},{4,36},{5,37},{6,38},{7,39},{8,104},{9... | collective-permute-start | bytes 1376264 | tf_op jit(solution)/shard_map/ppermute | solution.py:22
  49.8 11.2 %collective-permute-start.11 = (bf16[256,1024]{1,0:T(8,128)(2,1)S(1)}, bf16[256,1024]{1,0:T(8,128)(2,1)S(1)}, u32[]{:S(2)}, u32[]{:S(2)}) collective-permute-start(bf16[256,1024]{1,0:T(8,128)(2,1)S(1)} %collective-permute-done.10.refs_2_.refs_6_), channel_id=1, source_target_pairs={{0,2},{1,3},{2,4},{3,5},{4,6},{5,7},{6,0},{7,1},{8,14},{9,15},{10,... | collective-permute-start | bytes 1572872 | tf_op jit(solution)/shard_map/ppermute | solution.py:22
  55.4 11.2 %collective-permute-start.8 = (bf16[256,1024]{1,0:T(8,128)(2,1)S(1)}, bf16[256,1024]{1,0:T(8,128)(2,1)S(1)}, u32[]{:S(2)}, u32[]{:S(2)}) collective-permute-start(bf16[256,1024]{1,0:T(8,128)(2,1)S(1)} %collective-permute-done.7.refs_3_), channel_id=1, source_target_pairs={{0,2},{1,3},{2,4},{3,5},{4,6},{5,7},{6,0},{7,1},{8,14},{9,15},{10,... | collective-permute-start | bytes 1572872 | tf_op jit(solution)/shard_map/ppermute | solution.py:22
  58.0 13.0 %collective-permute-start.16 = (bf16[128,1792]{1,0:T(8,128)(2,1)S(1)}, bf16[128,1792]{1,0:T(8,128)(2,1)S(1)}, u32[]{:S(2)}, u32[]{:S(2)}) collective-permute-start(bf16[128,1792]{1,0:T(8,128)(2,1)S(1)} %collective-permute-done.15.refs_6_), channel_id=1, source_target_pairs={{0,32},{1,33},{2,34},{3,35},{4,36},{5,37},{6,38},{7,39},{8,104},{9... | collective-permute-start | bytes 1376264 | tf_op jit(solution)/shard_map/ppermute | solution.py:22
  61.1 11.2 %collective-permute-start.12 = (bf16[256,1024]{1,0:T(8,128)(2,1)S(1)}, bf16[256,1024]{1,0:T(8,128)(2,1)S(1)}, u32[]{:S(2)}, u32[]{:S(2)}) collective-permute-start(bf16[256,1024]{1,0:T(8,128)(2,1)S(1)} %collective-permute-done.11.refs_3_.refs_7_), channel_id=1, source_target_pairs={{0,2},{1,3},{2,4},{3,5},{4,6},{5,7},{6,0},{7,1},{8,14},{9,15},{10,... | collective-permute-start | bytes 1572872 | tf_op jit(solution)/shard_map/ppermute | solution.py:22
  81.0 43.8 %collective-permute-start.33 = (bf16[512,1792]{1,0:T(8,128)(2,1)S(1)}, bf16[512,1792]{1,0:T(8,128)(2,1)S(1)}, u32[]{:S(2)}, u32[]{:S(2)}) collective-permute-start(bf16[512,1792]{1,0:T(8,128)(2,1)S(1)} %shard_map.75), channel_id=1, source_target_pairs={{0,16},{1,17},{2,18},{3,19},{4,20},{5,21},{6,22},{7,23},{8,24},{9,... | collective-permute-start | bytes 5505032 | tf_op jit(solution)/shard_map/ppermute | solution.py:22
  89.3 13.8 %collective-permute-start.30 = (bf16[256,896]{1,0:T(8,128)(2,1)S(1)}, bf16[256,896]{1,0:T(8,128)(2,1)S(1)}, u32[]{:S(2)}, u32[]{:S(2)}) collective-permute-start(bf16[256,896]{1,0:T(8,128)(2,1)S(1)} %get-tuple-element.179), channel_id=1, source_target_pairs={{0,32},{1,33},{2,34},{3,35},{4,36},{5,37},{6,38},{7,39},{8,104},{9... | collective-permute-start | bytes 1376264 | tf_op jit(solution)/shard_map/ppermute | solution.py:22
  96.9 19.9 %collective-permute-start.27 = (bf16[512,896]{1,0:T(8,128)(2,1)S(1)}, bf16[512,896]{1,0:T(8,128)(2,1)S(1)}, u32[]{:S(2)}, u32[]{:S(2)}) collective-permute-start(bf16[512,896]{1,0:T(8,128)(2,1)S(1)} %get-tuple-element.165), channel_id=1, source_target_pairs={{0,8},{1,9},{2,10},{3,11},{4,12},{5,13},{6,14},{7,15},{8,0},{9,1},... | collective-permute-start | bytes 2752520 | tf_op jit(solution)/shard_map/ppermute | solution.py:22
  97.4 19.4 %collective-permute-start.28 = (bf16[512,896]{1,0:T(8,128)(2,1)S(1)}, bf16[512,896]{1,0:T(8,128)(2,1)S(1)}, u32[]{:S(2)}, u32[]{:S(2)}) collective-permute-start(bf16[512,896]{1,0:T(8,128)(2,1)S(1)} %get-tuple-element.166), channel_id=1, source_target_pairs={{0,8},{1,9},{2,10},{3,11},{4,12},{5,13},{6,14},{7,15},{8,0},{9,1},... | collective-permute-start | bytes 2752520 | tf_op jit(solution)/shard_map/ppermute | solution.py:22
  103.3 10.0 %collective-permute-start.31 = (bf16[256,896]{1,0:T(8,128)(2,1)S(1)}, bf16[256,896]{1,0:T(8,128)(2,1)S(1)}, u32[]{:S(2)}, u32[]{:S(2)}) collective-permute-start(bf16[256,896]{1,0:T(8,128)(2,1)S(1)} %add_convert_fusion.1), channel_id=1, source_target_pairs={{0,32},{1,33},{2,34},{3,35},{4,36},{5,37},{6,38},{7,39},{8,104},{9... | collective-permute-start | bytes 1376264 | tf_op jit(solution)/shard_map/ppermute | solution.py:22
  108.2 11.5 %collective-permute-start.29 = (bf16[256,896]{1,0:T(8,128)(2,1)S(1)}, bf16[256,896]{1,0:T(8,128)(2,1)S(1)}, u32[]{:S(2)}, u32[]{:S(2)}) collective-permute-start(bf16[256,896]{1,0:T(8,128)(2,1)S(1)} %add_convert_fusion.2), channel_id=1, source_target_pairs={{0,32},{1,33},{2,34},{3,35},{4,36},{5,37},{6,38},{7,39},{8,104},{9... | collective-permute-start | bytes 1376264 | tf_op jit(solution)/shard_map/ppermute | solution.py:22
  (14 other events, 79.2 us)
